TPU v7x, 32 devices: a whole 2x2x4 slice. The times are simulated.
32 devices in a mesh: groups: 2 (over y), tensor: 4 (over x, core), job: 4 (over z).
Axes of the slice: x: 2, y: 2, z: 4, core: 2. Of those that a mesh axis runs over, the one named last changes fastest.
Arguments:
- inputs: bfloat16 [8, 1024, 12288], P(('groups', 'job'), None, 'tensor'), parts along dimension 0, may hold values from -6 to 6
- grad_out: bfloat16 [8, 1024, 1024], P(('groups', 'job'), 'tensor'), parts along dimension 0, may hold values from -6 to 6
- value_weight: bfloat16 [12288, 1024], P('tensor'), may hold values from -0.1875 to 0.1875
- adapter_down: bfloat16 [8, 12288, 128], P(('groups', 'job'), 'tensor'), parts along dimension 0, may hold values from -0.25 to 0.25
- adapter_up: bfloat16 [8, 1024, 128], P(('groups', 'job'), 'tensor'), parts along dimension 0, may hold values from -0.1875 to 0.1875
- block_adapter: int32 [8, 8], P(('groups', 'job')), parts along dimension 0, may hold values from 0 to 3
- block_length: int32 [8, 8], P(('groups', 'job')), parts along dimension 0, may hold values from 1 to 128
- owner_slot: int32 [8], P('groups'), parts along dimension 0, may hold values from 0 to 3, as said below
- adapter_rank: int32 [8], P('groups'), parts along dimension 0, may hold values from 16 to 128, as said below
Outputs:
- grad_in: bfloat16 [8, 1024, 12288], P(('groups', 'job'), None, 'tensor'), parts along dimension 0
- grad_down: float32 [8, 12288, 128], P(('groups', 'job'), 'tensor'), parts along dimension 0
- grad_up: float32 [8, 1024, 128], P(('groups', 'job'), 'tensor'), parts along dimension 0
There are 2 independent parts, one for each index of `groups`. A program takes and returns all parts, laid end to end along the dimension named above; an argument that names none is the same for every part. Nothing has to cross between parts.
Inputs may be any that keep to these rules, and one draw needn't show every extreme that they name: `owner_slot`: each slot owns exactly one adapter. `adapter_rank`: every rank is 128, 64, 32 or 16, each for a quarter of the adapters.
All inputs are finite; a program needn't handle non-finite values.
Results may differ from a plain program's by a relative error of at most 0.015.
Values may be sent and summed in bfloat16 or wider, within the bound.
No kernel may reach another device: no remote copies, remote signals or barrier semaphores. Data moves between devices by JAX's collectives and lax.ppermute only.
A program may use at most 128 MiB of HBM per device.

v0:
```python
import math

import jax
import jax.numpy as jnp
from jax import lax
from jax.sharding import PartitionSpec as P


def block_tables(block_ids, block_sizes, owner_slot, adapter_rank, block_rows, rank_width):
    adapter_count = owner_slot.shape[0]
    matches = (block_ids[:, None] == jnp.arange(adapter_count, dtype=jnp.int32)[None, :]).astype(
        jnp.int32
    )
    slot_index = jnp.sum(matches * owner_slot[None, :], axis=1)
    rank_used = jnp.sum(matches * adapter_rank[None, :], axis=1)
    selector = (slot_index[:, None] == jnp.arange(adapter_count, dtype=jnp.int32)[None, :]).astype(
        jnp.float32
    )
    live_rows = (jnp.arange(block_rows, dtype=jnp.int32)[None, :] < block_sizes[:, None]).astype(
        jnp.float32
    )
    keep_ranks = (jnp.arange(rank_width, dtype=jnp.int32)[None, :] < rank_used[:, None]).astype(
        jnp.float32
    )
    scaling = rank_width / (2.0 * rank_used.astype(jnp.float32))
    factor = live_rows[:, :, None] * keep_ranks[:, None, :] * scaling[:, None, None]
    return (slot_index, selector, live_rows, factor)


def on_device(
    inputs,
    grad_out,
    value_weight,
    adapter_down,
    adapter_up,
    block_adapter,
    block_length,
    owner_slot,
    adapter_rank,
):
    highest = lax.Precision.HIGHEST
    features = inputs[0]
    row_count, local_width = features.shape
    block_count = block_adapter.shape[1]
    block_rows = row_count // block_count
    rank_width = adapter_down.shape[2]
    local_values = adapter_up.shape[1]
    scaling_norm = 1.0 / math.sqrt(lax.axis_size("job") * row_count)
    cotangent = lax.all_gather(grad_out, "tensor", axis=1, tiled=True)[0]
    slot_index, selector, live_rows, factor = block_tables(
        block_adapter[0], block_length[0], owner_slot, adapter_rank, block_rows, rank_width
    )
    base_term = lax.dot_general(
        cotangent, value_weight, (((1,), (1,)), ((), ())), preferred_element_type=jnp.float32
    )
    value_start = lax.axis_index("tensor") * local_values
    cot_slice = lax.dynamic_slice_in_dim(cotangent, value_start, local_values, 1).reshape(
        block_count, block_rows, local_values
    )
    feat_blocks = features.reshape(block_count, block_rows, local_width)
    down_all, up_all = (
        lax.all_gather(adapter_down, "job", axis=0, tiled=True),
        lax.all_gather(adapter_up, "job", axis=0, tiled=True),
    )
    down_used = jnp.take(down_all, slot_index, axis=0)
    up_used = jnp.take(up_all, slot_index, axis=0)
    projected = jnp.einsum(
        "btd,bdr->btr", feat_blocks, down_used, preferred_element_type=jnp.float32
    )
    pulled = jnp.einsum("btk,bkr->btr", cot_slice, up_used, preferred_element_type=jnp.float32)
    projected, pulled = (
        lax.psum(projected.astype(jnp.bfloat16), "tensor").astype(jnp.float32),
        lax.psum(pulled.astype(jnp.bfloat16), "tensor").astype(jnp.float32),
    )
    low_down = (projected * factor).astype(jnp.bfloat16)
    low_grad = (pulled * factor).astype(jnp.bfloat16)
    adapter_term = jnp.einsum(
        "btr,bdr->btd", low_grad, down_used, preferred_element_type=jnp.float32
    ).reshape(row_count, local_width)
    grad_rows = (base_term * live_rows.reshape(row_count)[:, None] + adapter_term).astype(
        jnp.bfloat16
    )[None]
    block_down = jnp.einsum(
        "btd,btr->bdr", feat_blocks, low_grad, preferred_element_type=jnp.float32
    )
    block_up = jnp.einsum("btk,btr->bkr", cot_slice, low_down, preferred_element_type=jnp.float32)
    part_down = jnp.einsum("bs,bdr->sdr", selector, block_down, precision=highest) * scaling_norm
    part_up = jnp.einsum("bs,bkr->skr", selector, block_up, precision=highest) * scaling_norm
    grad_down, grad_up = (
        lax.psum_scatter(
            part_down.astype(jnp.bfloat16), "job", scatter_dimension=0, tiled=True
        ).astype(jnp.float32),
        lax.psum_scatter(
            part_up.astype(jnp.bfloat16), "job", scatter_dimension=0, tiled=True
        ).astype(jnp.float32),
    )
    return (grad_rows, grad_down, grad_up)


def solution(mesh):
    placed = (
        P(("groups", "job"), None, "tensor"),
        P(("groups", "job"), "tensor", None),
        P("tensor", None),
        P(("groups", "job"), "tensor", None),
        P(("groups", "job"), "tensor", None),
        P(("groups", "job"), None),
        P(("groups", "job"), None),
        P("groups"),
        P("groups"),
    )
    return jax.shard_map(
        on_device,
        mesh=mesh,
        in_specs=placed,
        out_specs=(
            P(("groups", "job"), None, "tensor"),
            P(("groups", "job"), "tensor", None),
            P(("groups", "job"), "tensor", None),
        ),
        check_vma=False,
    )
```

profile of v0, /device:TPU:0, one launch (start us, length us, event | category | flops | bytes accessed | tf_op | source)
XLA Modules:
  0.0 252.6 jit_solution(17182570397678229221)
XLA Ops:
  7.2 0.7 all-gather.3.cloned.1.call-update
  7.9 0.7 all-gather.5.cloned.1.call-update
  8.7 15.8 %all_gather.10 = bf16[4,256,128]{2,1,0:T(8,128)(2,1)S(1)} all-gather(bf16[1,256,128]{2,1,0:T(8,128)(2,1)} %param.13), channel_id=1, replica_groups=mesh['groups'=2,'tensor'=4,'job'=4] {'job'}, dimensions={0}, use_global_device_ids=true | all-gather | bytes 327680 | tf_op jit(solution)/shard_map/all_gather | solution.py:63
  24.5 0.8 select_reduce_fusion
  25.3 0.6 gather_fusion
  26.0 8.9 %all-gather.3.cloned.1.call-done = bf16[1,1024,1024]{2,1,0:T(8,128)(2,1)} async-done(((bf16[1,256,1024]{2,1,0:T(8,128)(2,1)}), bf16[1,1024,1024]{2,1,0:T(8,128)(2,1)}) %all-gather.3.cloned.1.call-update) | async-done | bytes 2097168 | tf_op jit(solution)/shard_map/all_gather | solution.py:49
  34.9 1.1 constant_dynamic-slice_fusion
  36.0 1.1 convolution_convert_fusion
  37.0 63.0 %all-gather.5.cloned.1.call-done = bf16[4,3072,128]{2,1,0:T(8,128)(2,1)} async-done(((bf16[1,3072,128]{2,1,0:T(8,128)(2,1)}), bf16[4,3072,128]{2,1,0:T(8,128)(2,1)}) %all-gather.5.cloned.1.call-update) | async-done | bytes 3145744 | tf_op jit(solution)/shard_map/all_gather | solution.py:62
  100.0 5.9 %gather_fusion.1 = bf16[8,3072,128]{2,1,0:T(8,128)(2,1)} fusion(bf16[4,3072,128]{2,1,0:T(8,128)(2,1)} %all-gather.5.cloned.1.call-done, s32[1024]{0:T(1024)S(1)} %pad_clamp_fusion), kind=kCustom, calls=%fused_computation.1 | custom fusion | bytes 12582944 | tf_op jit(solution)/shard_map/jit(_take)/gather | solution.py:65
  105.9 7.8 %fusion.7 = bf16[8,128,128]{2,1,0:T(8,128)(2,1)} fusion(bf16[8,128,3072]{2,1,0:T(8,128)(2,1)} %bitcast.35, bf16[8,3072,128]{2,1,0:T(8,128)(2,1)} %gather_fusion.1, pred[8]{0:T(512)(128)(4,1)S(1)} %compare_and_fusion), kind=kOutput, calls=%fused_computation.15 | convolution fusion | flops 808583168 | bytes 12845064 | tf_op jit(solution)/shard_map/btd,bdr->btr/dot_general | solution.py:67
  113.9 31.9 %all-reduce.3.cloned.1.call-done = (bf16[8,128,128]{2,1,0:T(8,128)(2,1)}, bf16[8,128,128]{2,1,0:T(8,128)(2,1)}) async-done(((bf16[8,128,128]{2,1,0:T(8,128)(2,1)}, bf16[8,128,128]{2,1,0:T(8,128)(2,1)}), (bf16[8,128,128]{2,1,0:T(8,128)(2,1)}, bf16[8,128,128]{2,1,0:T(8,128)(2,1)})) %all-reduce.3.cloned.1.call-update) | async-done | bytes 524304 | tf_op jit(solution)/shard_map/psum | solution.py:73
  145.8 1.5 fusion.11
  147.3 1.2 fusion.5
  148.5 0.7 copy.23
  149.5 9.3 %convolution_bitcast_fusion = f32[8,3072,128]{1,2,0:T(8,128)} fusion(bf16[8,128,3072]{2,1,0:T(8,128)(2,1)} %bitcast.36, bf16[8,128,128]{2,1,0:T(8,128)(2,1)} %get-tuple-element.8, f32[8]{0:T(128)S(1)} %multiply_divide_fusion, f32[8,128]{1,0:T(8,128)S(1)} %get-tuple-element.12, f32[8,128]{1,0:T(8,128)S(1)} %get-tuple-element.11), kind=kOutput, calls=%fused_computation.4 | convolution fusion | flops 805961728 | bytes 19144736 | tf_op jit(solution)/shard_map/btd,btr->bdr/dot_general | solution.py:83
  158.8 12.6 %copy.17 = f32[8,3072,128]{2,0,1:T(8,128)} copy(f32[8,3072,128]{1,2,0:T(8,128)} %convolution_bitcast_fusion) | data formatting | bytes 25165824 | tf_op jit(solution)/shard_map/btd,btr->bdr/dot_general | solution.py:83
  171.4 9.6 %multiply_convert_fusion = bf16[4,3072,128]{2,0,1:T(4,128)(2,1)S(1)} fusion(f32[8,3072,128]{2,0,1:T(8,128)} %copy.17, s32[8]{0:T(128)S(1)} %get-tuple-element.7), kind=kOutput, calls=%fused_computation.5 | convolution fusion | flops 154140704 | bytes 15728672 | tf_op jit(solution)/shard_map/bs,bdr->sdr/dot_general | solution.py:87
  181.0 2.1 copy.18
  183.1 4.8 %fusion.3 = f32[8,128,3072]{2,1,0:T(8,128)S(1)} fusion(bf16[8,3072,128]{2,1,0:T(8,128)(2,1)} %gather_fusion.1, pred[8]{0:T(512)(128)(4,1)S(1)} %compare_and_fusion, bf16[8,128,128]{2,1,0:T(8,128)(2,1)S(1)} %copy-done, f32[8]{0:T(128)S(1)} %multiply_divide_fusion, f32[8,128]{1,0:T(8,128)S(1)} %get-tuple-element.12, f32[8,128]{1,0:T(8,128)S(1)} %get-tuple-element.11), kind=kOutput, calls=%fused_computation.9 | convolution fusion | flops 809107456 | bytes 19144744 | tf_op jit(solution)/shard_map/btr,bdr->btd/dot_general | solution.py:77
  188.0 12.4 %fusion.1 = bf16[1,1024,3072]{2,1,0:T(8,128)(2,1)} fusion(f32[8,128,3072]{2,1,0:T(8,128)S(1)} %fusion.3, f32[1024]{0:T(1024)S(1)} %get-tuple-element.10, bf16[3072,1024]{1,0:T(8,128)(2,1)} %param.11, bf16[1,1024,1024]{2,1,0:T(8,128)(2,1)S(1)} %copy-done.1), kind=kOutput, calls=%fused_computation.7 | convolution fusion | flops 6451888128 | bytes 27267072 | tf_op jit(solution)/shard_map/dot_general | solution.py:53
  200.4 1.5 convert_element_type.84
  201.9 41.8 %reduce-scatter.3.cloned.1.call-done = bf16[1,3072,128]{2,1,0:T(8,128)(2,1)} async-done(((bf16[4,3072,128]{2,1,0:T(8,128)(2,1)}), bf16[1,3072,128]{2,1,0:T(8,128)(2,1)}) %reduce-scatter.3.cloned.1.call-update) | async-done | bytes 786448 | tf_op jit(solution)/shard_map/reduce_scatter | solution.py:90
  243.7 2.4 convert_element_type.78
  (20 shorter events, 0.5 us)
Async XLA Ops:
  7.2 27.7 %all-gather.3.cloned.1.call-start = ((), (), s32[]{:S(2)}) async-start(), calls=%async_computation.2 | async-start | bytes 2621440 | tf_op jit(solution)/shard_map/all_gather | solution.py:49
  7.9 92.1 %all-gather.5.cloned.1.call-start = ((), (), s32[]{:S(2)}) async-start(), calls=%async_computation.3 | async-start | bytes 3932160 | tf_op jit(solution)/shard_map/all_gather | solution.py:62
  8.6 137.1 %all-reduce.3.cloned.1.call-start = ((), (), s32[]{:S(2)}) async-start(), calls=%async_computation.6 | async-start | bytes 1048576 | tf_op jit(solution)/shard_map/psum | solution.py:73
  105.9 7.9 %copy-start.2 = (s32[1,8]{1,0:T(1,128)S(1)}, s32[1,8]{1,0:T(1,128)}, u32[]{:S(2)}) copy-start(s32[1,8]{1,0:T(1,128)} %param.15) | copy-start | bytes 100
  113.7 86.6 %reduce-scatter.5.cloned.1.call-start = ((), (), s32[]{:S(2)}) async-start(), calls=%async_computation.5 | async-start | bytes 327680 | tf_op jit(solution)/shard_map/reduce_scatter | solution.py:93
  149.2 94.5 %reduce-scatter.3.cloned.1.call-start = ((), (), s32[]{:S(2)}) async-start(), calls=%async_computation.4 | async-start | bytes 3932160 | tf_op jit(solution)/shard_map/reduce_scatter | solution.py:90
  181.0 2.1 copy-start
  183.1 4.9 %copy-start.1 = (bf16[1,1024,1024]{2,1,0:T(8,128)(2,1)S(1)}, bf16[1,1024,1024]{2,1,0:T(8,128)(2,1)}, u32[]{:S(2)}) copy-start(bf16[1,1024,1024]{2,1,0:T(8,128)(2,1)} %all-gather.3.cloned.1.call-done) | copy-start | bytes 6291460
Sparse Core Ops, SparseCore 0:
  9.6 25.2 all-gather.2
  36.4 63.4 all-gather.4
  113.9 31.8 all-reduce.2
  149.4 19.8 reduce-scatter.4
  183.2 60.4 reduce-scatter.2
where the time goes:
time: 253 us
  waiting for transfers between devices  147 us (58%)
  matrix products  47.7 us (19%)
  local copies, waits for them, and re-layouts  23.1 us (9%)
  blocking collectives  15.8 us (6%)
  between operations  13.9 us (5%)
  other arithmetic  4.76 us (2%)
    all_gather x1, waiting for transfers between devices, on_device(): lax.all_gather(adapter_down, 'job', axis=0, tiled=True)  63 us
    reduce_scatter x1, waiting for transfers between devices, on_device(): lax.psum_scatter(part_down.astype(jnp.bfloat16), 'job', scatter_dimension...  41.8 us
    psum x1, waiting for transfers between devices, on_device(): lax.psum(pulled.astype(jnp.bfloat16), 'tensor').astype(jnp.float32)  31.9 us
    all_gather x1, blocking collectives, on_device(): lax.all_gather(adapter_up, 'job', axis=0, tiled=True)  15.8 us
    dot_general x1, local copies, waits for them, and re-layouts, on_device(): jnp.einsum('btd,btr->bdr', feat_blocks, low_grad, preferred_element_type=...  12.6 us
    dot_general x1, matrix products, on_device(): lax.dot_general(cotangent, value_weight, (((1,), (1,)), ((), ())), prefer...  12.4 us
    dot_general x1, matrix products, on_device(): jnp.einsum('bs,bdr->sdr', selector, block_down, precision=highest)  9.58 us
    dot_general x1, matrix products, on_device(): jnp.einsum('btd,btr->bdr', feat_blocks, low_grad, preferred_element_type=...  9.33 us
  transfers between devices with their start and end apart: 5, of which 4 were waited for; matrix products, arithmetic and copies ran while one was open for 22% of the time, Pallas kernels for 0%

commit v1 on v0

v1 whole, which is shorter than its diff:
```python
import functools
import math

import jax
import jax.numpy as jnp
from jax import lax
from jax.experimental import pallas as pl
from jax.experimental.pallas import tpu as pltpu
from jax.sharding import PartitionSpec as P

F32 = jnp.float32
BF16 = jnp.bfloat16
VMEM_LIMIT = 40 * 1024 * 1024
CHUNKS = 5
JOBS = 4
PAIR = [(0, 1), (1, 0), (2, 3), (3, 2)]
MIDDLE = [(1, 2), (2, 1)]
TENSOR_X = [(0, 2), (2, 0), (1, 3), (3, 1)]
TENSOR_CORE = [(0, 1), (1, 0), (2, 3), (3, 2)]


def params():
    return pltpu.CompilerParams(vmem_limit_bytes=VMEM_LIMIT)


def cost(flops, moved):
    return pl.CostEstimate(flops=flops, bytes_accessed=moved, transcendentals=0)


def whole(shape):
    return pl.BlockSpec(shape, lambda *_: (0,) * len(shape))


def smem():
    return pl.BlockSpec(memory_space=pltpu.SMEM)


def turn_kernel(down_ref, low_ref, high_ref):
    turned = down_ref[...].T
    half = low_ref.shape[0]
    low_ref[...] = turned[:half]
    high_ref[...] = turned[half:]


def turn(down, tile):
    width, rank = down.shape
    half = rank // 2
    out = jax.ShapeDtypeStruct((half, width), down.dtype)
    return pl.pallas_call(
        turn_kernel,
        grid=(width // tile,),
        in_specs=[pl.BlockSpec((tile, rank), lambda i: (i, 0))],
        out_specs=[pl.BlockSpec((half, tile), lambda i: (0, i))] * 2,
        out_shape=[out, out],
        compiler_params=params(),
        cost_estimate=cost(0, 4 * width * rank),
        name="turn_adapter",
    )(down)


def block_factor(ids, lengths, owners, ranks, b, rows, width):
    adapter = ids[0, b]
    rank = ranks[adapter]
    live = lax.broadcasted_iota(jnp.int32, (rows, width), 0) < lengths[0, b]
    keep = lax.broadcasted_iota(jnp.int32, (rows, width), 1) < rank
    scale = jnp.float32(width) / (2.0 * rank.astype(F32))
    return owners[adapter], jnp.where(live & keep, scale, 0.0)


def spread(low, slot):
    half = low.shape[1] // 2
    lanes = lax.broadcasted_iota(jnp.int32, low.shape, 1)
    turned = pltpu.roll(low, half, 1)
    twice = jnp.where(lanes < half, low, turned)
    chunk = jnp.where(lanes < half, 0, 1)
    return jnp.concatenate(
        [
            jnp.where(chunk == slot, twice, 0.0),
            jnp.where(chunk + 2 == slot, twice, 0.0),
            jnp.where(lanes < half, turned, 0.0),
        ],
        axis=1,
    )


def gathered(full, slot, rank):
    half = rank // 2
    odd = lax.rem(slot, 2)
    both = jnp.where(slot >= 2, full[:, rank : 2 * rank], full[:, :rank])
    turned = pltpu.roll(both, half, 1)
    lower = jnp.where(odd == 1, turned, both)
    upper = pltpu.roll(full[:, 2 * rank :], half, 1)
    lanes = lax.broadcasted_iota(jnp.int32, both.shape, 1)
    return jnp.where(lanes < half, lower, upper)


def pull_kernel(norm, ids, lengths, owners, ranks, place, g0, g1, g2, g3, u0, u1, u2, u3, x_ref,
                part_ref, wide_ref, up, turned):
    t, z = place[0], place[1]
    quarter, values = g0.shape
    rank = u0.shape[2]
    block = x_ref.shape[0] // ids.shape[1]

    @pl.when(pl.program_id(0) == 0)
    def _():
        for q, u in enumerate((u0, u1, u2, u3)):
            start = pl.multiple_of(jnp.bitwise_xor(t, q) * quarter, quarter)
            for d in range(JOBS):
                slot = lax.rem(z - d + JOBS, JOBS)
                up[slot, pl.ds(start, quarter), :] = u[d]
        for q, g in enumerate((g0, g1, g2, g3)):
            for j in range(quarter // block):
                b = jnp.bitwise_xor(t, q) * (quarter // block) + j
                slot, factor = block_factor(ids, lengths, owners, ranks, b, block, rank)
                pulled = jnp.dot(g[j * block : (j + 1) * block, :], up[slot], preferred_element_type=F32)
                low = spread((pulled * factor).astype(BF16).astype(F32), slot)
                rows = pl.ds(pl.multiple_of(b * block, block), block)
                wide_ref[rows, :] = low.astype(BF16)
                turned[:, rows] = low.T.astype(BF16)

    used = part_ref.shape[0]
    part_ref[...] = (
        jnp.dot(turned[:used, :], x_ref[...], preferred_element_type=F32) * norm
    ).astype(BF16)


def pull(tables, place, grads, ups, features, norm, tile):
    rows, width = features.shape
    quarter, values = grads[0].shape
    rank = ups[0].shape[2]
    used = CHUNKS * rank // 2
    return pl.pallas_call(
        functools.partial(pull_kernel, norm),
        grid=(width // tile,),
        in_specs=[smem()] * 5
        + [whole((quarter, values))] * 4
        + [whole((JOBS, quarter, rank))] * 4
        + [pl.BlockSpec((rows, tile), lambda i: (0, i))],
        out_specs=[
            pl.BlockSpec((used, tile), lambda i: (0, i)),
            whole((rows, 3 * rank)),
        ],
        out_shape=[
            jax.ShapeDtypeStruct((used, width), BF16),
            jax.ShapeDtypeStruct((rows, 3 * rank), BF16),
        ],
        scratch_shapes=[
            pltpu.VMEM((JOBS, values, rank), BF16),
            pltpu.VMEM((3 * rank, rows), BF16),
        ],
        compiler_params=params(),
        cost_estimate=cost(2 * used * rows * width, 2 * (rows * width + used * width + 2 * rows * values)),
        name="pull_and_part_down",
    )(*tables, place, *grads, *ups, features)


def project_kernel(ids, owners, where_to, *refs):
    chunks = refs[:9]
    x_ref, out_ref, table_ref, sems = refs[9:]
    half, width = chunks[0].shape
    rank = 2 * half
    rows = x_ref.shape[0]
    block = rank

    @pl.when(pl.program_id(0) == 0)
    def _():
        for k, chunk in enumerate(chunks):
            place = where_to[k]

            @pl.when(place < CHUNKS)
            def _():
                start = pl.multiple_of(place * half, half)
                pltpu.make_async_copy(chunk, table_ref.at[pl.ds(start, half), :], sems.at[k]).start()

        table_ref[CHUNKS * half :, :] = jnp.zeros((half, width), BF16)
        for k, chunk in enumerate(chunks):
            place = where_to[k]

            @pl.when(place < CHUNKS)
            def _():
                start = pl.multiple_of(place * half, half)
                pltpu.make_async_copy(chunk, table_ref.at[pl.ds(start, half), :], sems.at[k]).wait()

    full = lax.dot_general(
        x_ref[...], table_ref[...], (((1,), (1,)), ((), ())), preferred_element_type=F32
    )
    first = pl.program_id(0) * (rows // block)
    for j in range(rows // block):
        slot = owners[ids[0, first + j]]
        piece = gathered(full[j * block : (j + 1) * block], slot, rank)
        out_ref[j * block : (j + 1) * block, :] = piece.astype(BF16)


def project(ids, owners, where_to, chunks, features, tile):
    rows, width = features.shape
    half = chunks[0].shape[0]
    return pl.pallas_call(
        project_kernel,
        grid=(rows // tile,),
        in_specs=[smem()] * 3
        + [pl.BlockSpec(memory_space=pl.ANY)] * 9
        + [pl.BlockSpec((tile, width), lambda i: (i, 0))],
        out_specs=[
            pl.BlockSpec((tile, 2 * half), lambda i: (i, 0)),
            whole((6 * half, width)),
        ],
        out_shape=[
            jax.ShapeDtypeStruct((rows, 2 * half), BF16),
            jax.ShapeDtypeStruct((6 * half, width), BF16),
        ],
        scratch_shapes=[pltpu.SemaphoreType.DMA((9,))],
        compiler_params=params(),
        cost_estimate=cost(2 * 6 * half * rows * width, 2 * (rows * width + 12 * half * width)),
        name="project",
    )(ids, owners, where_to, *chunks, features)


def base_kernel(lengths, place, g0, g1, g2, g3, wide_ref, weight_ref, table_ref, out_ref):
    t = place[0]
    quarter, values = g0.shape
    block = out_ref.shape[0] // lengths.shape[1]
    tile = out_ref.shape[1]
    for q, g in enumerate((g0, g1, g2, g3)):
        start = pl.multiple_of(jnp.bitwise_xor(t, q) * quarter, quarter)
        base = lax.dot_general(
            g[...], weight_ref[...], (((1,), (1,)), ((), ())), preferred_element_type=F32
        )
        term = jnp.dot(wide_ref[pl.ds(start, quarter), :], table_ref[...], preferred_element_type=F32)
        for j in range(quarter // block):
            b = jnp.bitwise_xor(t, q) * (quarter // block) + j
            live = lax.broadcasted_iota(jnp.int32, (block, tile), 0) < lengths[0, b]
            part = slice(j * block, (j + 1) * block)
            out_ref[pl.ds(pl.multiple_of(start + j * block, block), block), :] = (
                jnp.where(live, base[part], 0.0) + term[part]
            ).astype(BF16)


def base(lengths, place, grads, wide, weight, table, tile):
    width, values = weight.shape
    quarter = grads[0].shape[0]
    rows, deep = wide.shape
    return pl.pallas_call(
        base_kernel,
        grid=(width // tile,),
        in_specs=[smem()] * 2
        + [whole((quarter, values))] * 4
        + [
            whole((rows, deep)),
            pl.BlockSpec((tile, values), lambda i: (i, 0)),
            pl.BlockSpec((deep, tile), lambda i: (0, i)),
        ],
        out_specs=pl.BlockSpec((rows, tile), lambda i: (0, i)),
        out_shape=jax.ShapeDtypeStruct((rows, width), BF16),
        compiler_params=params(),
        cost_estimate=cost(
            2 * rows * width * (values + deep), 2 * (rows * values + width * values + deep * width + rows * width)
        ),
        name="grad_rows",
    )(lengths, place, *grads, wide, weight, table)


def part_up_kernel(norm, ids, lengths, owners, ranks, place, g0, g1, g2, g3, a_ref, b_ref, *rest):
    outs, (slice_ref, wide) = rest[:JOBS], rest[JOBS:]
    t, z, excess = place[0], place[1], place[2]
    quarter, values = g0.shape
    rank = a_ref.shape[1]
    half = rank // 2
    block = a_ref.shape[0] // ids.shape[1]
    columns = pl.ds(pl.multiple_of(t * quarter, quarter), quarter)
    for q, g in enumerate((g0, g1, g2, g3)):
        start = pl.multiple_of(jnp.bitwise_xor(t, q) * quarter, quarter)
        slice_ref[pl.ds(start, quarter), :] = g[:, columns]
    for b in range(ids.shape[1]):
        slot, factor = block_factor(ids, lengths, owners, ranks, b, block, rank)
        rows = slice(b * block, (b + 1) * block)
        low = (a_ref[rows, :].astype(F32) + b_ref[rows, :].astype(F32)) * factor
        wide[rows, :] = spread(low.astype(BF16).astype(F32), slot).astype(BF16)
    full = (
        lax.dot_general(slice_ref[...], wide[...], (((0,), (0,)), ((), ())), preferred_element_type=F32) * norm
    )
    lanes = lax.broadcasted_iota(jnp.int32, (quarter, rank), 1)
    for d, out in enumerate(outs):
        slot = lax.rem(z + d, JOBS)
        keep = jnp.where(slot == excess, rank, half)
        out[...] = jnp.where(lanes < keep, gathered(full, slot, rank), 0.0).astype(BF16)


def part_up(tables, place, grads, sums, norm):
    quarter, values = grads[0].shape
    rows, rank = sums[0].shape
    vmem = pl.BlockSpec(memory_space=pltpu.VMEM)
    return pl.pallas_call(
        functools.partial(part_up_kernel, norm),
        in_specs=[smem()] * 5 + [vmem] * 6,
        out_specs=[vmem] * JOBS,
        out_shape=[jax.ShapeDtypeStruct((quarter, rank), BF16)] * JOBS,
        scratch_shapes=[
            pltpu.VMEM((rows, quarter), BF16),
            pltpu.VMEM((rows, 3 * rank), BF16),
        ],
        compiler_params=params(),
        cost_estimate=cost(2 * rows * quarter * 3 * rank, 2 * (rows * values + 2 * rows * rank)),
        name="part_up",
    )(*tables, place, *grads, *sums)


def last_kernel(place, own0, own1, t1, n1, t2, n2, out_ref):
    half = own0.shape[0]
    rank = 2 * half
    total = (
        jnp.concatenate([own0[...], own1[...]], axis=0).astype(F32)
        + jnp.concatenate([t1[...], t2[...]], axis=0).astype(F32)
        + jnp.concatenate([n1[...], n2[...]], axis=0).astype(F32)
    )
    keep = jnp.where(place[1] == place[2], rank, half)
    rows = lax.broadcasted_iota(jnp.int32, total.shape, 0)
    out_ref[...] = jnp.where(rows < keep, total, 0.0).T


def last(place, parts, t1, n1, t2, n2, tile):
    half, width = t1.shape
    piece = pl.BlockSpec((half, tile), lambda i, place: (0, i))
    return pl.pallas_call(
        last_kernel,
        grid_spec=pltpu.PrefetchScalarGridSpec(
            num_scalar_prefetch=1,
            grid=(width // tile,),
            in_specs=[
                pl.BlockSpec((half, tile), lambda i, place: (place[1], i)),
                pl.BlockSpec((half, tile), lambda i, place: (CHUNKS - 1, i)),
            ]
            + [piece] * 4,
            out_specs=pl.BlockSpec((tile, 2 * half), lambda i, place: (i, 0)),
        ),
        out_shape=jax.ShapeDtypeStruct((width, 2 * half), F32),
        compiler_params=params(),
        cost_estimate=cost(0, 2 * 6 * half * width + 8 * half * width),
        name="grad_down",
    )(place, parts, parts, t1, n1, t2, n2)


def on_device(
    inputs,
    grad_out,
    value_weight,
    adapter_down,
    adapter_up,
    block_adapter,
    block_length,
    owner_slot,
    adapter_rank,
):
    features = inputs[0]
    row_count, local_width = features.shape
    half = adapter_down.shape[2] // 2
    tile = 512
    norm = 1.0 / math.sqrt(JOBS * row_count)
    t, z = lax.axis_index("tensor"), lax.axis_index("job")
    excess = jnp.sum(jnp.where(adapter_rank > half, owner_slot, 0)).astype(jnp.int32)
    place = jnp.stack([t, z, excess]).astype(jnp.int32)
    tables = (block_adapter, block_length, owner_slot, adapter_rank)

    inner = (z == 1) | (z == 2)
    mine = jnp.where(z < 2, 1, 2)
    outer = jnp.where(z < 2, 0, 3)
    far_in, far_out = 3 - mine, 3 - outer
    top_in, top_out = excess == mine, excess == outer
    top_far_in, top_far_out = excess == far_in, excess == far_out

    pair = lambda value: lax.ppermute(value, "job", PAIR)
    middle = lambda value: lax.ppermute(value, "job", MIDDLE)
    shift = lambda value, d: lax.ppermute(value, "job", [(i, (i + d) % JOBS) for i in range(JOBS)])
    across = lambda value: lax.ppermute(value, "tensor", TENSOR_X)
    beside = lambda value: lax.ppermute(value, "tensor", TENSOR_CORE)

    low, high = turn(adapter_down[0], tile)
    s1 = pair(low)
    m1 = middle(low)

    up = adapter_up[0]
    g0 = grad_out[0]
    up_z = jnp.stack([up] + [shift(up, d) for d in (1, 2, 3)])
    g2 = across(g0)
    g1 = beside(g0)
    up_x = across(up_z)
    g3 = beside(g2)
    up_c = beside(jnp.stack([up_z, up_x]))
    grads = (g0, g1, g2, g3)
    ups = (up_z, up_c[0], up_x, up_c[1])

    s2 = pair(jnp.where(inner & ~top_in, m1, high))
    m2 = middle(jnp.where(top_in, high, s1))

    parts, wide = pull(tables, place, grads, ups, features, norm, tile)

    def chunk(index):
        return lax.dynamic_slice_in_dim(parts, index * half, half, 0)

    def added(index, value, use):
        return (chunk(index).astype(F32) + jnp.where(use, value.astype(F32), 0.0)).astype(BF16)

    spare = CHUNKS - 1
    c4 = jnp.where(top_in | top_far_in, far_out, spare)
    c3 = jnp.where(top_in, far_in, jnp.where(top_far_in, spare, far_out))
    s3 = pair(jnp.where(inner, jnp.where(top_in, m1, m2), chunk(c4)))
    m3 = middle(jnp.where(top_in, s1, s2))
    s4 = pair(jnp.where(inner, jnp.where(top_in, m2, m3), chunk(c3)))
    n3 = middle(added(jnp.where(top_far_in, far_out, spare), s3, ~top_in))

    none = jnp.int32(CHUNKS + 1)
    here = [
        jnp.where(inner, mine, outer),
        jnp.where(excess == z, spare, none),
        jnp.where(inner, outer, mine),
        jnp.where(
            inner, jnp.where(top_out, spare, none), jnp.where(top_in, spare, far_in)
        ),
        jnp.where(inner, none, jnp.where(top_in, far_in, jnp.where(top_far_in, spare, far_out))),
        jnp.where(
            inner, none, jnp.where(top_in | top_far_in, far_out, jnp.where(top_far_out, spare, none))
        ),
        jnp.where(inner, far_in, none),
        jnp.where(inner, jnp.where(top_far_in, spare, far_out), none),
        jnp.where(
            inner, jnp.where(top_far_in, far_out, jnp.where(top_far_out, spare, none)), none
        ),
    ]
    where_to = jnp.stack(here).astype(jnp.int32)
    partial, table = project(
        block_adapter, owner_slot, where_to, (low, high, s1, s2, s3, s4, m1, m2, m3), features, 512
    )
    both = (partial.astype(F32) + beside(partial).astype(F32)).astype(BF16)
    other = across(both)

    grad_rows = base(block_length, place, grads, wide, value_weight, table, tile)

    s5 = pair(
        jnp.where(
            inner,
            added(spare, n3, ~top_in),
            chunk(jnp.where(top_in, spare, far_in)),
        )
    )
    n2 = middle(added(jnp.where(top_far_in, spare, far_out), jnp.where(top_in, s3, s4), True))
    s6 = pair(
        jnp.where(inner, added(outer, jnp.where(top_in, n3, n2), True), chunk(mine))
    )
    n1 = middle(added(far_in, jnp.where(top_in, s4, s5), True))

    ours = part_up(tables, place, grads, (both, other), norm)
    theirs = [shift(ours[d], d) for d in (1, 2, 3)]
    grad_up = ours[0].astype(F32)
    for value in theirs:
        grad_up = grad_up + value.astype(F32)

    grad_down = last(place, parts, s6, n1, s5, n2, tile)
    return (grad_rows[None], grad_down[None], grad_up[None])


def block_tables(block_ids, block_sizes, owner_slot, adapter_rank, block_rows, rank_width):
    adapter_count = owner_slot.shape[0]
    matches = (block_ids[:, None] == jnp.arange(adapter_count, dtype=jnp.int32)[None, :]).astype(
        jnp.int32
    )
    slot_index = jnp.sum(matches * owner_slot[None, :], axis=1)
    rank_used = jnp.sum(matches * adapter_rank[None, :], axis=1)
    selector = (slot_index[:, None] == jnp.arange(adapter_count, dtype=jnp.int32)[None, :]).astype(F32)
    live_rows = (jnp.arange(block_rows, dtype=jnp.int32)[None, :] < block_sizes[:, None]).astype(F32)
    keep_ranks = (jnp.arange(rank_width, dtype=jnp.int32)[None, :] < rank_used[:, None]).astype(F32)
    scaling = rank_width / (2.0 * rank_used.astype(F32))
    factor = live_rows[:, :, None] * keep_ranks[:, None, :] * scaling[:, None, None]
    return (slot_index, selector, live_rows, factor)


def on_any_device(
    inputs,
    grad_out,
    value_weight,
    adapter_down,
    adapter_up,
    block_adapter,
    block_length,
    owner_slot,
    adapter_rank,
):
    highest = lax.Precision.HIGHEST
    features = inputs[0]
    row_count, local_width = features.shape
    block_count = block_adapter.shape[1]
    block_rows = row_count // block_count
    rank_width = adapter_down.shape[2]
    local_values = adapter_up.shape[1]
    norm = 1.0 / math.sqrt(lax.axis_size("job") * row_count)
    cotangent = lax.all_gather(grad_out, "tensor", axis=1, tiled=True)[0]
    slot_index, selector, live_rows, factor = block_tables(
        block_adapter[0], block_length[0], owner_slot, adapter_rank, block_rows, rank_width
    )
    base_term = lax.dot_general(
        cotangent, value_weight, (((1,), (1,)), ((), ())), preferred_element_type=F32
    )
    value_start = lax.axis_index("tensor") * local_values
    cot_slice = lax.dynamic_slice_in_dim(cotangent, value_start, local_values, 1).reshape(
        block_count, block_rows, local_values
    )
    feat_blocks = features.reshape(block_count, block_rows, local_width)
    down_all = lax.all_gather(adapter_down, "job", axis=0, tiled=True)
    up_all = lax.all_gather(adapter_up, "job", axis=0, tiled=True)
    down_used = jnp.take(down_all, slot_index, axis=0)
    up_used = jnp.take(up_all, slot_index, axis=0)
    projected = jnp.einsum("btd,bdr->btr", feat_blocks, down_used, preferred_element_type=F32)
    pulled = jnp.einsum("btk,bkr->btr", cot_slice, up_used, preferred_element_type=F32)
    projected = lax.psum(projected.astype(BF16), "tensor").astype(F32)
    pulled = lax.psum(pulled.astype(BF16), "tensor").astype(F32)
    low_down = (projected * factor).astype(BF16)
    low_grad = (pulled * factor).astype(BF16)
    adapter_term = jnp.einsum(
        "btr,bdr->btd", low_grad, down_used, preferred_element_type=F32
    ).reshape(row_count, local_width)
    grad_rows = (base_term * live_rows.reshape(row_count)[:, None] + adapter_term).astype(BF16)[None]
    block_down = jnp.einsum("btd,btr->bdr", feat_blocks, low_grad, preferred_element_type=F32)
    block_up = jnp.einsum("btk,btr->bkr", cot_slice, low_down, preferred_element_type=F32)
    part_down = jnp.einsum("bs,bdr->sdr", selector, block_down, precision=highest) * norm
    part_up_sum = jnp.einsum("bs,bkr->skr", selector, block_up, precision=highest) * norm
    grad_down = lax.psum_scatter(part_down.astype(BF16), "job", scatter_dimension=0, tiled=True).astype(F32)
    grad_up = lax.psum_scatter(part_up_sum.astype(BF16), "job", scatter_dimension=0, tiled=True).astype(F32)
    return (grad_rows, grad_down, grad_up)


def solution(mesh):
    placed = (
        P(("groups", "job"), None, "tensor"),
        P(("groups", "job"), "tensor", None),
        P("tensor", None),
        P(("groups", "job"), "tensor", None),
        P(("groups", "job"), "tensor", None),
        P(("groups", "job"), None),
        P(("groups", "job"), None),
        P("groups"),
        P("groups"),
    )
    small = mesh.shape["job"] == JOBS and mesh.shape["tensor"] == 4
    return jax.shard_map(
        on_device if small else on_any_device,
        mesh=mesh,
        in_specs=placed,
        out_specs=(
            P(("groups", "job"), None, "tensor"),
            P(("groups", "job"), "tensor", None),
            P(("groups", "job"), "tensor", None),
        ),
        check_vma=False,
    )
```

time: 253 us -> 153 us (0.60)
  waiting for transfers between devices: 147 us -> 20.2 us
  starting transfers between devices: 0.38 us -> 61.7 us
  matrix products: 47.7 us -> 0 us
  Pallas kernels: 0 us -> 32.4 us
  blocking collectives: 15.8 us -> 0 us
  between operations: 13.9 us -> 4.35 us
  other arithmetic: 4.76 us -> 11.9 us
    all_gather x2 -> x0, waiting for transfers between devices: 71.8 us -> none  [the longest x1 63 us: on_device(): lax.all_gather(adapter_down, 'job', axis=0, tiled=True)]
    ppermute x0 -> x25, starting transfers between devices: none -> 61.7 us  [the longest x6 40.1 us: on_device(): pair = lambda value: lax.ppermute(value, 'job', PAIR)]
    dot_general x8 -> x0, matrix products: 47.7 us -> none  [the longest x1 12.4 us: on_device(): lax.dot_general(cotangent, value_weight, (((1,), (1,)), ((), ())), prefer...]
    reduce_scatter x2 -> x0, waiting for transfers between devices: 41.8 us -> none  [the longest x1 41.8 us: on_device(): lax.psum_scatter(part_down.astype(jnp.bfloat16), 'job', scatter_dimension...]
    pallas_call x0 -> x6, Pallas kernels: none -> 32.4 us  [the longest x1 13 us: base(): pl.pallas_call(base_kernel, grid=(width // tile,), in_specs=[smem()] * 2...]
    psum x1 -> x0, waiting for transfers between devices: 31.9 us -> none  [on_device(): lax.psum(pulled.astype(jnp.bfloat16), 'tensor').astype(jnp.float32)]
    unnamed x6 -> x68, local copies, waits for them, and re-layouts: 0.01 us -> 21 us
    ppermute x0 -> x25, waiting for transfers between devices: none -> 20.2 us  [the longest x3 11.4 us: on_device(): across = lambda value: lax.ppermute(value, 'tensor', TENSOR_X)]
  transfers between devices with their start and end apart: 5 -> 25, of which waited for: 4 -> 3; matrix products, arithmetic and copies ran while one was open for 22% -> 7% of each run, Pallas kernels for 0% -> 18%
where the time goes in v1:
time: 153 us; the launch traced here: 152 us
  starting transfers between devices  61.7 us (40%)
  Pallas kernels  32.4 us (21%)
  local copies, waits for them, and re-layouts  21.7 us (14%)
  waiting for transfers between devices  20.2 us (13%)
  other arithmetic  11.9 us (8%)
  between operations  4.35 us (3%)
    ppermute x6, starting transfers between devices, on_device(): pair = lambda value: lax.ppermute(value, 'job', PAIR)  40.1 us
    unnamed x68, local copies, waits for them, and re-layouts  21 us
    pallas_call x1, Pallas kernels, base(): pl.pallas_call(base_kernel, grid=(width // tile,), in_specs=[smem()] * 2...  13 us
    ppermute x6, starting transfers between devices, on_device(): lax.ppermute(value, 'job', [(i, (i + d) % JOBS) for i in range(JOBS)])  12.6 us
    ppermute x3, waiting for transfers between devices, on_device(): across = lambda value: lax.ppermute(value, 'tensor', TENSOR_X)  11.4 us
    ppermute x6, waiting for transfers between devices, on_device(): pair = lambda value: lax.ppermute(value, 'job', PAIR)  8.67 us
    pallas_call x1, Pallas kernels, project(): pl.pallas_call(project_kernel, grid=(rows // tile,), in_specs=[smem()] *...  6.04 us
    pallas_call x1, Pallas kernels, pull(): pl.pallas_call(functools.partial(pull_kernel, norm), grid=(width // tile,...  5.84 us
  transfers between devices with their start and end apart: 25, of which 3 were waited for; matrix products, arithmetic and copies ran while one was open for 7% of the time, Pallas kernels for 18%

profile of v1, /device:TPU:0, one launch (start us, length us, event | category | flops | bytes accessed | tf_op | source)
XLA Modules:
  0.0 152.3 jit_solution(4456863530905187879)
XLA Ops:
  1.8 2.2 %turn_adapter.1 = (bf16[64,3072]{1,0:T(8,128)(2,1)}, bf16[64,3072]{1,0:T(8,128)(2,1)S(1)}) custom-call(bf16[3072,128]{1,0:T(8,128)(2,1)S(1)} %bitcast.37), custom_call_target="tpu_custom_call" | custom-call | bytes 1572864 | tf_op jit(solution)/shard_map/turn_adapter/pallas_call | solution.py:49
  4.8 5.1 %collective-permute-start.5 = (bf16[256,128]{1,0:T(8,128)(2,1)}, bf16[256,128]{1,0:T(8,128)(2,1)S(1)}, u32[]{:S(2)}, u32[]{:S(2)}) collective-permute-start(bf16[256,128]{1,0:T(8,128)(2,1)} %bitcast.39), channel_id=1, source_target_pairs={{0,3},{1,0},{2,1},{3,2},{4,7},{5,4},{6,5},{7,6},{8,11},{9,8},{10,9... | collective-permute-start | bytes 196616 | tf_op jit(solution)/shard_map/ppermute | solution.py:372
  9.9 2.2 %collective-permute-start.4 = (bf16[256,128]{1,0:T(8,128)(2,1)}, bf16[256,128]{1,0:T(8,128)(2,1)S(1)}, u32[]{:S(2)}, u32[]{:S(2)}) collective-permute-start(bf16[256,128]{1,0:T(8,128)(2,1)} %bitcast.40), channel_id=1, source_target_pairs={{0,2},{1,3},{2,0},{3,1},{4,6},{5,7},{6,4},{7,5},{8,10},{9,11},{10,... | collective-permute-start | bytes 196616 | tf_op jit(solution)/shard_map/ppermute | solution.py:372
  17.7 8.6 %collective-permute-start.10 = (bf16[64,3072]{1,0:T(8,128)(2,1)}, bf16[64,3072]{1,0:T(8,128)(2,1)S(1)}, u32[]{:S(2)}, u32[]{:S(2)}) collective-permute-start(bf16[64,3072]{1,0:T(8,128)(2,1)} %broadcast_select_fusion.2), channel_id=1, source_target_pairs={{0,1},{1,0},{2,3},{3,2},{4,5},{5,4},{6,7},{7,6},{8,9},{9,8},{10,11... | collective-permute-start | bytes 1179656 | tf_op jit(solution)/shard_map/ppermute | solution.py:370
  29.0 4.9 %collective-permute-done.6.u2 = bf16[4,256,128]{2,1,0:T(8,128)(2,1)} collective-permute-done((bf16[4,256,128]{2,1,0:T(8,128)(2,1)S(1)}, bf16[4,256,128]{2,1,0:T(8,128)(2,1)}, u32[]{:S(2)}, u32[]{:S(2)}) %collective-permute-start.6) | collective-permute-done | bytes 262176 | tf_op jit(solution)/shard_map/ppermute | solution.py:373
  38.0 2.9 %copy-done = bf16[1,1024,3072]{2,1,0:T(8,128)(2,1)S(1)} copy-done((bf16[1,1024,3072]{2,1,0:T(8,128)(2,1)S(1)}, bf16[1,1024,3072]{2,1,0:T(8,128)(2,1)}, u32[]{:S(2)}) %copy-start) | copy-done | bytes 6291480
  43.0 5.8 %pull_and_part_down.1 = (bf16[320,3072]{1,0:T(8,128)(2,1)S(1)}, bf16[1024,384]{1,0:T(8,128)(2,1)S(1)}) custom-call(s32[1,8]{1,0:T(1,128)S(1)} %copy-done.23, s32[1,8]{1,0:T(1,128)S(1)} %copy-done.25, s32[4]{0:T(128)S(1)} %copy-done.22, s32[4]{0:T(128)S(1)} %copy-done.24, s32[3]{0:T(128)S(1)} %pad_add_fusion.place, bf16[256,1024]{1,0:T(8,128)(2,1)S(1)} %bitcast.34, ...), custom_call_target="tpu_custom_call" | custom-call | flops 2013265920 | bytes 12451840 | tf_op jit(solution)/shard_map/pull_and_part_down/pallas_call | solution.py:132
  50.2 15.9 %collective-permute-start.12 = (bf16[64,3072]{1,0:T(8,128)(2,1)S(1)}, bf16[64,3072]{1,0:T(8,128)(2,1)S(1)}, u32[]{:S(2)}, u32[]{:S(2)}) collective-permute-start(bf16[64,3072]{1,0:T(8,128)(2,1)S(1)} %get-tuple-element.26), channel_id=1, source_target_pairs={{0,1},{1,0},{2,3},{3,2},{4,5},{5,4},{6,7},{7,6},{8,9},{9,8},{10,11... | collective-permute-start | bytes 1179656 | tf_op jit(solution)/shard_map/ppermute | solution.py:370
  66.1 8.7 %collective-permute-done.12.refs_4_ = bf16[64,3072]{1,0:T(8,128)(2,1)S(1)} collective-permute-done((bf16[64,3072]{1,0:T(8,128)(2,1)S(1)}, bf16[64,3072]{1,0:T(8,128)(2,1)S(1)}, u32[]{:S(2)}, u32[]{:S(2)}) %collective-permute-start.12) | collective-permute-done | bytes 393248 | tf_op jit(solution)/shard_map/ppermute | solution.py:370
  76.3 3.9 %collective-permute-start.14 = (bf16[64,3072]{1,0:T(8,128)(2,1)}, bf16[64,3072]{1,0:T(8,128)(2,1)}, u32[]{:S(2)}, u32[]{:S(2)}) collective-permute-start(bf16[64,3072]{1,0:T(8,128)(2,1)} %get-tuple-element.25), channel_id=1, source_target_pairs={{0,1},{1,0},{2,3},{3,2},{4,5},{5,4},{6,7},{7,6},{8,9},{9,8},{10,11... | collective-permute-start | bytes 1179656 | tf_op jit(solution)/shard_map/ppermute | solution.py:370
  80.2 1.9 %fusion.1 = bf16[64,3072]{1,0:T(8,128)(2,1)} fusion(bf16[64,3072]{1,0:T(8,128)(2,1)} %collective-permute-done.15, bf16[320,3072]{1,0:T(8,128)(2,1)S(1)} %get-tuple-element.16.own0.own1, s32[]{:T(128)S(6)} %select_n.222, pred[]{:T(512)S(6)} %not.2, pred[]{:T(512)S(6)} %or.7), kind=kLoop, calls=%fused_computation.8 | loop fusion | flops 1179648 | bytes 1572870 | tf_op jit(solution)/shard_map/jit(_where)/select_n | solution.py:438
  82.1 7.9 %collective-permute-start.18 = (bf16[64,3072]{1,0:T(8,128)(2,1)}, bf16[64,3072]{1,0:T(8,128)(2,1)S(1)}, u32[]{:S(2)}, u32[]{:S(2)}) collective-permute-start(bf16[64,3072]{1,0:T(8,128)(2,1)} %fusion.1), channel_id=1, source_target_pairs={{0,1},{1,0},{2,3},{3,2},{4,5},{5,4},{6,7},{7,6},{8,9},{9,8},{10,11... | collective-permute-start | bytes 1179656 | tf_op jit(solution)/shard_map/ppermute | solution.py:370
  92.6 2.8 %copy-done.1 = bf16[1,1024,3072]{2,1,0:T(8,128)(2,1)S(1)} copy-done((bf16[1,1024,3072]{2,1,0:T(8,128)(2,1)S(1)}, bf16[1,1024,3072]{2,1,0:T(8,128)(2,1)}, u32[]{:S(2)}) %copy-start.1) | copy-done | bytes 6291480
  100.1 6.0 %project.1 = (bf16[1024,128]{1,0:T(8,128)(2,1)S(1)}, bf16[384,3072]{1,0:T(8,128)(2,1)S(1)}) custom-call(s32[1,8]{1,0:T(1,128)S(1)} %copy-done.23, s32[4]{0:T(128)S(1)} %copy-done.22, s32[9]{0:T(128)S(1)} %copy-done.27, bf16[64,3072]{1,0:T(8,128)(2,1)} %get-tuple-element.14.refs_0_, bf16[64,3072]{1,0:T(8,128)(2,1)S(1)} %get-tuple-element.15.refs_1_, ...), custom_call_target="tpu_custom_call" | custom-call | flops 2415919104 | bytes 11010048 | tf_op jit(solution)/shard_map/project/pallas_call | solution.py:197
  106.2 2.9 %add_convert_fusion = (bf16[64,3072]{1,0:T(8,128)(2,1)}, bf16[64,3072]{1,0:T(8,128)(2,1)}) fusion(bf16[64,3072]{1,0:T(8,128)(2,1)} %collective-permute-done.14.refs_5_, bf16[64,3072]{1,0:T(8,128)(2,1)S(1)} %collective-permute-done.18.t2, bf16[320,3072]{1,0:T(8,128)(2,1)S(1)} %get-tuple-element.16.own0.own1, s32[]{:T(128)S(6)} %select_n.220, pred[]{:T(512)S(6)} %eq.25, ...), kind=kLoop, calls=%fused_computation | loop fusion | flops 1966080 | bytes 2752521 | tf_op jit(solution)/shard_map/convert_element_type | solution.py:400
  109.9 1.6 %collective-permute-start.21 = (bf16[1024,128]{1,0:T(8,128)(2,1)S(1)}, bf16[1024,128]{1,0:T(8,128)(2,1)}, u32[]{:S(2)}, u32[]{:S(2)}) collective-permute-start(bf16[1024,128]{1,0:T(8,128)(2,1)S(1)} %add_convert_fusion.5.a_ref), channel_id=1, source_target_pairs={{0,8},{8,0},{4,12},{12,4},{1,9},{9,1},{5,13},{13,5},{2,10},{10,2},... | collective-permute-start | bytes 786440 | tf_op jit(solution)/shard_map/ppermute | solution.py:373
  111.5 6.6 %collective-permute-done.21.b_ref = bf16[1024,128]{1,0:T(8,128)(2,1)} collective-permute-done((bf16[1024,128]{1,0:T(8,128)(2,1)S(1)}, bf16[1024,128]{1,0:T(8,128)(2,1)}, u32[]{:S(2)}, u32[]{:S(2)}) %collective-permute-start.21) | collective-permute-done | bytes 262176 | tf_op jit(solution)/shard_map/ppermute | solution.py:373
  121.8 1.9 %part_up.1 = (bf16[256,128]{1,0:T(8,128)(2,1)S(1)}, bf16[256,128]{1,0:T(8,128)(2,1)S(1)}, bf16[256,128]{1,0:T(8,128)(2,1)S(1)}, bf16[256,128]{1,0:T(8,128)(2,1)S(1)}) custom-call(s32[1,8]{1,0:T(1,128)S(1)} %copy-done.23, s32[1,8]{1,0:T(1,128)S(1)} %copy-done.26, s32[4]{0:T(128)S(1)} %copy-done.22, s32[4]{0:T(128)S(1)} %copy-done.24, ...), custom_call_target="tpu_custom_call" | custom-call | flops 201326592 | bytes 2621440 | tf_op jit(solution)/shard_map/part_up/pallas_call | solution.py:292
  123.7 1.9 %collective-permute-start.22 = (bf16[256,128]{1,0:T(8,128)(2,1)S(1)}, bf16[256,128]{1,0:T(8,128)(2,1)S(1)}, u32[]{:S(2)}, u32[]{:S(2)}) collective-permute-start(bf16[256,128]{1,0:T(8,128)(2,1)S(1)} %get-tuple-element.20), channel_id=1, source_target_pairs={{0,1},{1,2},{2,3},{3,0},{4,5},{5,6},{6,7},{7,4},{8,9},{9,10},{10,1... | collective-permute-start | bytes 196616 | tf_op jit(solution)/shard_map/ppermute | solution.py:372
  126.7 1.8 %collective-permute-start.24 = (bf16[256,128]{1,0:T(8,128)(2,1)S(1)}, bf16[256,128]{1,0:T(8,128)(2,1)S(1)}, u32[]{:S(2)}, u32[]{:S(2)}) collective-permute-start(bf16[256,128]{1,0:T(8,128)(2,1)S(1)} %get-tuple-element.22), channel_id=1, source_target_pairs={{0,3},{1,0},{2,1},{3,2},{4,7},{5,4},{6,5},{7,6},{8,11},{9,8},{10,9... | collective-permute-start | bytes 196616 | tf_op jit(solution)/shard_map/ppermute | solution.py:372
  129.4 3.0 %collective-permute-start.17 = (bf16[64,3072]{1,0:T(8,128)(2,1)S(1)}, bf16[64,3072]{1,0:T(8,128)(2,1)S(1)}, u32[]{:S(2)}, u32[]{:S(2)}) collective-permute-start(bf16[64,3072]{1,0:T(8,128)(2,1)S(1)} %fusion), channel_id=1, source_target_pairs={{0,1},{1,0},{2,3},{3,2},{4,5},{5,4},{6,7},{7,6},{8,9},{9,8},{10,11... | collective-permute-start | bytes 1179656 | tf_op jit(solution)/shard_map/ppermute | solution.py:370
  132.4 2.8 %copy-done.28 = bf16[3072,1024]{1,0:T(8,128)(2,1)S(1)} copy-done((bf16[3072,1024]{1,0:T(8,128)(2,1)S(1)}, bf16[3072,1024]{1,0:T(8,128)(2,1)}, u32[]{:S(2)}) %copy-start.28) | copy-done | bytes 6291480
  135.2 13.0 %grad_rows.1 = bf16[1024,3072]{1,0:T(8,128)(2,1)} custom-call(s32[1,8]{1,0:T(1,128)S(1)} %copy-done.26, s32[3]{0:T(128)S(1)} %pad_add_fusion.place, bf16[256,1024]{1,0:T(8,128)(2,1)S(1)} %bitcast.36, bf16[256,1024]{1,0:T(8,128)(2,1)S(1)} %copy-done.10, bf16[256,1024]{1,0:T(8,128)(2,1)S(1)} %copy-done.7, bf16[256,1024]{1,0:T(8,128)(2,1)S(1)} %copy-done.12, ...), custom_call_target="tpu_custom_call" | custom-call | flops 8858370048 | bytes 17039360 | tf_op jit(solution)/shard_map/grad_rows/pallas_call | solution.py:242
  148.9 3.4 %grad_down.1 = f32[3072,128]{1,0:T(8,128)} custom-call(s32[3]{0:T(128)S(1)} %pad_add_fusion.place, bf16[320,3072]{1,0:T(8,128)(2,1)S(1)} %get-tuple-element.16.own0.own1, bf16[320,3072]{1,0:T(8,128)(2,1)S(1)} %get-tuple-element.16.own0.own1, bf16[64,3072]{1,0:T(8,128)(2,1)S(1)} %collective-permute-done.17.t1, ...), custom_call_target="tpu_custom_call" | custom-call | bytes 3932160 | tf_op jit(solution)/shard_map/grad_down/pallas_call | solution.py:323
  (115 shorter events, 30.3 us)
Async XLA Ops:
  4.1 11.2 %collective-permute-start.9 = (bf16[64,3072]{1,0:T(8,128)(2,1)}, bf16[64,3072]{1,0:T(8,128)(2,1)S(1)}, u32[]{:S(2)}, u32[]{:S(2)}) collective-permute-start(bf16[64,3072]{1,0:T(8,128)(2,1)} %get-tuple-element.14.refs_0_), channel_id=1, source_target_pairs={{1,2},{2,1},{5,6},{6,5},{9,10},{10,9},{13,14},{14,13},{17,18},{18,... | collective-permute-start | bytes 1179656 | tf_op jit(solution)/shard_map/ppermute | solution.py:371
  4.8 12.9 %collective-permute-start.5 = (bf16[256,128]{1,0:T(8,128)(2,1)}, bf16[256,128]{1,0:T(8,128)(2,1)S(1)}, u32[]{:S(2)}, u32[]{:S(2)}) collective-permute-start(bf16[256,128]{1,0:T(8,128)(2,1)} %bitcast.39), channel_id=1, source_target_pairs={{0,3},{1,0},{2,1},{3,2},{4,7},{5,4},{6,5},{7,6},{8,11},{9,8},{10,9... | collective-permute-start | bytes 196616 | tf_op jit(solution)/shard_map/ppermute | solution.py:372
  9.9 16.4 %collective-permute-start.4 = (bf16[256,128]{1,0:T(8,128)(2,1)}, bf16[256,128]{1,0:T(8,128)(2,1)S(1)}, u32[]{:S(2)}, u32[]{:S(2)}) collective-permute-start(bf16[256,128]{1,0:T(8,128)(2,1)} %bitcast.40), channel_id=1, source_target_pairs={{0,2},{1,3},{2,0},{3,1},{4,6},{5,7},{6,4},{7,5},{8,10},{9,11},{10,... | collective-permute-start | bytes 196616 | tf_op jit(solution)/shard_map/ppermute | solution.py:372
  12.1 14.2 %collective-permute-start.3 = (bf16[256,128]{1,0:T(8,128)(2,1)}, bf16[256,128]{1,0:T(8,128)(2,1)S(1)}, u32[]{:S(2)}, u32[]{:S(2)}) collective-permute-start(bf16[256,128]{1,0:T(8,128)(2,1)} %bitcast.41), channel_id=1, source_target_pairs={{0,1},{1,2},{2,3},{3,0},{4,5},{5,6},{6,7},{7,4},{8,9},{9,10},{10,1... | collective-permute-start | bytes 196616 | tf_op jit(solution)/shard_map/ppermute | solution.py:372
  12.5 23.1 %collective-permute-start.8 = (bf16[64,3072]{1,0:T(8,128)(2,1)}, bf16[64,3072]{1,0:T(8,128)(2,1)S(1)}, u32[]{:S(2)}, u32[]{:S(2)}) collective-permute-start(bf16[64,3072]{1,0:T(8,128)(2,1)} %get-tuple-element.14.refs_0_), channel_id=1, source_target_pairs={{0,1},{1,0},{2,3},{3,2},{4,5},{5,4},{6,7},{7,6},{8,9},{9,8},{10,11... | collective-permute-start | bytes 1179656 | tf_op jit(solution)/shard_map/ppermute | solution.py:370
  15.3 19.8 %collective-permute-start.1 = (bf16[256,1024]{1,0:T(8,128)(2,1)}, bf16[256,1024]{1,0:T(8,128)(2,1)S(1)}, u32[]{:S(2)}, u32[]{:S(2)}) collective-permute-start(bf16[256,1024]{1,0:T(8,128)(2,1)} %bitcast.32), channel_id=1, source_target_pairs={{0,8},{8,0},{4,12},{12,4},{1,9},{9,1},{5,13},{13,5},{2,10},{10,2},... | collective-permute-start | bytes 1572872 | tf_op jit(solution)/shard_map/ppermute | solution.py:373
  17.7 17.9 %collective-permute-start.10 = (bf16[64,3072]{1,0:T(8,128)(2,1)}, bf16[64,3072]{1,0:T(8,128)(2,1)S(1)}, u32[]{:S(2)}, u32[]{:S(2)}) collective-permute-start(bf16[64,3072]{1,0:T(8,128)(2,1)} %broadcast_select_fusion.2), channel_id=1, source_target_pairs={{0,1},{1,0},{2,3},{3,2},{4,5},{5,4},{6,7},{7,6},{8,9},{9,8},{10,11... | collective-permute-start | bytes 1179656 | tf_op jit(solution)/shard_map/ppermute | solution.py:370
  27.1 6.8 %collective-permute-start.6 = (bf16[4,256,128]{2,1,0:T(8,128)(2,1)S(1)}, bf16[4,256,128]{2,1,0:T(8,128)(2,1)}, u32[]{:S(2)}, u32[]{:S(2)}) collective-permute-start(bf16[4,256,128]{2,1,0:T(8,128)(2,1)S(1)} %get-tuple-element.32.u0), channel_id=1, source_target_pairs={{0,8},{8,0},{4,12},{12,4},{1,9},{9,1},{5,13},{13,5},{2,10},{10,2},... | collective-permute-start | bytes 786440 | tf_op jit(solution)/shard_map/ppermute | solution.py:373
  27.6 9.5 %collective-permute-start = (bf16[256,1024]{1,0:T(8,128)(2,1)S(1)}, bf16[256,1024]{1,0:T(8,128)(2,1)S(1)}, u32[]{:S(2)}, u32[]{:S(2)}) collective-permute-start(bf16[256,1024]{1,0:T(8,128)(2,1)S(1)} %bitcast.33), channel_id=1, source_target_pairs={{0,4},{4,0},{8,12},{12,8},{1,5},{5,1},{9,13},{13,9},{2,6},{6,2},{1... | collective-permute-start | bytes 1572872 | tf_op jit(solution)/shard_map/ppermute | solution.py:374
  35.1 2.8 %collective-permute-start.2 = (bf16[256,1024]{1,0:T(8,128)(2,1)S(1)}, bf16[256,1024]{1,0:T(8,128)(2,1)S(1)}, u32[]{:S(2)}, u32[]{:S(2)}) collective-permute-start(bf16[256,1024]{1,0:T(8,128)(2,1)S(1)} %collective-permute-done.1.g2), channel_id=1, source_target_pairs={{0,4},{4,0},{8,12},{12,8},{1,5},{5,1},{9,13},{13,9},{2,6},{6,2},{1... | collective-permute-start | bytes 1572872 | tf_op jit(solution)/shard_map/ppermute | solution.py:374
  35.7 13.2 %collective-permute-start.13 = (bf16[64,3072]{1,0:T(8,128)(2,1)S(1)}, bf16[64,3072]{1,0:T(8,128)(2,1)S(1)}, u32[]{:S(2)}, u32[]{:S(2)}) collective-permute-start(bf16[64,3072]{1,0:T(8,128)(2,1)S(1)} %get-tuple-element.29), channel_id=1, source_target_pairs={{1,2},{2,1},{5,6},{6,5},{9,10},{10,9},{13,14},{14,13},{17,18},{18,... | collective-permute-start | bytes 1179656 | tf_op jit(solution)/shard_map/ppermute | solution.py:371
  36.4 12.5 %collective-permute-start.11 = (bf16[64,3072]{1,0:T(8,128)(2,1)S(1)}, bf16[64,3072]{1,0:T(8,128)(2,1)S(1)}, u32[]{:S(2)}, u32[]{:S(2)}) collective-permute-start(bf16[64,3072]{1,0:T(8,128)(2,1)S(1)} %get-tuple-element.30), channel_id=1, source_target_pairs={{1,2},{2,1},{5,6},{6,5},{9,10},{10,9},{13,14},{14,13},{17,18},{18,... | collective-permute-start | bytes 1179656 | tf_op jit(solution)/shard_map/ppermute | solution.py:371
  50.2 24.6 %collective-permute-start.12 = (bf16[64,3072]{1,0:T(8,128)(2,1)S(1)}, bf16[64,3072]{1,0:T(8,128)(2,1)S(1)}, u32[]{:S(2)}, u32[]{:S(2)}) collective-permute-start(bf16[64,3072]{1,0:T(8,128)(2,1)S(1)} %get-tuple-element.26), channel_id=1, source_target_pairs={{0,1},{1,0},{2,3},{3,2},{4,5},{5,4},{6,7},{7,6},{8,9},{9,8},{10,11... | collective-permute-start | bytes 1179656 | tf_op jit(solution)/shard_map/ppermute | solution.py:370
  74.9 5.3 %collective-permute-start.15 = (bf16[64,3072]{1,0:T(8,128)(2,1)S(1)}, bf16[64,3072]{1,0:T(8,128)(2,1)}, u32[]{:S(2)}, u32[]{:S(2)}) collective-permute-start(bf16[64,3072]{1,0:T(8,128)(2,1)S(1)} %add_convert_fusion.4), channel_id=1, source_target_pairs={{1,2},{2,1},{5,6},{6,5},{9,10},{10,9},{13,14},{14,13},{17,18},{18,... | collective-permute-start | bytes 1179656 | tf_op jit(solution)/shard_map/ppermute | solution.py:371
  76.3 16.3 %collective-permute-start.14 = (bf16[64,3072]{1,0:T(8,128)(2,1)}, bf16[64,3072]{1,0:T(8,128)(2,1)}, u32[]{:S(2)}, u32[]{:S(2)}) collective-permute-start(bf16[64,3072]{1,0:T(8,128)(2,1)} %get-tuple-element.25), channel_id=1, source_target_pairs={{0,1},{1,0},{2,3},{3,2},{4,5},{5,4},{6,7},{7,6},{8,9},{9,8},{10,11... | collective-permute-start | bytes 1179656 | tf_op jit(solution)/shard_map/ppermute | solution.py:370
  82.1 24.1 %collective-permute-start.18 = (bf16[64,3072]{1,0:T(8,128)(2,1)}, bf16[64,3072]{1,0:T(8,128)(2,1)S(1)}, u32[]{:S(2)}, u32[]{:S(2)}) collective-permute-start(bf16[64,3072]{1,0:T(8,128)(2,1)} %fusion.1), channel_id=1, source_target_pairs={{0,1},{1,0},{2,3},{3,2},{4,5},{5,4},{6,7},{7,6},{8,9},{9,8},{10,11... | collective-permute-start | bytes 1179656 | tf_op jit(solution)/shard_map/ppermute | solution.py:370
  106.1 3.7 %collective-permute-start.20 = (bf16[1024,128]{1,0:T(8,128)(2,1)S(1)}, bf16[1024,128]{1,0:T(8,128)(2,1)S(1)}, u32[]{:S(2)}, u32[]{:S(2)}) collective-permute-start(bf16[1024,128]{1,0:T(8,128)(2,1)S(1)} %get-tuple-element.18), channel_id=1, source_target_pairs={{0,4},{4,0},{8,12},{12,8},{1,5},{5,1},{9,13},{13,9},{2,6},{6,2},{1... | collective-permute-start | bytes 786440 | tf_op jit(solution)/shard_map/ppermute | solution.py:374
  109.1 20.0 %collective-permute-start.16 = (bf16[64,3072]{1,0:T(8,128)(2,1)}, bf16[64,3072]{1,0:T(8,128)(2,1)S(1)}, u32[]{:S(2)}, u32[]{:S(2)}) collective-permute-start(bf16[64,3072]{1,0:T(8,128)(2,1)} %get-tuple-element.24), channel_id=1, source_target_pairs={{1,2},{2,1},{5,6},{6,5},{9,10},{10,9},{13,14},{14,13},{17,18},{18,... | collective-permute-start | bytes 1179656 | tf_op jit(solution)/shard_map/ppermute | solution.py:371
  109.9 8.1 %collective-permute-start.21 = (bf16[1024,128]{1,0:T(8,128)(2,1)S(1)}, bf16[1024,128]{1,0:T(8,128)(2,1)}, u32[]{:S(2)}, u32[]{:S(2)}) collective-permute-start(bf16[1024,128]{1,0:T(8,128)(2,1)S(1)} %add_convert_fusion.5.a_ref), channel_id=1, source_target_pairs={{0,8},{8,0},{4,12},{12,4},{1,9},{9,1},{5,13},{13,5},{2,10},{10,2},... | collective-permute-start | bytes 786440 | tf_op jit(solution)/shard_map/ppermute | solution.py:373
  123.7 24.5 %collective-permute-start.22 = (bf16[256,128]{1,0:T(8,128)(2,1)S(1)}, bf16[256,128]{1,0:T(8,128)(2,1)S(1)}, u32[]{:S(2)}, u32[]{:S(2)}) collective-permute-start(bf16[256,128]{1,0:T(8,128)(2,1)S(1)} %get-tuple-element.20), channel_id=1, source_target_pairs={{0,1},{1,2},{2,3},{3,0},{4,5},{5,6},{6,7},{7,4},{8,9},{9,10},{10,1... | collective-permute-start | bytes 196616 | tf_op jit(solution)/shard_map/ppermute | solution.py:372
  125.6 22.6 %collective-permute-start.23 = (bf16[256,128]{1,0:T(8,128)(2,1)S(1)}, bf16[256,128]{1,0:T(8,128)(2,1)S(1)}, u32[]{:S(2)}, u32[]{:S(2)}) collective-permute-start(bf16[256,128]{1,0:T(8,128)(2,1)S(1)} %get-tuple-element.21), channel_id=1, source_target_pairs={{0,2},{1,3},{2,0},{3,1},{4,6},{5,7},{6,4},{7,5},{8,10},{9,11},{10,... | collective-permute-start | bytes 196616 | tf_op jit(solution)/shard_map/ppermute | solution.py:372
  126.7 21.5 %collective-permute-start.24 = (bf16[256,128]{1,0:T(8,128)(2,1)S(1)}, bf16[256,128]{1,0:T(8,128)(2,1)S(1)}, u32[]{:S(2)}, u32[]{:S(2)}) collective-permute-start(bf16[256,128]{1,0:T(8,128)(2,1)S(1)} %get-tuple-element.22), channel_id=1, source_target_pairs={{0,3},{1,0},{2,1},{3,2},{4,7},{5,4},{6,5},{7,6},{8,11},{9,8},{10,9... | collective-permute-start | bytes 196616 | tf_op jit(solution)/shard_map/ppermute | solution.py:372
  128.5 20.4 %collective-permute-start.19 = (bf16[64,3072]{1,0:T(8,128)(2,1)}, bf16[64,3072]{1,0:T(8,128)(2,1)S(1)}, u32[]{:S(2)}, u32[]{:S(2)}) collective-permute-start(bf16[64,3072]{1,0:T(8,128)(2,1)} %get-tuple-element.23), channel_id=1, source_target_pairs={{1,2},{2,1},{5,6},{6,5},{9,10},{10,9},{13,14},{14,13},{17,18},{18,... | collective-permute-start | bytes 1179656 | tf_op jit(solution)/shard_map/ppermute | solution.py:371
  129.4 19.5 %collective-permute-start.17 = (bf16[64,3072]{1,0:T(8,128)(2,1)S(1)}, bf16[64,3072]{1,0:T(8,128)(2,1)S(1)}, u32[]{:S(2)}, u32[]{:S(2)}) collective-permute-start(bf16[64,3072]{1,0:T(8,128)(2,1)S(1)} %fusion), channel_id=1, source_target_pairs={{0,1},{1,0},{2,3},{3,2},{4,5},{5,4},{6,7},{7,6},{8,9},{9,8},{10,11... | collective-permute-start | bytes 1179656 | tf_op jit(solution)/shard_map/ppermute | solution.py:370
  (35 other events, 160.7 us)

commit v2 on v1

--- a/solution.py
+++ b/solution.py
@@ -10,11 +10,15 @@
 
 F32 = jnp.float32
 BF16 = jnp.bfloat16
-VMEM_LIMIT = 40 * 1024 * 1024
+VMEM_LIMIT = 60 * 1024 * 1024
 CHUNKS = 5
 JOBS = 4
 PAIR = [(0, 1), (1, 0), (2, 3), (3, 2)]
-MIDDLE = [(1, 2), (2, 1)]
+MIDDLE = [
+    pair
+    for t in range(4)
+    for pair in ((t * 4 + 1, t * 4 + 2), (t * 4 + 2, t * 4 + 1), (t * 4, (t ^ 1) * 4), (t * 4 + 3, (t ^ 1) * 4 + 3))
+]
 TENSOR_X = [(0, 2), (2, 0), (1, 3), (3, 1)]
 TENSOR_CORE = [(0, 1), (1, 0), (2, 3), (3, 2)]
 
@@ -154,7 +158,32 @@
     )(*tables, place, *grads, *ups, features)
 
 
-def project_kernel(ids, owners, where_to, *refs):
+def arrivals(z, excess):
+    inner = (z == 1) | (z == 2)
+    mine = jnp.where(z < 2, 1, 2)
+    outer = jnp.where(z < 2, 0, 3)
+    far_in, far_out = 3 - mine, 3 - outer
+    top_in, top_out = excess == mine, excess == outer
+    top_far_in, top_far_out = excess == far_in, excess == far_out
+    spare, none = CHUNKS - 1, CHUNKS + 1
+    return [
+        z,
+        jnp.where(excess == z, spare, none),
+        jnp.where(inner, outer, mine),
+        jnp.where(inner, jnp.where(top_out, spare, none), jnp.where(top_in, spare, far_in)),
+        jnp.where(inner, none, jnp.where(top_in, far_in, jnp.where(top_far_in, spare, far_out))),
+        jnp.where(
+            inner, none, jnp.where(top_in | top_far_in, far_out, jnp.where(top_far_out, spare, none))
+        ),
+        jnp.where(inner, far_in, none),
+        jnp.where(inner, jnp.where(top_far_in, spare, far_out), none),
+        jnp.where(
+            inner, jnp.where(top_far_in, far_out, jnp.where(top_far_out, spare, none)), none
+        ),
+    ]
+
+
+def project_kernel(ids, owners, place, *refs):
     chunks = refs[:9]
     x_ref, out_ref, table_ref, sems = refs[9:]
     half, width = chunks[0].shape
@@ -164,21 +193,22 @@
 
     @pl.when(pl.program_id(0) == 0)
     def _():
+        where_to = arrivals(place[1], place[2])
         for k, chunk in enumerate(chunks):
-            place = where_to[k]
-
-            @pl.when(place < CHUNKS)
+            spot = where_to[k]
+
+            @pl.when(spot < CHUNKS)
             def _():
-                start = pl.multiple_of(place * half, half)
+                start = pl.multiple_of(spot * half, half)
                 pltpu.make_async_copy(chunk, table_ref.at[pl.ds(start, half), :], sems.at[k]).start()
 
         table_ref[CHUNKS * half :, :] = jnp.zeros((half, width), BF16)
         for k, chunk in enumerate(chunks):
-            place = where_to[k]
-
-            @pl.when(place < CHUNKS)
+            spot = where_to[k]
+
+            @pl.when(spot < CHUNKS)
             def _():
-                start = pl.multiple_of(place * half, half)
+                start = pl.multiple_of(spot * half, half)
                 pltpu.make_async_copy(chunk, table_ref.at[pl.ds(start, half), :], sems.at[k]).wait()
 
     full = lax.dot_general(
@@ -191,7 +221,7 @@
         out_ref[j * block : (j + 1) * block, :] = piece.astype(BF16)
 
 
-def project(ids, owners, where_to, chunks, features, tile):
+def project(ids, owners, place, chunks, features, tile):
     rows, width = features.shape
     half = chunks[0].shape[0]
     return pl.pallas_call(
@@ -212,51 +242,79 @@
         compiler_params=params(),
         cost_estimate=cost(2 * 6 * half * rows * width, 2 * (rows * width + 12 * half * width)),
         name="project",
-    )(ids, owners, where_to, *chunks, features)
-
-
-def base_kernel(lengths, place, g0, g1, g2, g3, wide_ref, weight_ref, table_ref, out_ref):
+    )(ids, owners, place, *chunks, features)
+
+
+def base_kernel(lengths, place, g0, g1, g2, g3, weight_ref, out_ref):
     t = place[0]
     quarter, values = g0.shape
     block = out_ref.shape[0] // lengths.shape[1]
     tile = out_ref.shape[1]
     for q, g in enumerate((g0, g1, g2, g3)):
         start = pl.multiple_of(jnp.bitwise_xor(t, q) * quarter, quarter)
-        base = lax.dot_general(
+        term = lax.dot_general(
             g[...], weight_ref[...], (((1,), (1,)), ((), ())), preferred_element_type=F32
         )
-        term = jnp.dot(wide_ref[pl.ds(start, quarter), :], table_ref[...], preferred_element_type=F32)
         for j in range(quarter // block):
             b = jnp.bitwise_xor(t, q) * (quarter // block) + j
             live = lax.broadcasted_iota(jnp.int32, (block, tile), 0) < lengths[0, b]
-            part = slice(j * block, (j + 1) * block)
-            out_ref[pl.ds(pl.multiple_of(start + j * block, block), block), :] = (
-                jnp.where(live, base[part], 0.0) + term[part]
+            out_ref[pl.ds(pl.multiple_of(start + j * block, block), block), :] = jnp.where(
+                live, term[j * block : (j + 1) * block], 0.0
             ).astype(BF16)
 
 
-def base(lengths, place, grads, wide, weight, table, tile):
-    width, values = weight.shape
+def base(lengths, place, grads, weight, half_index, tile):
+    width, values = weight.shape[0] // 2, weight.shape[1]
     quarter = grads[0].shape[0]
-    rows, deep = wide.shape
+    rows = 4 * quarter
+    first = half_index * (width // tile)
     return pl.pallas_call(
         base_kernel,
         grid=(width // tile,),
         in_specs=[smem()] * 2
         + [whole((quarter, values))] * 4
-        + [
-            whole((rows, deep)),
-            pl.BlockSpec((tile, values), lambda i: (i, 0)),
-            pl.BlockSpec((deep, tile), lambda i: (0, i)),
-        ],
+        + [pl.BlockSpec((tile, values), lambda i: (first + i, 0))],
         out_specs=pl.BlockSpec((rows, tile), lambda i: (0, i)),
         out_shape=jax.ShapeDtypeStruct((rows, width), BF16),
         compiler_params=params(),
-        cost_estimate=cost(
-            2 * rows * width * (values + deep), 2 * (rows * values + width * values + deep * width + rows * width)
-        ),
+        cost_estimate=cost(2 * rows * width * values, 2 * (rows * values + width * values + rows * width)),
+        name="base_term",
+    )(lengths, place, *grads, weight)
+
+
+def rows_kernel(wide_ref, table_ref, first_ref, second_ref, out_ref):
+    term = jnp.dot(wide_ref[...], table_ref[...], preferred_element_type=F32)
+    late = pl.program_id(0) >= pl.num_programs(0) // 2
+
+    @pl.when(jnp.logical_not(late))
+    def _():
+        out_ref[...] = (first_ref[...].astype(F32) + term).astype(BF16)
+
+    @pl.when(late)
+    def _():
+        out_ref[...] = (second_ref[...].astype(F32) + term).astype(BF16)
+
+
+def add_rows(wide, table, halves, tile):
+    rows, deep = wide.shape
+    width = table.shape[1]
+    steps = width // tile
+    half = steps // 2
+    return pl.pallas_call(
+        rows_kernel,
+        grid=(steps,),
+        in_specs=[
+            whole((rows, deep)),
+            pl.BlockSpec((deep, tile), lambda i: (0, i)),
+            pl.BlockSpec((rows, tile), lambda i: (0, jnp.minimum(i, half - 1))),
+            pl.BlockSpec((rows, tile), lambda i: (0, jnp.maximum(i - half, 0))),
+        ],
+        out_specs=pl.BlockSpec((rows, tile), lambda i: (0, i)),
+        out_shape=jax.ShapeDtypeStruct((rows, width), BF16),
+        compiler_params=params(),
+        cost_estimate=cost(2 * rows * width * deep, 2 * (2 * rows * width + deep * (rows + width))),
         name="grad_rows",
-    )(lengths, place, *grads, wide, weight, table)
+    )(wide, table, *halves)
 
 
 def part_up_kernel(norm, ids, lengths, owners, ranks, place, g0, g1, g2, g3, a_ref, b_ref, *rest):
@@ -310,8 +368,9 @@
     total = (
         jnp.concatenate([own0[...], own1[...]], axis=0).astype(F32)
         + jnp.concatenate([t1[...], t2[...]], axis=0).astype(F32)
-        + jnp.concatenate([n1[...], n2[...]], axis=0).astype(F32)
-    )
+    )
+    inner = (place[1] == 1) | (place[1] == 2)
+    total += jnp.where(inner, jnp.concatenate([n1[...], n2[...]], axis=0).astype(F32), 0.0)
     keep = jnp.where(place[1] == place[2], rank, half)
     rows = lax.broadcasted_iota(jnp.int32, total.shape, 0)
     out_ref[...] = jnp.where(rows < keep, total, 0.0).T
@@ -368,30 +427,33 @@
     top_far_in, top_far_out = excess == far_in, excess == far_out
 
     pair = lambda value: lax.ppermute(value, "job", PAIR)
-    middle = lambda value: lax.ppermute(value, "job", MIDDLE)
+    middle = lambda value: lax.ppermute(value, ("tensor", "job"), MIDDLE)
     shift = lambda value, d: lax.ppermute(value, "job", [(i, (i + d) % JOBS) for i in range(JOBS)])
     across = lambda value: lax.ppermute(value, "tensor", TENSOR_X)
     beside = lambda value: lax.ppermute(value, "tensor", TENSOR_CORE)
 
-    low, high = turn(adapter_down[0], tile)
+    tie = lax.optimization_barrier
+
+    up = adapter_up[0]
+    g0 = grad_out[0]
+    g2 = across(g0)
+    g1 = beside(g0)
+    up_z = jnp.stack([up] + [shift(up, d) for d in (1, 2, 3)])
+    up_x = across(up_z)
+
+    low, high = turn(adapter_down[0], local_width)
     s1 = pair(low)
     m1 = middle(low)
 
-    up = adapter_up[0]
-    g0 = grad_out[0]
-    up_z = jnp.stack([up] + [shift(up, d) for d in (1, 2, 3)])
-    g2 = across(g0)
-    g1 = beside(g0)
-    up_x = across(up_z)
+    s1, m1, up_x, g2, g1, up_z = tie((s1, m1, up_x, g2, g1, up_z))
     g3 = beside(g2)
     up_c = beside(jnp.stack([up_z, up_x]))
+    s2 = pair(jnp.where(inner & ~top_in, m1, high))
+    m2 = middle(jnp.where(top_in, high, s1))
+
     grads = (g0, g1, g2, g3)
     ups = (up_z, up_c[0], up_x, up_c[1])
-
-    s2 = pair(jnp.where(inner & ~top_in, m1, high))
-    m2 = middle(jnp.where(top_in, high, s1))
-
-    parts, wide = pull(tables, place, grads, ups, features, norm, tile)
+    parts, wide = pull(tables, place, grads, ups, features, norm, 1024)
 
     def chunk(index):
         return lax.dynamic_slice_in_dim(parts, index * half, half, 0)
@@ -402,50 +464,43 @@
     spare = CHUNKS - 1
     c4 = jnp.where(top_in | top_far_in, far_out, spare)
     c3 = jnp.where(top_in, far_in, jnp.where(top_far_in, spare, far_out))
-    s3 = pair(jnp.where(inner, jnp.where(top_in, m1, m2), chunk(c4)))
-    m3 = middle(jnp.where(top_in, s1, s2))
-    s4 = pair(jnp.where(inner, jnp.where(top_in, m2, m3), chunk(c3)))
-    n3 = middle(added(jnp.where(top_far_in, far_out, spare), s3, ~top_in))
-
-    none = jnp.int32(CHUNKS + 1)
-    here = [
-        jnp.where(inner, mine, outer),
-        jnp.where(excess == z, spare, none),
-        jnp.where(inner, outer, mine),
-        jnp.where(
-            inner, jnp.where(top_out, spare, none), jnp.where(top_in, spare, far_in)
-        ),
-        jnp.where(inner, none, jnp.where(top_in, far_in, jnp.where(top_far_in, spare, far_out))),
-        jnp.where(
-            inner, none, jnp.where(top_in | top_far_in, far_out, jnp.where(top_far_out, spare, none))
-        ),
-        jnp.where(inner, far_in, none),
-        jnp.where(inner, jnp.where(top_far_in, spare, far_out), none),
-        jnp.where(
-            inner, jnp.where(top_far_in, far_out, jnp.where(top_far_out, spare, none)), none
-        ),
-    ]
-    where_to = jnp.stack(here).astype(jnp.int32)
+    parts, s2, m2 = tie((parts, s2, m2))
+    to_s3 = jnp.where(inner, jnp.where(top_in, m1, m2), chunk(c4))
+    to_m3 = jnp.where(top_in, s1, s2)
+    to_s3, to_m3, *grads = tie((to_s3, to_m3, *grads))
+    s3 = pair(to_s3)
+    m3 = middle(to_m3)
+    base_a = base(block_length, place, grads, value_weight, 0, 768)
+    s3, m3, base_a = tie((s3, m3, base_a))
+    to_s4 = jnp.where(inner, jnp.where(top_in, m2, m3), chunk(c3))
+    to_n3 = added(jnp.where(top_far_in, far_out, spare), s3, ~top_in)
+    to_s4, to_n3, *grads = tie((to_s4, to_n3, *grads))
+    s4 = pair(to_s4)
+    n3 = middle(to_n3)
+    base_b = base(block_length, place, grads, value_weight, 1, 768)
+    s4, n3, base_b = tie((s4, n3, base_b))
+
     partial, table = project(
-        block_adapter, owner_slot, where_to, (low, high, s1, s2, s3, s4, m1, m2, m3), features, 512
-    )
-    both = (partial.astype(F32) + beside(partial).astype(F32)).astype(BF16)
+        block_adapter, owner_slot, place, (low, high, s1, s2, s3, s4, m1, m2, m3), features, 512
+    )
+    partial, s4, n3 = tie((partial, s4, n3))
+    beyond = beside(partial)
+    to_s5 = jnp.where(inner, added(spare, n3, ~top_in), chunk(jnp.where(top_in, spare, far_in)))
+    to_n2 = added(jnp.where(top_far_in, spare, far_out), jnp.where(top_in, s3, s4), True)
+    to_s5, to_n2, beyond = tie((to_s5, to_n2, beyond))
+    s5 = pair(to_s5)
+    n2 = middle(to_n2)
+    both = (partial.astype(F32) + beyond.astype(F32)).astype(BF16)
+    both, wide, table, base_a, base_b = tie((both, wide, table, base_a, base_b))
     other = across(both)
-
-    grad_rows = base(block_length, place, grads, wide, value_weight, table, tile)
-
-    s5 = pair(
-        jnp.where(
-            inner,
-            added(spare, n3, ~top_in),
-            chunk(jnp.where(top_in, spare, far_in)),
-        )
-    )
-    n2 = middle(added(jnp.where(top_far_in, spare, far_out), jnp.where(top_in, s3, s4), True))
-    s6 = pair(
-        jnp.where(inner, added(outer, jnp.where(top_in, n3, n2), True), chunk(mine))
-    )
-    n1 = middle(added(far_in, jnp.where(top_in, s4, s5), True))
+    grad_rows = add_rows(wide, table, (base_a, base_b), 512)
+    grad_rows, s5, n2 = tie((grad_rows, s5, n2))
+
+    to_s6 = jnp.where(inner, added(outer, jnp.where(top_in, n3, n2), True), chunk(mine))
+    to_n1 = added(far_in, jnp.where(top_in, s4, s5), True)
+    to_s6, to_n1, other = tie((to_s6, to_n1, other))
+    s6 = pair(to_s6)
+    n1 = middle(to_n1)
 
     ours = part_up(tables, place, grads, (both, other), norm)
     theirs = [shift(ours[d], d) for d in (1, 2, 3)]
@@ -453,7 +508,7 @@
     for value in theirs:
         grad_up = grad_up + value.astype(F32)
 
-    grad_down = last(place, parts, s6, n1, s5, n2, tile)
+    grad_down = last(place, parts, s6, n1, s5, n2, 1024)
     return (grad_rows[None], grad_down[None], grad_up[None])
 
 

time: 153 us -> 118 us (0.77)
  starting transfers between devices: 61.7 us -> 19.9 us
  Pallas kernels: 32.4 us -> 51.3 us
  local copies, waits for them, and re-layouts: 21.7 us -> 3.93 us
  other arithmetic: 11.9 us -> 16 us
  waiting for transfers between devices: 20.2 us -> 23.6 us
  between operations: 4.35 us -> 2.18 us
    ppermute x6, starting transfers between devices: 40.1 us -> 4.62 us  [on_device(): pair = lambda value: lax.ppermute(value, 'job', PAIR)]
    unnamed x68 -> x42, local copies, waits for them, and re-layouts: 21 us -> 3.09 us
    ppermute x6, waiting for transfers between devices: 0.02 us -> 11.5 us  [on_device(): lax.ppermute(value, 'job', [(i, (i + d) % JOBS) for i in range(JOBS)])]
    pallas_call x0 -> x1, Pallas kernels: none -> 10.4 us  [add_rows(): pl.pallas_call(rows_kernel, grid=(steps,), in_specs=[whole((rows, deep)),...]
    ppermute x3, waiting for transfers between devices: 11.4 us -> 3.62 us  [on_device(): across = lambda value: lax.ppermute(value, 'tensor', TENSOR_X)]
    ppermute x6, starting transfers between devices: 4.81 us -> 0.29 us  [on_device(): middle = lambda value: lax.ppermute(value, ('tensor', 'job'), MIDDLE)]
    select_n x3, other arithmetic: 2.09 us -> 5.12 us  [the longest x1 2.32 us: on_device(): to_s3 = jnp.where(inner, jnp.where(top_in, m1, m2), chunk(c4))]
    pallas_call x1, Pallas kernels: 6.04 us -> 8.83 us  [project(): pl.pallas_call(project_kernel, grid=(rows // tile,), in_specs=[smem()] *...]
  transfers between devices with their start and end apart: 25 -> 25, of which waited for: 3 -> 8; matrix products, arithmetic and copies ran while one was open for 7% -> 11% of each run, Pallas kernels for 18% -> 32%
where the time goes in v2:
time: 118 us; the launch traced here: 117 us
  Pallas kernels  51.3 us (43%)
  waiting for transfers between devices  23.6 us (20%)
  starting transfers between devices  19.9 us (17%)
  other arithmetic  16 us (14%)
  local copies, waits for them, and re-layouts  3.93 us (3%)
  between operations  2.18 us (2%)
    pallas_call x2, Pallas kernels, base(): pl.pallas_call(base_kernel, grid=(width // tile,), in_specs=[smem()] * 2...  14 us
    ppermute x6, waiting for transfers between devices, on_device(): lax.ppermute(value, 'job', [(i, (i + d) % JOBS) for i in range(JOBS)])  11.5 us
    pallas_call x1, Pallas kernels, add_rows(): pl.pallas_call(rows_kernel, grid=(steps,), in_specs=[whole((rows, deep)),...  10.4 us
    ppermute x6, starting transfers between devices, on_device(): lax.ppermute(value, 'job', [(i, (i + d) % JOBS) for i in range(JOBS)])  10.1 us
    pallas_call x1, Pallas kernels, project(): pl.pallas_call(project_kernel, grid=(rows // tile,), in_specs=[smem()] *...  8.83 us
    ppermute x6, waiting for transfers between devices, on_device(): pair = lambda value: lax.ppermute(value, 'job', PAIR)  8.52 us
    pallas_call x1, Pallas kernels, pull(): pl.pallas_call(functools.partial(pull_kernel, norm), grid=(width // tile,...  7.97 us
    pallas_call x1, Pallas kernels, last(): pl.pallas_call(last_kernel, grid_spec=pltpu.PrefetchScalarGridSpec(num_sc...  4.71 us
  transfers between devices with their start and end apart: 25, of which 8 were waited for; matrix products, arithmetic and copies ran while one was open for 11% of the time, Pallas kernels for 32%

profile of v2, /device:TPU:0, one launch (start us, length us, event | category | flops | bytes accessed | tf_op | source)
XLA Modules:
  0.0 116.9 jit_solution(1230316075844021948)
XLA Ops:
  1.1 2.6 %collective-permute-start.6 = (bf16[256,1024]{1,0:T(8,128)(2,1)}, bf16[256,1024]{1,0:T(8,128)(2,1)S(1)}, u32[]{:S(2)}, u32[]{:S(2)}) collective-permute-start(bf16[256,1024]{1,0:T(8,128)(2,1)} %bitcast.25), channel_id=1, source_target_pairs={{0,8},{8,0},{4,12},{12,4},{1,9},{9,1},{5,13},{13,5},{2,10},{10,2},... | collective-permute-start | bytes 1572872 | tf_op jit(solution)/shard_map/ppermute | solution.py:432
  3.7 3.6 %collective-permute-start.4 = (bf16[256,128]{1,0:T(8,128)(2,1)}, bf16[256,128]{1,0:T(8,128)(2,1)S(1)}, u32[]{:S(2)}, u32[]{:S(2)}) collective-permute-start(bf16[256,128]{1,0:T(8,128)(2,1)} %bitcast.33), channel_id=1, source_target_pairs={{0,3},{1,0},{2,1},{3,2},{4,7},{5,4},{6,5},{7,6},{8,11},{9,8},{10,9... | collective-permute-start | bytes 196616 | tf_op jit(solution)/shard_map/ppermute | solution.py:431
  8.3 2.3 %turn_adapter.1 = (bf16[64,3072]{1,0:T(8,128)(2,1)}, bf16[64,3072]{1,0:T(8,128)(2,1)}) custom-call(bf16[3072,128]{1,0:T(8,128)(2,1)} %bitcast.32), custom_call_target="tpu_custom_call" | custom-call | bytes 1572864 | tf_op jit(solution)/shard_map/turn_adapter/pallas_call | solution.py:53
  10.6 3.7 %collective-permute-done.3 = bf16[256,128]{1,0:T(8,128)(2,1)S(1)} collective-permute-done((bf16[256,128]{1,0:T(8,128)(2,1)}, bf16[256,128]{1,0:T(8,128)(2,1)S(1)}, u32[]{:S(2)}, u32[]{:S(2)}) %collective-permute-start.3) | collective-permute-done | bytes 65568 | tf_op jit(solution)/shard_map/ppermute | solution.py:431
  19.7 3.6 %collective-permute-done.5.u2 = bf16[4,256,128]{2,1,0:T(8,128)(2,1)S(1)} collective-permute-done((bf16[4,256,128]{2,1,0:T(8,128)(2,1)S(1)}, bf16[4,256,128]{2,1,0:T(8,128)(2,1)S(1)}, u32[]{:S(2)}, u32[]{:S(2)}) %collective-permute-start.5) | collective-permute-done | bytes 262176 | tf_op jit(solution)/shard_map/ppermute | solution.py:432
  23.3 2.1 %collective-permute-done.refs_2_ = bf16[64,3072]{1,0:T(8,128)(2,1)S(1)} collective-permute-done((bf16[64,3072]{1,0:T(8,128)(2,1)}, bf16[64,3072]{1,0:T(8,128)(2,1)S(1)}, u32[]{:S(2)}, u32[]{:S(2)}) %collective-permute-start) | collective-permute-done | bytes 393248 | tf_op jit(solution)/shard_map/ppermute | solution.py:429
  26.0 1.8 %broadcast_select_fusion.1 = (bf16[64,3072]{1,0:T(8,128)(2,1)}, bf16[64,3072]{1,0:T(8,128)(2,1)S(1)}) fusion(bf16[64,3072]{1,0:T(8,128)(2,1)} %get-tuple-element.58.refs_1_, bf16[64,3072]{1,0:T(8,128)(2,1)S(1)} %collective-permute-done.refs_2_, pred[]{:T(512)S(6)} %eq.14, bf16[64,3072]{1,0:T(8,128)(2,1)S(1)} %collective-permute-done.1.refs_6_, pred[]{:T(512)S(6)} %and.5), kind=kLoop, calls=%fused_computation.12 | loop fusion | flops 393216 | bytes 1966082 | tf_op jit(solution)/shard_map/jit(_where)/select_n | solution.py:452
  29.8 8.0 %pull_and_part_down.1 = (bf16[320,3072]{1,0:T(8,128)(2,1)}, bf16[1024,384]{1,0:T(8,128)(2,1)}) custom-call(s32[1,8]{1,0:T(1,128)} %ids.5, s32[1,8]{1,0:T(1,128)} %lengths.7, s32[4]{0:T(128)} %owners.5, s32[4]{0:T(128)} %ranks.3, s32[3]{0:T(128)} %pad_add_fusion.place, bf16[256,1024]{1,0:T(8,128)(2,1)} %bitcast.26, bf16[256,1024]{1,0:T(8,128)(2,1)} %copy-done.9, ...), custom_call_target="tpu_custom_call" | custom-call | flops 2013265920 | bytes 12451840 | tf_op jit(solution)/shard_map/pull_and_part_down/pallas_call | solution.py:136
  37.8 1.6 %collective-permute-done.10.refs_3_ = bf16[64,3072]{1,0:T(8,128)(2,1)S(1)} collective-permute-done((bf16[64,3072]{1,0:T(8,128)(2,1)S(1)}, bf16[64,3072]{1,0:T(8,128)(2,1)S(1)}, u32[]{:S(2)}, u32[]{:S(2)}) %collective-permute-start.10) | collective-permute-done | bytes 393248 | tf_op jit(solution)/shard_map/ppermute | solution.py:429
  39.4 2.3 %dynamic-slice_select_fusion.1 = (bf16[64,3072]{1,0:T(8,128)(2,1)}, bf16[64,3072]{1,0:T(8,128)(2,1)}) fusion(bf16[320,3072]{1,0:T(8,128)(2,1)} %get-tuple-element.68.own0.own1, s32[]{:T(128)S(6)} %select_n.140, bf16[64,3072]{1,0:T(8,128)(2,1)S(1)} %collective-permute-done.1.refs_6_, bf16[64,3072]{1,0:T(8,128)(2,1)S(1)} %collective-permute-done.11.refs_7_, ...), kind=kLoop, calls=%fused_computation.10 | loop fusion | flops 589824 | bytes 2752518 | tf_op jit(solution)/shard_map/jit(_where)/select_n | solution.py:468
  42.1 7.1 %base_term.2.first_ref = bf16[1024,1536]{1,0:T(8,128)(2,1)} custom-call(s32[1,8]{1,0:T(1,128)} %lengths.7, s32[3]{0:T(128)} %pad_add_fusion.place, bf16[256,1024]{1,0:T(8,128)(2,1)} %bitcast.27, bf16[256,1024]{1,0:T(8,128)(2,1)} %copy-done.9, bf16[256,1024]{1,0:T(8,128)(2,1)} %copy-done.10, bf16[256,1024]{1,0:T(8,128)(2,1)} %copy-done.11, ...), custom_call_target="tpu_custom_call" | custom-call | flops 3221225472 | bytes 8388608 | tf_op jit(solution)/shard_map/base_term/pallas_call | solution.py:271
  49.1 3.5 %collective-permute-done.12.refs_4_ = bf16[64,3072]{1,0:T(8,128)(2,1)S(1)} collective-permute-done((bf16[64,3072]{1,0:T(8,128)(2,1)}, bf16[64,3072]{1,0:T(8,128)(2,1)S(1)}, u32[]{:S(2)}, u32[]{:S(2)}) %collective-permute-start.12) | collective-permute-done | bytes 393248 | tf_op jit(solution)/shard_map/ppermute | solution.py:429
  54.5 1.6 %collective-permute-start.14 = (bf16[64,3072]{1,0:T(8,128)(2,1)}, bf16[64,3072]{1,0:T(8,128)(2,1)S(1)}, u32[]{:S(2)}, u32[]{:S(2)}) collective-permute-start(bf16[64,3072]{1,0:T(8,128)(2,1)} %dynamic-slice_select_fusion), channel_id=1, source_target_pairs={{0,1},{1,0},{2,3},{3,2},{4,5},{5,4},{6,7},{7,6},{8,9},{9,8},{10,11... | collective-permute-start | bytes 1179656 | tf_op jit(solution)/shard_map/ppermute | solution.py:429
  56.1 7.0 %base_term.3.second_ref = bf16[1024,1536]{1,0:T(8,128)(2,1)} custom-call(s32[1,8]{1,0:T(1,128)} %lengths.7, s32[3]{0:T(128)} %pad_add_fusion.place, bf16[256,1024]{1,0:T(8,128)(2,1)} %bitcast.28, bf16[256,1024]{1,0:T(8,128)(2,1)} %copy-done.9, bf16[256,1024]{1,0:T(8,128)(2,1)} %copy-done.10, bf16[256,1024]{1,0:T(8,128)(2,1)} %copy-done.11, ...), custom_call_target="tpu_custom_call" | custom-call | flops 3221225472 | bytes 8388608 | tf_op jit(solution)/shard_map/base_term/pallas_call | solution.py:271
  65.2 8.8 %project.1 = (bf16[1024,128]{1,0:T(8,128)(2,1)}, bf16[384,3072]{1,0:T(8,128)(2,1)}) custom-call(s32[1,8]{1,0:T(1,128)} %ids.5, s32[4]{0:T(128)} %owners.5, s32[3]{0:T(128)} %pad_add_fusion.place, bf16[64,3072]{1,0:T(8,128)(2,1)} %get-tuple-element.57.refs_0_, bf16[64,3072]{1,0:T(8,128)(2,1)} %get-tuple-element.58.refs_1_, bf16[64,3072]{1,0:T(8,128)(2,1)} %copy-done.2, ...), custom_call_target="tpu_custom_call" | custom-call | flops 2415919104 | bytes 11010048 | tf_op jit(solution)/shard_map/project/pallas_call | solution.py:227
  74.2 1.9 %add_convert_fusion.2 = bf16[64,3072]{1,0:T(8,128)(2,1)} fusion(bf16[64,3072]{1,0:T(8,128)(2,1)S(1)} %copy-done.4, bf16[64,3072]{1,0:T(8,128)(2,1)} %copy-done.5, bf16[320,3072]{1,0:T(8,128)(2,1)S(1)} %copy-done, s32[]{:T(128)S(6)} %select_n.156, pred[]{:T(512)S(6)} %eq.14), kind=kLoop, calls=%fused_computation.2 | loop fusion | flops 983040 | bytes 1572869 | tf_op jit(solution)/shard_map/convert_element_type | solution.py:462
  79.4 10.4 %grad_rows.1 = bf16[1024,3072]{1,0:T(8,128)(2,1)} custom-call(bf16[1024,384]{1,0:T(8,128)(2,1)} %get-tuple-element.94.wide_ref, bf16[384,3072]{1,0:T(8,128)(2,1)} %get-tuple-element.95.table_ref, bf16[1024,1536]{1,0:T(8,128)(2,1)} %base_term.2.first_ref, bf16[1024,1536]{1,0:T(8,128)(2,1)} %base_term.3.second_ref), custom_call_target="tpu_custom_call" | custom-call | flops 2415919104 | bytes 15728640 | tf_op jit(solution)/shard_map/grad_rows/pallas_call | solution.py:303
  92.8 3.1 %part_up.1 = (bf16[256,128]{1,0:T(8,128)(2,1)}, bf16[256,128]{1,0:T(8,128)(2,1)}, bf16[256,128]{1,0:T(8,128)(2,1)}, bf16[256,128]{1,0:T(8,128)(2,1)}) custom-call(s32[1,8]{1,0:T(1,128)} %ids.5, s32[1,8]{1,0:T(1,128)} %lengths.7, s32[4]{0:T(128)} %owners.5, s32[4]{0:T(128)} %ranks.3, s32[3]{0:T(128)} %pad_add_fusion.place, bf16[256,1024]{1,0:T(8,128)(2,1)} %bitcast.29, ...), custom_call_target="tpu_custom_call" | custom-call | flops 201326592 | bytes 2621440 | tf_op jit(solution)/shard_map/part_up/pallas_call | solution.py:350
  96.0 1.6 %collective-permute-start.22 = (bf16[256,128]{1,0:T(8,128)(2,1)}, bf16[256,128]{1,0:T(8,128)(2,1)S(1)}, u32[]{:S(2)}, u32[]{:S(2)}) collective-permute-start(bf16[256,128]{1,0:T(8,128)(2,1)} %get-tuple-element.108), channel_id=1, source_target_pairs={{0,1},{1,2},{2,3},{3,0},{4,5},{5,6},{6,7},{7,4},{8,9},{9,10},{10,1... | collective-permute-start | bytes 196616 | tf_op jit(solution)/shard_map/ppermute | solution.py:431
  98.9 2.5 %collective-permute-start.24 = (bf16[256,128]{1,0:T(8,128)(2,1)}, bf16[256,128]{1,0:T(8,128)(2,1)S(1)}, u32[]{:S(2)}, u32[]{:S(2)}) collective-permute-start(bf16[256,128]{1,0:T(8,128)(2,1)} %get-tuple-element.110), channel_id=1, source_target_pairs={{0,3},{1,0},{2,1},{3,2},{4,7},{5,4},{6,5},{7,6},{8,11},{9,8},{10,9... | collective-permute-start | bytes 196616 | tf_op jit(solution)/shard_map/ppermute | solution.py:431
  101.4 5.3 %collective-permute-done.22 = bf16[256,128]{1,0:T(8,128)(2,1)S(1)} collective-permute-done((bf16[256,128]{1,0:T(8,128)(2,1)}, bf16[256,128]{1,0:T(8,128)(2,1)S(1)}, u32[]{:S(2)}, u32[]{:S(2)}) %collective-permute-start.22) | collective-permute-done | bytes 65568 | tf_op jit(solution)/shard_map/ppermute | solution.py:431
  106.8 2.4 %collective-permute-done.23 = bf16[256,128]{1,0:T(8,128)(2,1)S(1)} collective-permute-done((bf16[256,128]{1,0:T(8,128)(2,1)}, bf16[256,128]{1,0:T(8,128)(2,1)S(1)}, u32[]{:S(2)}, u32[]{:S(2)}) %collective-permute-start.23) | collective-permute-done | bytes 65568 | tf_op jit(solution)/shard_map/ppermute | solution.py:431
  109.2 1.5 %add_bitcast_fusion = f32[1,256,128]{2,1,0:T(8,128)} fusion(bf16[256,128]{1,0:T(8,128)(2,1)S(1)} %collective-permute-done.24, bf16[256,128]{1,0:T(8,128)(2,1)S(1)} %collective-permute-done.23, bf16[256,128]{1,0:T(8,128)(2,1)S(1)} %collective-permute-done.22, bf16[256,128]{1,0:T(8,128)(2,1)} %get-tuple-element.107), kind=kLoop, calls=%fused_computation.17 | loop fusion | flops 229376 | bytes 393216 | tf_op jit(solution)/shard_map/broadcast_in_dim | solution.py:512
  112.2 4.7 %grad_down.1 = f32[3072,128]{1,0:T(8,128)} custom-call(s32[3]{0:T(128)} %pad_add_fusion.place, bf16[320,3072]{1,0:T(8,128)(2,1)} %get-tuple-element.68.own0.own1, bf16[320,3072]{1,0:T(8,128)(2,1)} %get-tuple-element.68.own0.own1, bf16[64,3072]{1,0:T(8,128)(2,1)} %copy-done.18, bf16[64,3072]{1,0:T(8,128)(2,1)} %copy-done.19, bf16[64,3072]{1,0:T(8,128)(2,1)} %copy-done.12, ...), custom_call_target="tpu_custom_call" | custom-call | bytes 3932160 | tf_op jit(solution)/shard_map/grad_down/pallas_call | solution.py:382
  (91 shorter events, 21.8 us)
Async XLA Ops:
  0.6 24.8 %collective-permute-start.7 = (bf16[256,1024]{1,0:T(8,128)(2,1)}, bf16[256,1024]{1,0:T(8,128)(2,1)S(1)}, u32[]{:S(2)}, u32[]{:S(2)}) collective-permute-start(bf16[256,1024]{1,0:T(8,128)(2,1)} %bitcast.24), channel_id=1, source_target_pairs={{0,4},{4,0},{8,12},{12,8},{1,5},{5,1},{9,13},{13,9},{2,6},{6,2},{1... | collective-permute-start | bytes 1572872 | tf_op jit(solution)/shard_map/ppermute | solution.py:433
  1.1 24.2 %collective-permute-start.6 = (bf16[256,1024]{1,0:T(8,128)(2,1)}, bf16[256,1024]{1,0:T(8,128)(2,1)S(1)}, u32[]{:S(2)}, u32[]{:S(2)}) collective-permute-start(bf16[256,1024]{1,0:T(8,128)(2,1)} %bitcast.25), channel_id=1, source_target_pairs={{0,8},{8,0},{4,12},{12,4},{1,9},{9,1},{5,13},{13,5},{2,10},{10,2},... | collective-permute-start | bytes 1572872 | tf_op jit(solution)/shard_map/ppermute | solution.py:432
  3.7 6.9 %collective-permute-start.4 = (bf16[256,128]{1,0:T(8,128)(2,1)}, bf16[256,128]{1,0:T(8,128)(2,1)S(1)}, u32[]{:S(2)}, u32[]{:S(2)}) collective-permute-start(bf16[256,128]{1,0:T(8,128)(2,1)} %bitcast.33), channel_id=1, source_target_pairs={{0,3},{1,0},{2,1},{3,2},{4,7},{5,4},{6,5},{7,6},{8,11},{9,8},{10,9... | collective-permute-start | bytes 196616 | tf_op jit(solution)/shard_map/ppermute | solution.py:431
  7.3 7.0 %collective-permute-start.3 = (bf16[256,128]{1,0:T(8,128)(2,1)}, bf16[256,128]{1,0:T(8,128)(2,1)S(1)}, u32[]{:S(2)}, u32[]{:S(2)}) collective-permute-start(bf16[256,128]{1,0:T(8,128)(2,1)} %bitcast.34), channel_id=1, source_target_pairs={{0,2},{1,3},{2,0},{3,1},{4,6},{5,7},{6,4},{7,5},{8,10},{9,11},{10,... | collective-permute-start | bytes 196616 | tf_op jit(solution)/shard_map/ppermute | solution.py:431
  7.3 7.0 %collective-permute-start.2 = (bf16[256,128]{1,0:T(8,128)(2,1)}, bf16[256,128]{1,0:T(8,128)(2,1)S(1)}, u32[]{:S(2)}, u32[]{:S(2)}) collective-permute-start(bf16[256,128]{1,0:T(8,128)(2,1)} %bitcast.35), channel_id=1, source_target_pairs={{0,1},{1,2},{2,3},{3,0},{4,5},{5,6},{6,7},{7,4},{8,9},{9,10},{10,1... | collective-permute-start | bytes 196616 | tf_op jit(solution)/shard_map/ppermute | solution.py:431
  10.6 12.7 %collective-permute-start.1 = (bf16[64,3072]{1,0:T(8,128)(2,1)}, bf16[64,3072]{1,0:T(8,128)(2,1)S(1)}, u32[]{:S(2)}, u32[]{:S(2)}) collective-permute-start(bf16[64,3072]{1,0:T(8,128)(2,1)} %get-tuple-element.57.refs_0_), channel_id=1, source_target_pairs={{1,2},{2,1},{0,4},{3,7},{5,6},{6,5},{4,0},{7,3},{9,10},{10,9},{8,1... | collective-permute-start | bytes 1179656 | tf_op jit(solution)/shard_map/ppermute | solution.py:430
  14.3 11.1 %collective-permute-start = (bf16[64,3072]{1,0:T(8,128)(2,1)}, bf16[64,3072]{1,0:T(8,128)(2,1)S(1)}, u32[]{:S(2)}, u32[]{:S(2)}) collective-permute-start(bf16[64,3072]{1,0:T(8,128)(2,1)} %get-tuple-element.57.refs_0_), channel_id=1, source_target_pairs={{0,1},{1,0},{2,3},{3,2},{4,5},{5,4},{6,7},{7,6},{8,9},{9,8},{10,11... | collective-permute-start | bytes 1179656 | tf_op jit(solution)/shard_map/ppermute | solution.py:429
  15.2 8.1 %collective-permute-start.5 = (bf16[4,256,128]{2,1,0:T(8,128)(2,1)S(1)}, bf16[4,256,128]{2,1,0:T(8,128)(2,1)S(1)}, u32[]{:S(2)}, u32[]{:S(2)}) collective-permute-start(bf16[4,256,128]{2,1,0:T(8,128)(2,1)S(1)} %pad_maximum_fusion.1.u0), channel_id=1, source_target_pairs={{0,8},{8,0},{4,12},{12,4},{1,9},{9,1},{5,13},{13,5},{2,10},{10,2},... | collective-permute-start | bytes 786440 | tf_op jit(solution)/shard_map/ppermute | solution.py:432
  25.5 3.4 %collective-permute-start.8 = (bf16[256,1024]{1,0:T(8,128)(2,1)S(1)}, bf16[256,1024]{1,0:T(8,128)(2,1)S(1)}, u32[]{:S(2)}, u32[]{:S(2)}) collective-permute-start(bf16[256,1024]{1,0:T(8,128)(2,1)S(1)} %collective-permute-done.6.g2), channel_id=1, source_target_pairs={{0,4},{4,0},{8,12},{12,8},{1,5},{5,1},{9,13},{13,9},{2,6},{6,2},{1... | collective-permute-start | bytes 1572872 | tf_op jit(solution)/shard_map/ppermute | solution.py:433
  27.8 9.9 %collective-permute-start.11 = (bf16[64,3072]{1,0:T(8,128)(2,1)}, bf16[64,3072]{1,0:T(8,128)(2,1)S(1)}, u32[]{:S(2)}, u32[]{:S(2)}) collective-permute-start(bf16[64,3072]{1,0:T(8,128)(2,1)} %get-tuple-element.113), channel_id=1, source_target_pairs={{1,2},{2,1},{0,4},{3,7},{5,6},{6,5},{4,0},{7,3},{9,10},{10,9},{8,1... | collective-permute-start | bytes 1179656 | tf_op jit(solution)/shard_map/ppermute | solution.py:430
  27.9 11.5 %collective-permute-start.10 = (bf16[64,3072]{1,0:T(8,128)(2,1)S(1)}, bf16[64,3072]{1,0:T(8,128)(2,1)S(1)}, u32[]{:S(2)}, u32[]{:S(2)}) collective-permute-start(bf16[64,3072]{1,0:T(8,128)(2,1)S(1)} %get-tuple-element.114), channel_id=1, source_target_pairs={{0,1},{1,0},{2,3},{3,2},{4,5},{5,4},{6,7},{7,6},{8,9},{9,8},{10,11... | collective-permute-start | bytes 1179656 | tf_op jit(solution)/shard_map/ppermute | solution.py:429
  41.7 10.9 %collective-permute-start.12 = (bf16[64,3072]{1,0:T(8,128)(2,1)}, bf16[64,3072]{1,0:T(8,128)(2,1)S(1)}, u32[]{:S(2)}, u32[]{:S(2)}) collective-permute-start(bf16[64,3072]{1,0:T(8,128)(2,1)} %get-tuple-element.69), channel_id=1, source_target_pairs={{0,1},{1,0},{2,3},{3,2},{4,5},{5,4},{6,7},{7,6},{8,9},{9,8},{10,11... | collective-permute-start | bytes 1179656 | tf_op jit(solution)/shard_map/ppermute | solution.py:429
  42.1 10.5 %collective-permute-start.13 = (bf16[64,3072]{1,0:T(8,128)(2,1)}, bf16[64,3072]{1,0:T(8,128)(2,1)S(1)}, u32[]{:S(2)}, u32[]{:S(2)}) collective-permute-start(bf16[64,3072]{1,0:T(8,128)(2,1)} %get-tuple-element.70), channel_id=1, source_target_pairs={{1,2},{2,1},{0,4},{3,7},{5,6},{6,5},{4,0},{7,3},{9,10},{10,9},{8,1... | collective-permute-start | bytes 1179656 | tf_op jit(solution)/shard_map/ppermute | solution.py:430
  54.5 10.0 %collective-permute-start.14 = (bf16[64,3072]{1,0:T(8,128)(2,1)}, bf16[64,3072]{1,0:T(8,128)(2,1)S(1)}, u32[]{:S(2)}, u32[]{:S(2)}) collective-permute-start(bf16[64,3072]{1,0:T(8,128)(2,1)} %dynamic-slice_select_fusion), channel_id=1, source_target_pairs={{0,1},{1,0},{2,3},{3,2},{4,5},{5,4},{6,7},{7,6},{8,9},{9,8},{10,11... | collective-permute-start | bytes 1179656 | tf_op jit(solution)/shard_map/ppermute | solution.py:429
  56.1 8.4 %collective-permute-start.15 = (bf16[64,3072]{1,0:T(8,128)(2,1)}, bf16[64,3072]{1,0:T(8,128)(2,1)S(1)}, u32[]{:S(2)}, u32[]{:S(2)}) collective-permute-start(bf16[64,3072]{1,0:T(8,128)(2,1)} %add_convert_fusion.4), channel_id=1, source_target_pairs={{1,2},{2,1},{0,4},{3,7},{5,6},{6,5},{4,0},{7,3},{9,10},{10,9},{8,1... | collective-permute-start | bytes 1179656 | tf_op jit(solution)/shard_map/ppermute | solution.py:430
  74.1 3.0 %collective-permute-start.16 = (bf16[1024,128]{1,0:T(8,128)(2,1)}, bf16[1024,128]{1,0:T(8,128)(2,1)S(1)}, u32[]{:S(2)}, u32[]{:S(2)}) collective-permute-start(bf16[1024,128]{1,0:T(8,128)(2,1)} %get-tuple-element.86), channel_id=1, source_target_pairs={{0,4},{4,0},{8,12},{12,8},{1,5},{5,1},{9,13},{13,9},{2,6},{6,2},{1... | collective-permute-start | bytes 786440 | tf_op jit(solution)/shard_map/ppermute | solution.py:433
  77.1 12.7 %collective-permute-start.17 = (bf16[64,3072]{1,0:T(8,128)(2,1)}, bf16[64,3072]{1,0:T(8,128)(2,1)S(1)}, u32[]{:S(2)}, u32[]{:S(2)}) collective-permute-start(bf16[64,3072]{1,0:T(8,128)(2,1)} %fusion), channel_id=1, source_target_pairs={{0,1},{1,0},{2,3},{3,2},{4,5},{5,4},{6,7},{7,6},{8,9},{9,8},{10,11... | collective-permute-start | bytes 1179656 | tf_op jit(solution)/shard_map/ppermute | solution.py:429
  78.5 11.3 %collective-permute-start.18 = (bf16[64,3072]{1,0:T(8,128)(2,1)}, bf16[64,3072]{1,0:T(8,128)(2,1)S(1)}, u32[]{:S(2)}, u32[]{:S(2)}) collective-permute-start(bf16[64,3072]{1,0:T(8,128)(2,1)} %add_convert_fusion.2), channel_id=1, source_target_pairs={{1,2},{2,1},{0,4},{3,7},{5,6},{6,5},{4,0},{7,3},{9,10},{10,9},{8,1... | collective-permute-start | bytes 1179656 | tf_op jit(solution)/shard_map/ppermute | solution.py:430
  78.8 13.0 %collective-permute-start.19 = (bf16[1024,128]{1,0:T(8,128)(2,1)S(1)}, bf16[1024,128]{1,0:T(8,128)(2,1)}, u32[]{:S(2)}, u32[]{:S(2)}) collective-permute-start(bf16[1024,128]{1,0:T(8,128)(2,1)S(1)} %add_convert_fusion.5.a_ref), channel_id=1, source_target_pairs={{0,8},{8,0},{4,12},{12,4},{1,9},{9,1},{5,13},{13,5},{2,10},{10,2},... | collective-permute-start | bytes 786440 | tf_op jit(solution)/shard_map/ppermute | solution.py:432
  91.8 18.9 %collective-permute-start.20 = (bf16[64,3072]{1,0:T(8,128)(2,1)}, bf16[64,3072]{1,0:T(8,128)(2,1)S(1)}, u32[]{:S(2)}, u32[]{:S(2)}) collective-permute-start(bf16[64,3072]{1,0:T(8,128)(2,1)} %fusion.1), channel_id=1, source_target_pairs={{0,1},{1,0},{2,3},{3,2},{4,5},{5,4},{6,7},{7,6},{8,9},{9,8},{10,11... | collective-permute-start | bytes 1179656 | tf_op jit(solution)/shard_map/ppermute | solution.py:429
  92.8 17.9 %collective-permute-start.21 = (bf16[64,3072]{1,0:T(8,128)(2,1)}, bf16[64,3072]{1,0:T(8,128)(2,1)S(1)}, u32[]{:S(2)}, u32[]{:S(2)}) collective-permute-start(bf16[64,3072]{1,0:T(8,128)(2,1)} %add_convert_fusion), channel_id=1, source_target_pairs={{1,2},{2,1},{0,4},{3,7},{5,6},{6,5},{4,0},{7,3},{9,10},{10,9},{8,1... | collective-permute-start | bytes 1179656 | tf_op jit(solution)/shard_map/ppermute | solution.py:430
  96.0 10.8 %collective-permute-start.22 = (bf16[256,128]{1,0:T(8,128)(2,1)}, bf16[256,128]{1,0:T(8,128)(2,1)S(1)}, u32[]{:S(2)}, u32[]{:S(2)}) collective-permute-start(bf16[256,128]{1,0:T(8,128)(2,1)} %get-tuple-element.108), channel_id=1, source_target_pairs={{0,1},{1,2},{2,3},{3,0},{4,5},{5,6},{6,7},{7,4},{8,9},{9,10},{10,1... | collective-permute-start | bytes 196616 | tf_op jit(solution)/shard_map/ppermute | solution.py:431
  97.5 11.7 %collective-permute-start.23 = (bf16[256,128]{1,0:T(8,128)(2,1)}, bf16[256,128]{1,0:T(8,128)(2,1)S(1)}, u32[]{:S(2)}, u32[]{:S(2)}) collective-permute-start(bf16[256,128]{1,0:T(8,128)(2,1)} %get-tuple-element.109), channel_id=1, source_target_pairs={{0,2},{1,3},{2,0},{3,1},{4,6},{5,7},{6,4},{7,5},{8,10},{9,11},{10,... | collective-permute-start | bytes 196616 | tf_op jit(solution)/shard_map/ppermute | solution.py:431
  98.9 10.3 %collective-permute-start.24 = (bf16[256,128]{1,0:T(8,128)(2,1)}, bf16[256,128]{1,0:T(8,128)(2,1)S(1)}, u32[]{:S(2)}, u32[]{:S(2)}) collective-permute-start(bf16[256,128]{1,0:T(8,128)(2,1)} %get-tuple-element.110), channel_id=1, source_target_pairs={{0,3},{1,0},{2,1},{3,2},{4,7},{5,4},{6,5},{7,6},{8,11},{9,8},{10,9... | collective-permute-start | bytes 196616 | tf_op jit(solution)/shard_map/ppermute | solution.py:431
  (22 other events, 160.1 us)

commit v3 on v2

--- a/solution.py
+++ b/solution.py
@@ -10,7 +10,7 @@
 
 F32 = jnp.float32
 BF16 = jnp.bfloat16
-VMEM_LIMIT = 60 * 1024 * 1024
+VMEM_LIMIT = 28 * 1024 * 1024
 CHUNKS = 5
 JOBS = 4
 PAIR = [(0, 1), (1, 0), (2, 3), (3, 2)]
@@ -33,6 +33,10 @@
 
 def whole(shape):
     return pl.BlockSpec(shape, lambda *_: (0,) * len(shape))
+
+
+def far(value):
+    return pltpu.with_memory_space_constraint(value, pltpu.HBM)
 
 
 def smem():
@@ -98,11 +102,36 @@
     return jnp.where(lanes < half, lower, upper)
 
 
-def pull_kernel(norm, ids, lengths, owners, ranks, place, g0, g1, g2, g3, u0, u1, u2, u3, x_ref,
-                part_ref, wide_ref, up, turned):
+def roles(z, excess):
+    inner = (z == 1) | (z == 2)
+    mine = jnp.where(z < 2, 1, 2)
+    far_in = 3 - mine
+    far_out = jnp.where(z < 2, 3, 0)
+    top_in, top_far_in = excess == mine, excess == far_in
+    spare = CHUNKS - 1
+    return [
+        jnp.where(
+            inner, jnp.where(top_far_in, far_out, spare), jnp.where(top_in | top_far_in, far_out, spare)
+        ),
+        jnp.where(
+            inner,
+            jnp.where(top_far_in, spare, far_out),
+            jnp.where(top_in, far_in, jnp.where(top_far_in, spare, far_out)),
+        ),
+        jnp.where(inner | top_in, spare, far_in),
+        jnp.bitwise_xor(z, 1),
+        far_in,
+        z,
+        jnp.int32(spare),
+    ]
+
+
+def pull_kernel(norm, ids, lengths, owners, ranks, place, g0, g1, g2, g3, u0, u1, u2, u3, x_ref, *rest):
+    parts, (wide_ref, up, turned, sums) = rest[:7], rest[7:]
     t, z = place[0], place[1]
     quarter, values = g0.shape
     rank = u0.shape[2]
+    half = rank // 2
     block = x_ref.shape[0] // ids.shape[1]
 
     @pl.when(pl.program_id(0) == 0)
@@ -110,7 +139,7 @@
         for q, u in enumerate((u0, u1, u2, u3)):
             start = pl.multiple_of(jnp.bitwise_xor(t, q) * quarter, quarter)
             for d in range(JOBS):
-                slot = lax.rem(z - d + JOBS, JOBS)
+                slot = jnp.bitwise_xor(z, d)
                 up[slot, pl.ds(start, quarter), :] = u[d]
         for q, g in enumerate((g0, g1, g2, g3)):
             for j in range(quarter // block):
@@ -122,10 +151,11 @@
                 wide_ref[rows, :] = low.astype(BF16)
                 turned[:, rows] = low.T.astype(BF16)
 
-    used = part_ref.shape[0]
-    part_ref[...] = (
-        jnp.dot(turned[:used, :], x_ref[...], preferred_element_type=F32) * norm
+    sums[...] = (
+        jnp.dot(turned[: CHUNKS * half, :], x_ref[...], preferred_element_type=F32) * norm
     ).astype(BF16)
+    for part, chunk in zip(parts, roles(z, place[2])):
+        part[...] = sums[pl.ds(pl.multiple_of(chunk * half, half), half), :]
 
 
 def pull(tables, place, grads, ups, features, norm, tile):
@@ -140,22 +170,18 @@
         + [whole((quarter, values))] * 4
         + [whole((JOBS, quarter, rank))] * 4
         + [pl.BlockSpec((rows, tile), lambda i: (0, i))],
-        out_specs=[
-            pl.BlockSpec((used, tile), lambda i: (0, i)),
-            whole((rows, 3 * rank)),
-        ],
-        out_shape=[
-            jax.ShapeDtypeStruct((used, width), BF16),
-            jax.ShapeDtypeStruct((rows, 3 * rank), BF16),
-        ],
+        out_specs=[pl.BlockSpec((rank // 2, tile), lambda i: (0, i))] * 7 + [whole((rows, 3 * rank))],
+        out_shape=[jax.ShapeDtypeStruct((rank // 2, width), BF16)] * 7
+        + [jax.ShapeDtypeStruct((rows, 3 * rank), BF16)],
         scratch_shapes=[
             pltpu.VMEM((JOBS, values, rank), BF16),
             pltpu.VMEM((3 * rank, rows), BF16),
+            pltpu.VMEM((used, tile), BF16),
         ],
         compiler_params=params(),
         cost_estimate=cost(2 * used * rows * width, 2 * (rows * width + used * width + 2 * rows * values)),
         name="pull_and_part_down",
-    )(*tables, place, *grads, *ups, features)
+    )(*tables, place, *map(far, grads), *ups, far(features))
 
 
 def arrivals(z, excess):
@@ -242,7 +268,7 @@
         compiler_params=params(),
         cost_estimate=cost(2 * 6 * half * rows * width, 2 * (rows * width + 12 * half * width)),
         name="project",
-    )(ids, owners, place, *chunks, features)
+    )(ids, owners, place, *chunks, far(features))
 
 
 def base_kernel(lengths, place, g0, g1, g2, g3, weight_ref, out_ref):
@@ -279,7 +305,7 @@
         compiler_params=params(),
         cost_estimate=cost(2 * rows * width * values, 2 * (rows * values + width * values + rows * width)),
         name="base_term",
-    )(lengths, place, *grads, weight)
+    )(lengths, place, *map(far, grads), far(weight))
 
 
 def rows_kernel(wide_ref, table_ref, first_ref, second_ref, out_ref):
@@ -338,7 +364,7 @@
     )
     lanes = lax.broadcasted_iota(jnp.int32, (quarter, rank), 1)
     for d, out in enumerate(outs):
-        slot = lax.rem(z + d, JOBS)
+        slot = jnp.bitwise_xor(z, d)
         keep = jnp.where(slot == excess, rank, half)
         out[...] = jnp.where(lanes < keep, gathered(full, slot, rank), 0.0).astype(BF16)
 
@@ -376,7 +402,7 @@
     out_ref[...] = jnp.where(rows < keep, total, 0.0).T
 
 
-def last(place, parts, t1, n1, t2, n2, tile):
+def last(place, own0, own1, t1, n1, t2, n2, tile):
     half, width = t1.shape
     piece = pl.BlockSpec((half, tile), lambda i, place: (0, i))
     return pl.pallas_call(
@@ -384,18 +410,14 @@
         grid_spec=pltpu.PrefetchScalarGridSpec(
             num_scalar_prefetch=1,
             grid=(width // tile,),
-            in_specs=[
-                pl.BlockSpec((half, tile), lambda i, place: (place[1], i)),
-                pl.BlockSpec((half, tile), lambda i, place: (CHUNKS - 1, i)),
-            ]
-            + [piece] * 4,
+            in_specs=[piece] * 6,
             out_specs=pl.BlockSpec((tile, 2 * half), lambda i, place: (i, 0)),
         ),
         out_shape=jax.ShapeDtypeStruct((width, 2 * half), F32),
         compiler_params=params(),
         cost_estimate=cost(0, 2 * 6 * half * width + 8 * half * width),
         name="grad_down",
-    )(place, parts, parts, t1, n1, t2, n2)
+    )(place, own0, own1, t1, n1, t2, n2)
 
 
 def on_device(
@@ -421,14 +443,11 @@
 
     inner = (z == 1) | (z == 2)
     mine = jnp.where(z < 2, 1, 2)
-    outer = jnp.where(z < 2, 0, 3)
-    far_in, far_out = 3 - mine, 3 - outer
-    top_in, top_out = excess == mine, excess == outer
-    top_far_in, top_far_out = excess == far_in, excess == far_out
+    top_in = excess == mine
 
     pair = lambda value: lax.ppermute(value, "job", PAIR)
     middle = lambda value: lax.ppermute(value, ("tensor", "job"), MIDDLE)
-    shift = lambda value, d: lax.ppermute(value, "job", [(i, (i + d) % JOBS) for i in range(JOBS)])
+    swap = lambda value, d: lax.ppermute(value, "job", [(i, i ^ d) for i in range(JOBS)])
     across = lambda value: lax.ppermute(value, "tensor", TENSOR_X)
     beside = lambda value: lax.ppermute(value, "tensor", TENSOR_CORE)
 
@@ -438,7 +457,7 @@
     g0 = grad_out[0]
     g2 = across(g0)
     g1 = beside(g0)
-    up_z = jnp.stack([up] + [shift(up, d) for d in (1, 2, 3)])
+    up_z = jnp.stack([up] + [swap(up, d) for d in (1, 2, 3)])
     up_x = across(up_z)
 
     low, high = turn(adapter_down[0], local_width)
@@ -453,27 +472,22 @@
 
     grads = (g0, g1, g2, g3)
     ups = (up_z, up_c[0], up_x, up_c[1])
-    parts, wide = pull(tables, place, grads, ups, features, norm, 1024)
-
-    def chunk(index):
-        return lax.dynamic_slice_in_dim(parts, index * half, half, 0)
-
-    def added(index, value, use):
-        return (chunk(index).astype(F32) + jnp.where(use, value.astype(F32), 0.0)).astype(BF16)
-
-    spare = CHUNKS - 1
-    c4 = jnp.where(top_in | top_far_in, far_out, spare)
-    c3 = jnp.where(top_in, far_in, jnp.where(top_far_in, spare, far_out))
-    parts, s2, m2 = tie((parts, s2, m2))
-    to_s3 = jnp.where(inner, jnp.where(top_in, m1, m2), chunk(c4))
+    *parts, wide = pull(tables, place, grads, ups, features, norm, 1024)
+
+    def added(part, value, use=None):
+        value = value.astype(F32)
+        return (part.astype(F32) + (value if use is None else jnp.where(use, value, 0.0))).astype(BF16)
+
+    *parts, s2, m2 = tie((*parts, s2, m2))
+    to_s3 = jnp.where(inner, jnp.where(top_in, m1, m2), parts[0])
     to_m3 = jnp.where(top_in, s1, s2)
     to_s3, to_m3, *grads = tie((to_s3, to_m3, *grads))
     s3 = pair(to_s3)
     m3 = middle(to_m3)
     base_a = base(block_length, place, grads, value_weight, 0, 768)
     s3, m3, base_a = tie((s3, m3, base_a))
-    to_s4 = jnp.where(inner, jnp.where(top_in, m2, m3), chunk(c3))
-    to_n3 = added(jnp.where(top_far_in, far_out, spare), s3, ~top_in)
+    to_s4 = jnp.where(inner, jnp.where(top_in, m2, m3), parts[1])
+    to_n3 = added(parts[0], s3, ~top_in)
     to_s4, to_n3, *grads = tie((to_s4, to_n3, *grads))
     s4 = pair(to_s4)
     n3 = middle(to_n3)
@@ -485,8 +499,8 @@
     )
     partial, s4, n3 = tie((partial, s4, n3))
     beyond = beside(partial)
-    to_s5 = jnp.where(inner, added(spare, n3, ~top_in), chunk(jnp.where(top_in, spare, far_in)))
-    to_n2 = added(jnp.where(top_far_in, spare, far_out), jnp.where(top_in, s3, s4), True)
+    to_s5 = added(parts[2], n3, inner & ~top_in)
+    to_n2 = added(parts[1], jnp.where(top_in, s3, s4))
     to_s5, to_n2, beyond = tie((to_s5, to_n2, beyond))
     s5 = pair(to_s5)
     n2 = middle(to_n2)
@@ -496,19 +510,19 @@
     grad_rows = add_rows(wide, table, (base_a, base_b), 512)
     grad_rows, s5, n2 = tie((grad_rows, s5, n2))
 
-    to_s6 = jnp.where(inner, added(outer, jnp.where(top_in, n3, n2), True), chunk(mine))
-    to_n1 = added(far_in, jnp.where(top_in, s4, s5), True)
+    to_s6 = added(parts[3], jnp.where(top_in, n3, n2), inner)
+    to_n1 = added(parts[4], jnp.where(top_in, s4, s5))
     to_s6, to_n1, other = tie((to_s6, to_n1, other))
     s6 = pair(to_s6)
     n1 = middle(to_n1)
 
     ours = part_up(tables, place, grads, (both, other), norm)
-    theirs = [shift(ours[d], d) for d in (1, 2, 3)]
+    theirs = [swap(ours[d], d) for d in (1, 2, 3)]
+    grad_down = last(place, parts[5], parts[6], s6, n1, s5, n2, 1024)
+    grad_down, *theirs = tie((grad_down, *theirs))
     grad_up = ours[0].astype(F32)
     for value in theirs:
         grad_up = grad_up + value.astype(F32)
-
-    grad_down = last(place, parts, s6, n1, s5, n2, 1024)
     return (grad_rows[None], grad_down[None], grad_up[None])
 
 

time: 118 us -> 95.2 us (0.81)
  Pallas kernels: 51.3 us -> 37.2 us
  other arithmetic: 16 us -> 4.69 us
  waiting for transfers between devices: 23.6 us -> 27.9 us
  local copies, waits for them, and re-layouts: 3.93 us -> 2.03 us
  starting transfers between devices: 19.9 us -> 21.6 us
    ppermute x6, waiting for transfers between devices: 8.52 us -> 15.4 us  [on_device(): pair = lambda value: lax.ppermute(value, 'job', PAIR)]
    ppermute x6, waiting for transfers between devices: 11.5 us -> 6.33 us  [on_device(): lax.ppermute(value, 'job', [(i, i ^ d) for i in range(JOBS)])]
    select_n x4 -> x2, other arithmetic: 5.21 us -> 0.18 us  [the longest x1 0.13 us: on_device(): to_s3 = jnp.where(inner, jnp.where(top_in, m1, m2), parts[0])]
    pallas_call x1, Pallas kernels: 10.4 us -> 7 us  [add_rows(): pl.pallas_call(rows_kernel, grid=(steps,), in_specs=[whole((rows, deep)),...]
    convert_element_type x3 -> x5, other arithmetic: 3.87 us -> 0.72 us  [added(): (part.astype(F32) + (value if use is None else jnp.where(use, value, 0.0)...]
    ppermute x6, starting transfers between devices: 4.62 us -> 7.53 us  [on_device(): pair = lambda value: lax.ppermute(value, 'job', PAIR)]
    pallas_call x2, Pallas kernels: 14 us -> 11.9 us  [base(): pl.pallas_call(base_kernel, grid=(width // tile,), in_specs=[smem()] * 2...]
    pallas_call x1, Pallas kernels: 2.29 us -> 0.25 us  [turn(): pl.pallas_call(turn_kernel, grid=(width // tile,), in_specs=[pl.BlockSpec...]
  transfers between devices with their start and end apart: 25 -> 25, of which waited for: 8 -> 12; matrix products, arithmetic and copies ran while one was open for 11% -> 4% of each run, Pallas kernels for 32% -> 32%
where the time goes in v3:
time: 95.2 us; the launch traced here: 94.9 us
  Pallas kernels  37.2 us (39%)
  waiting for transfers between devices  27.9 us (29%)
  starting transfers between devices  21.6 us (23%)
  other arithmetic  4.69 us (5%)
  local copies, waits for them, and re-layouts  2.03 us (2%)
  between operations  1.53 us (2%)
    ppermute x6, waiting for transfers between devices, on_device(): pair = lambda value: lax.ppermute(value, 'job', PAIR)  15.4 us
    pallas_call x2, Pallas kernels, base(): pl.pallas_call(base_kernel, grid=(width // tile,), in_specs=[smem()] * 2...  11.9 us
    ppermute x6, starting transfers between devices, on_device(): lax.ppermute(value, 'job', [(i, i ^ d) for i in range(JOBS)])  8.84 us
    ppermute x6, starting transfers between devices, on_device(): pair = lambda value: lax.ppermute(value, 'job', PAIR)  7.53 us
    pallas_call x1, Pallas kernels, pull(): pl.pallas_call(functools.partial(pull_kernel, norm), grid=(width // tile,...  7.04 us
    pallas_call x1, Pallas kernels, add_rows(): pl.pallas_call(rows_kernel, grid=(steps,), in_specs=[whole((rows, deep)),...  7 us
    pallas_call x1, Pallas kernels, project(): pl.pallas_call(project_kernel, grid=(rows // tile,), in_specs=[smem()] *...  6.91 us
    ppermute x6, waiting for transfers between devices, on_device(): lax.ppermute(value, 'job', [(i, i ^ d) for i in range(JOBS)])  6.33 us
  transfers between devices with their start and end apart: 25, of which 12 were waited for; matrix products, arithmetic and copies ran while one was open for 4% of the time, Pallas kernels for 32%

profile of v3, /device:TPU:0, one launch (start us, length us, event | category | flops | bytes accessed | tf_op | source)
XLA Modules:
  0.0 94.9 jit_solution(9346697287554538633)
XLA Ops:
  1.2 2.6 %collective-permute-start.6 = (bf16[256,1024]{1,0:T(8,128)(2,1)}, bf16[256,1024]{1,0:T(8,128)(2,1)S(1)}, u32[]{:S(2)}, u32[]{:S(2)}) collective-permute-start(bf16[256,1024]{1,0:T(8,128)(2,1)} %bitcast.22), channel_id=1, source_target_pairs={{0,8},{8,0},{4,12},{12,4},{1,9},{9,1},{5,13},{13,5},{2,10},{10,2},... | collective-permute-start | bytes 1572872 | tf_op jit(solution)/shard_map/ppermute | solution.py:451
  3.8 3.6 %collective-permute-start.4 = (bf16[256,128]{1,0:T(8,128)(2,1)}, bf16[256,128]{1,0:T(8,128)(2,1)S(1)}, u32[]{:S(2)}, u32[]{:S(2)}) collective-permute-start(bf16[256,128]{1,0:T(8,128)(2,1)} %bitcast.33), channel_id=1, source_target_pairs={{0,3},{1,2},{2,1},{3,0},{4,7},{5,6},{6,5},{7,4},{8,11},{9,10},{10,... | collective-permute-start | bytes 196616 | tf_op jit(solution)/shard_map/ppermute | solution.py:450
  10.3 3.6 %collective-permute-done.3 = bf16[256,128]{1,0:T(8,128)(2,1)S(1)} collective-permute-done((bf16[256,128]{1,0:T(8,128)(2,1)}, bf16[256,128]{1,0:T(8,128)(2,1)S(1)}, u32[]{:S(2)}, u32[]{:S(2)}) %collective-permute-start.3) | collective-permute-done | bytes 65568 | tf_op jit(solution)/shard_map/ppermute | solution.py:450
  18.0 4.3 %collective-permute-done.5.u2 = bf16[4,256,128]{2,1,0:T(8,128)(2,1)S(1)} collective-permute-done((bf16[4,256,128]{2,1,0:T(8,128)(2,1)S(1)}, bf16[4,256,128]{2,1,0:T(8,128)(2,1)S(1)}, u32[]{:S(2)}, u32[]{:S(2)}) %collective-permute-start.5) | collective-permute-done | bytes 262176 | tf_op jit(solution)/shard_map/ppermute | solution.py:451
  22.3 1.9 %collective-permute-done.refs_2_ = bf16[64,3072]{1,0:T(8,128)(2,1)S(1)} collective-permute-done((bf16[64,3072]{1,0:T(8,128)(2,1)S(1)}, bf16[64,3072]{1,0:T(8,128)(2,1)S(1)}, u32[]{:S(2)}, u32[]{:S(2)}) %collective-permute-start) | collective-permute-done | bytes 393248 | tf_op jit(solution)/shard_map/ppermute | solution.py:448
  25.1 1.4 %collective-permute-start.10 = (bf16[64,3072]{1,0:T(8,128)(2,1)S(1)}, bf16[64,3072]{1,0:T(8,128)(2,1)S(1)}, u32[]{:S(2)}, u32[]{:S(2)}) collective-permute-start(bf16[64,3072]{1,0:T(8,128)(2,1)S(1)} %get-tuple-element.146), channel_id=1, source_target_pairs={{0,1},{1,0},{2,3},{3,2},{4,5},{5,4},{6,7},{7,6},{8,9},{9,8},{10,11... | collective-permute-start | bytes 1179656 | tf_op jit(solution)/shard_map/ppermute | solution.py:448
  27.8 7.0 %pull_and_part_down.1 = (bf16[64,3072]{1,0:T(8,128)(2,1)S(1)}, bf16[64,3072]{1,0:T(8,128)(2,1)S(1)}, bf16[64,3072]{1,0:T(8,128)(2,1)S(1)}, bf16[64,3072]{1,0:T(8...) custom-call(s32[1,8]{1,0:T(1,128)S(1)} %copy-done.8, ...), custom_call_target="tpu_custom_call" | custom-call | flops 2013265920 | bytes 12451840 | tf_op jit(solution)/shard_map/pull_and_part_down/pallas_call | solution.py:166
  34.9 1.6 %collective-permute-done.10.refs_3_ = bf16[64,3072]{1,0:T(8,128)(2,1)S(1)} collective-permute-done((bf16[64,3072]{1,0:T(8,128)(2,1)S(1)}, bf16[64,3072]{1,0:T(8,128)(2,1)S(1)}, u32[]{:S(2)}, u32[]{:S(2)}) %collective-permute-start.10) | collective-permute-done | bytes 393248 | tf_op jit(solution)/shard_map/ppermute | solution.py:448
  37.4 5.9 %base_term.2.first_ref = bf16[1024,1536]{1,0:T(8,128)(2,1)S(1)} custom-call(s32[1,8]{1,0:T(1,128)S(1)} %copy-done.10, s32[3]{0:T(128)S(1)} %pad_add_fusion.place, bf16[256,1024]{1,0:T(8,128)(2,1)} %bitcast.24, bf16[256,1024]{1,0:T(8,128)(2,1)} %copy-done.1, bf16[256,1024]{1,0:T(8,128)(2,1)} %copy-done.3, bf16[256,1024]{1,0:T(8,128)(2,1)} %copy-done.5, ...), custom_call_target="tpu_custom_call" | custom-call | flops 3221225472 | bytes 8388608 | tf_op jit(solution)/shard_map/base_term/pallas_call | solution.py:297
  43.4 4.0 %collective-permute-done.12.refs_4_ = bf16[64,3072]{1,0:T(8,128)(2,1)S(1)} collective-permute-done((bf16[64,3072]{1,0:T(8,128)(2,1)S(1)}, bf16[64,3072]{1,0:T(8,128)(2,1)S(1)}, u32[]{:S(2)}, u32[]{:S(2)}) %collective-permute-start.12) | collective-permute-done | bytes 393248 | tf_op jit(solution)/shard_map/ppermute | solution.py:448
  47.6 1.8 %collective-permute-start.14 = (bf16[64,3072]{1,0:T(8,128)(2,1)S(1)}, bf16[64,3072]{1,0:T(8,128)(2,1)S(1)}, u32[]{:S(2)}, u32[]{:S(2)}) collective-permute-start(bf16[64,3072]{1,0:T(8,128)(2,1)S(1)} %select_select_fusion), channel_id=1, source_target_pairs={{0,1},{1,0},{2,3},{3,2},{4,5},{5,4},{6,7},{7,6},{8,9},{9,8},{10,11... | collective-permute-start | bytes 1179656 | tf_op jit(solution)/shard_map/ppermute | solution.py:448
  49.4 5.9 %base_term.3.second_ref = bf16[1024,1536]{1,0:T(8,128)(2,1)S(1)} custom-call(s32[1,8]{1,0:T(1,128)S(1)} %copy-done.10, s32[3]{0:T(128)S(1)} %pad_add_fusion.place, bf16[256,1024]{1,0:T(8,128)(2,1)} %bitcast.25, bf16[256,1024]{1,0:T(8,128)(2,1)} %copy-done.1, bf16[256,1024]{1,0:T(8,128)(2,1)} %copy-done.3, bf16[256,1024]{1,0:T(8,128)(2,1)} %copy-done.5, ...), custom_call_target="tpu_custom_call" | custom-call | flops 3221225472 | bytes 8388608 | tf_op jit(solution)/shard_map/base_term/pallas_call | solution.py:297
  55.4 2.1 %collective-permute-done.14.refs_5_ = bf16[64,3072]{1,0:T(8,128)(2,1)S(1)} collective-permute-done((bf16[64,3072]{1,0:T(8,128)(2,1)S(1)}, bf16[64,3072]{1,0:T(8,128)(2,1)S(1)}, u32[]{:S(2)}, u32[]{:S(2)}) %collective-permute-start.14) | collective-permute-done | bytes 393248 | tf_op jit(solution)/shard_map/ppermute | solution.py:448
  57.4 6.9 %project.1 = (bf16[1024,128]{1,0:T(8,128)(2,1)S(1)}, bf16[384,3072]{1,0:T(8,128)(2,1)S(1)}) custom-call(s32[1,8]{1,0:T(1,128)S(1)} %copy-done.8, s32[4]{0:T(128)S(1)} %copy-done.9, s32[3]{0:T(128)S(1)} %pad_add_fusion.place, bf16[64,3072]{1,0:T(8,128)(2,1)S(1)} %get-tuple-element.73.refs_0_, bf16[64,3072]{1,0:T(8,128)(2,1)S(1)} %get-tuple-element.74.refs_1_, ...), custom_call_target="tpu_custom_call" | custom-call | flops 2415919104 | bytes 11010048 | tf_op jit(solution)/shard_map/project/pallas_call | solution.py:253
  64.7 1.4 %collective-permute-done.16 = bf16[1024,128]{1,0:T(8,128)(2,1)S(1)} collective-permute-done((bf16[1024,128]{1,0:T(8,128)(2,1)S(1)}, bf16[1024,128]{1,0:T(8,128)(2,1)S(1)}, u32[]{:S(2)}, u32[]{:S(2)}) %collective-permute-start.16) | collective-permute-done | bytes 262176 | tf_op jit(solution)/shard_map/ppermute | solution.py:452
  66.1 1.8 %collective-permute-start.17 = (bf16[64,3072]{1,0:T(8,128)(2,1)S(1)}, bf16[64,3072]{1,0:T(8,128)(2,1)S(1)}, u32[]{:S(2)}, u32[]{:S(2)}) collective-permute-start(bf16[64,3072]{1,0:T(8,128)(2,1)S(1)} %add_convert_fusion.3), channel_id=1, source_target_pairs={{0,1},{1,0},{2,3},{3,2},{4,5},{5,4},{6,7},{7,6},{8,9},{9,8},{10,11... | collective-permute-start | bytes 1179656 | tf_op jit(solution)/shard_map/ppermute | solution.py:448
  68.7 7.0 %grad_rows.1 = bf16[1024,3072]{1,0:T(8,128)(2,1)} custom-call(bf16[1024,384]{1,0:T(8,128)(2,1)S(1)} %get-tuple-element.118.wide_ref, bf16[384,3072]{1,0:T(8,128)(2,1)S(1)} %get-tuple-element.119.table_ref, bf16[1024,1536]{1,0:T(8,128)(2,1)S(1)} %base_term.2.first_ref, bf16[1024,1536]{1,0:T(8,128)(2,1)S(1)} %base_term.3.second_ref), custom_call_target="tpu_custom_call" | custom-call | flops 2415919104 | bytes 15728640 | tf_op jit(solution)/shard_map/grad_rows/pallas_call | solution.py:329
  75.7 1.6 %collective-permute-done.17.t2 = bf16[64,3072]{1,0:T(8,128)(2,1)S(1)} collective-permute-done((bf16[64,3072]{1,0:T(8,128)(2,1)S(1)}, bf16[64,3072]{1,0:T(8,128)(2,1)S(1)}, u32[]{:S(2)}, u32[]{:S(2)}) %collective-permute-start.17) | collective-permute-done | bytes 393248 | tf_op jit(solution)/shard_map/ppermute | solution.py:448
  77.7 1.8 %collective-permute-start.20 = (bf16[64,3072]{1,0:T(8,128)(2,1)S(1)}, bf16[64,3072]{1,0:T(8,128)(2,1)S(1)}, u32[]{:S(2)}, u32[]{:S(2)}) collective-permute-start(bf16[64,3072]{1,0:T(8,128)(2,1)S(1)} %add_convert_fusion.1), channel_id=1, source_target_pairs={{0,1},{1,0},{2,3},{3,2},{4,5},{5,4},{6,7},{7,6},{8,9},{9,8},{10,11... | collective-permute-start | bytes 1179656 | tf_op jit(solution)/shard_map/ppermute | solution.py:448
  80.8 1.5 %collective-permute-start.22 = (bf16[256,128]{1,0:T(8,128)(2,1)S(1)}, bf16[256,128]{1,0:T(8,128)(2,1)S(1)}, u32[]{:S(2)}, u32[]{:S(2)}) collective-permute-start(bf16[256,128]{1,0:T(8,128)(2,1)S(1)} %get-tuple-element.135), channel_id=1, source_target_pairs={{0,1},{1,0},{2,3},{3,2},{4,5},{5,4},{6,7},{7,6},{8,9},{9,8},{10,11... | collective-permute-start | bytes 196616 | tf_op jit(solution)/shard_map/ppermute | solution.py:450
  83.5 1.8 %collective-permute-start.24 = (bf16[256,128]{1,0:T(8,128)(2,1)S(1)}, bf16[256,128]{1,0:T(8,128)(2,1)S(1)}, u32[]{:S(2)}, u32[]{:S(2)}) collective-permute-start(bf16[256,128]{1,0:T(8,128)(2,1)S(1)} %get-tuple-element.137), channel_id=1, source_target_pairs={{0,3},{1,2},{2,1},{3,0},{4,7},{5,6},{6,5},{7,4},{8,11},{9,10},{10,... | collective-permute-start | bytes 196616 | tf_op jit(solution)/shard_map/ppermute | solution.py:450
  85.3 4.2 %collective-permute-done.20.t1 = bf16[64,3072]{1,0:T(8,128)(2,1)S(1)} collective-permute-done((bf16[64,3072]{1,0:T(8,128)(2,1)S(1)}, bf16[64,3072]{1,0:T(8,128)(2,1)S(1)}, u32[]{:S(2)}, u32[]{:S(2)}) %collective-permute-start.20) | collective-permute-done | bytes 393248 | tf_op jit(solution)/shard_map/ppermute | solution.py:448
  89.5 2.7 %grad_down.1 = f32[3072,128]{1,0:T(8,128)} custom-call(s32[3]{0:T(128)S(1)} %pad_add_fusion.place, bf16[64,3072]{1,0:T(8,128)(2,1)S(1)} %get-tuple-element.125.own0, bf16[64,3072]{1,0:T(8,128)(2,1)S(1)} %get-tuple-element.126.own1, bf16[64,3072]{1,0:T(8,128)(2,1)S(1)} %collective-permute-done.20.t1, bf16[64,3072]{1,0:T(8,128)(2,1)S(1)} %collective-permute-done.21.n1, ...), custom_call_target="tpu_custom_call" | custom-call | bytes 3932160 | tf_op jit(solution)/shard_map/grad_down/pallas_call | solution.py:408
  92.2 2.0 %collective-permute-done.23 = bf16[256,128]{1,0:T(8,128)(2,1)S(1)} collective-permute-done((bf16[256,128]{1,0:T(8,128)(2,1)S(1)}, bf16[256,128]{1,0:T(8,128)(2,1)S(1)}, u32[]{:S(2)}, u32[]{:S(2)}) %collective-permute-start.23) | collective-permute-done | bytes 65568 | tf_op jit(solution)/shard_map/ppermute | solution.py:450
  (73 shorter events, 15.0 us)
Async XLA Ops:
  0.7 23.5 %collective-permute-start.7 = (bf16[256,1024]{1,0:T(8,128)(2,1)}, bf16[256,1024]{1,0:T(8,128)(2,1)S(1)}, u32[]{:S(2)}, u32[]{:S(2)}) collective-permute-start(bf16[256,1024]{1,0:T(8,128)(2,1)} %bitcast.21), channel_id=1, source_target_pairs={{0,4},{4,0},{8,12},{12,8},{1,5},{5,1},{9,13},{13,9},{2,6},{6,2},{1... | collective-permute-start | bytes 1572872 | tf_op jit(solution)/shard_map/ppermute | solution.py:452
  1.2 23.0 %collective-permute-start.6 = (bf16[256,1024]{1,0:T(8,128)(2,1)}, bf16[256,1024]{1,0:T(8,128)(2,1)S(1)}, u32[]{:S(2)}, u32[]{:S(2)}) collective-permute-start(bf16[256,1024]{1,0:T(8,128)(2,1)} %bitcast.22), channel_id=1, source_target_pairs={{0,8},{8,0},{4,12},{12,4},{1,9},{9,1},{5,13},{13,5},{2,10},{10,2},... | collective-permute-start | bytes 1572872 | tf_op jit(solution)/shard_map/ppermute | solution.py:451
  3.8 6.5 %collective-permute-start.4 = (bf16[256,128]{1,0:T(8,128)(2,1)}, bf16[256,128]{1,0:T(8,128)(2,1)S(1)}, u32[]{:S(2)}, u32[]{:S(2)}) collective-permute-start(bf16[256,128]{1,0:T(8,128)(2,1)} %bitcast.33), channel_id=1, source_target_pairs={{0,3},{1,2},{2,1},{3,0},{4,7},{5,6},{6,5},{7,4},{8,11},{9,10},{10,... | collective-permute-start | bytes 196616 | tf_op jit(solution)/shard_map/ppermute | solution.py:450
  7.4 6.5 %collective-permute-start.3 = (bf16[256,128]{1,0:T(8,128)(2,1)}, bf16[256,128]{1,0:T(8,128)(2,1)S(1)}, u32[]{:S(2)}, u32[]{:S(2)}) collective-permute-start(bf16[256,128]{1,0:T(8,128)(2,1)} %bitcast.34), channel_id=1, source_target_pairs={{0,2},{1,3},{2,0},{3,1},{4,6},{5,7},{6,4},{7,5},{8,10},{9,11},{10,... | collective-permute-start | bytes 196616 | tf_op jit(solution)/shard_map/ppermute | solution.py:450
  7.4 6.5 %collective-permute-start.2 = (bf16[256,128]{1,0:T(8,128)(2,1)}, bf16[256,128]{1,0:T(8,128)(2,1)S(1)}, u32[]{:S(2)}, u32[]{:S(2)}) collective-permute-start(bf16[256,128]{1,0:T(8,128)(2,1)} %bitcast.35), channel_id=1, source_target_pairs={{0,1},{1,0},{2,3},{3,2},{4,5},{5,4},{6,7},{7,6},{8,9},{9,8},{10,11... | collective-permute-start | bytes 196616 | tf_op jit(solution)/shard_map/ppermute | solution.py:450
  10.3 12.1 %collective-permute-start.1 = (bf16[64,3072]{1,0:T(8,128)(2,1)S(1)}, bf16[64,3072]{1,0:T(8,128)(2,1)S(1)}, u32[]{:S(2)}, u32[]{:S(2)}) collective-permute-start(bf16[64,3072]{1,0:T(8,128)(2,1)S(1)} %get-tuple-element.73.refs_0_), channel_id=1, source_target_pairs={{1,2},{2,1},{0,4},{3,7},{5,6},{6,5},{4,0},{7,3},{9,10},{10,9},{8,1... | collective-permute-start | bytes 1179656 | tf_op jit(solution)/shard_map/ppermute | solution.py:449
  13.9 10.3 %collective-permute-start = (bf16[64,3072]{1,0:T(8,128)(2,1)S(1)}, bf16[64,3072]{1,0:T(8,128)(2,1)S(1)}, u32[]{:S(2)}, u32[]{:S(2)}) collective-permute-start(bf16[64,3072]{1,0:T(8,128)(2,1)S(1)} %get-tuple-element.73.refs_0_), channel_id=1, source_target_pairs={{0,1},{1,0},{2,3},{3,2},{4,5},{5,4},{6,7},{7,6},{8,9},{9,8},{10,11... | collective-permute-start | bytes 1179656 | tf_op jit(solution)/shard_map/ppermute | solution.py:448
  14.8 7.6 %collective-permute-start.5 = (bf16[4,256,128]{2,1,0:T(8,128)(2,1)S(1)}, bf16[4,256,128]{2,1,0:T(8,128)(2,1)S(1)}, u32[]{:S(2)}, u32[]{:S(2)}) collective-permute-start(bf16[4,256,128]{2,1,0:T(8,128)(2,1)S(1)} %pad_maximum_fusion.1.u0), channel_id=1, source_target_pairs={{0,8},{8,0},{4,12},{12,4},{1,9},{9,1},{5,13},{13,5},{2,10},{10,2},... | collective-permute-start | bytes 786440 | tf_op jit(solution)/shard_map/ppermute | solution.py:451
  24.3 2.2 %collective-permute-start.9 = (bf16[2,4,256,128]{3,2,1,0:T(8,128)(2,1)S(1)}, bf16[2,4,256,128]{3,2,1,0:T(8,128)(2,1)S(1)}, u32[]{:S(2)}, u32[]{:S(2)}) collective-permute-start(bf16[2,4,256,128]{3,2,1,0:T(8,128)(2,1)S(1)} %pad_maximum_fusion), channel_id=1, source_target_pairs={{0,4},{4,0},{8,12},{12,8},{1,5},{5,1},{9,13},{13,9},{2,6},{6,2},{1... | collective-permute-start | bytes 1572872 | tf_op jit(solution)/shard_map/ppermute | solution.py:452
  24.3 2.6 %collective-permute-start.8 = (bf16[256,1024]{1,0:T(8,128)(2,1)S(1)}, bf16[256,1024]{1,0:T(8,128)(2,1)S(1)}, u32[]{:S(2)}, u32[]{:S(2)}) collective-permute-start(bf16[256,1024]{1,0:T(8,128)(2,1)S(1)} %collective-permute-done.6.g2), channel_id=1, source_target_pairs={{0,4},{4,0},{8,12},{12,8},{1,5},{5,1},{9,13},{13,9},{2,6},{6,2},{1... | collective-permute-start | bytes 1572872 | tf_op jit(solution)/shard_map/ppermute | solution.py:452
  24.9 10.0 %collective-permute-start.11 = (bf16[64,3072]{1,0:T(8,128)(2,1)S(1)}, bf16[64,3072]{1,0:T(8,128)(2,1)S(1)}, u32[]{:S(2)}, u32[]{:S(2)}) collective-permute-start(bf16[64,3072]{1,0:T(8,128)(2,1)S(1)} %get-tuple-element.145), channel_id=1, source_target_pairs={{1,2},{2,1},{0,4},{3,7},{5,6},{6,5},{4,0},{7,3},{9,10},{10,9},{8,1... | collective-permute-start | bytes 1179656 | tf_op jit(solution)/shard_map/ppermute | solution.py:449
  25.1 11.5 %collective-permute-start.10 = (bf16[64,3072]{1,0:T(8,128)(2,1)S(1)}, bf16[64,3072]{1,0:T(8,128)(2,1)S(1)}, u32[]{:S(2)}, u32[]{:S(2)}) collective-permute-start(bf16[64,3072]{1,0:T(8,128)(2,1)S(1)} %get-tuple-element.146), channel_id=1, source_target_pairs={{0,1},{1,0},{2,3},{3,2},{4,5},{5,4},{6,7},{7,6},{8,9},{9,8},{10,11... | collective-permute-start | bytes 1179656 | tf_op jit(solution)/shard_map/ppermute | solution.py:448
  36.7 10.7 %collective-permute-start.12 = (bf16[64,3072]{1,0:T(8,128)(2,1)S(1)}, bf16[64,3072]{1,0:T(8,128)(2,1)S(1)}, u32[]{:S(2)}, u32[]{:S(2)}) collective-permute-start(bf16[64,3072]{1,0:T(8,128)(2,1)S(1)} %get-tuple-element.91), channel_id=1, source_target_pairs={{0,1},{1,0},{2,3},{3,2},{4,5},{5,4},{6,7},{7,6},{8,9},{9,8},{10,11... | collective-permute-start | bytes 1179656 | tf_op jit(solution)/shard_map/ppermute | solution.py:448
  37.4 10.0 %collective-permute-start.13 = (bf16[64,3072]{1,0:T(8,128)(2,1)S(1)}, bf16[64,3072]{1,0:T(8,128)(2,1)S(1)}, u32[]{:S(2)}, u32[]{:S(2)}) collective-permute-start(bf16[64,3072]{1,0:T(8,128)(2,1)S(1)} %get-tuple-element.92), channel_id=1, source_target_pairs={{1,2},{2,1},{0,4},{3,7},{5,6},{6,5},{4,0},{7,3},{9,10},{10,9},{8,1... | collective-permute-start | bytes 1179656 | tf_op jit(solution)/shard_map/ppermute | solution.py:449
  47.6 9.9 %collective-permute-start.14 = (bf16[64,3072]{1,0:T(8,128)(2,1)S(1)}, bf16[64,3072]{1,0:T(8,128)(2,1)S(1)}, u32[]{:S(2)}, u32[]{:S(2)}) collective-permute-start(bf16[64,3072]{1,0:T(8,128)(2,1)S(1)} %select_select_fusion), channel_id=1, source_target_pairs={{0,1},{1,0},{2,3},{3,2},{4,5},{5,4},{6,7},{7,6},{8,9},{9,8},{10,11... | collective-permute-start | bytes 1179656 | tf_op jit(solution)/shard_map/ppermute | solution.py:448
  49.4 8.0 %collective-permute-start.15 = (bf16[64,3072]{1,0:T(8,128)(2,1)S(1)}, bf16[64,3072]{1,0:T(8,128)(2,1)S(1)}, u32[]{:S(2)}, u32[]{:S(2)}) collective-permute-start(bf16[64,3072]{1,0:T(8,128)(2,1)S(1)} %add_convert_fusion.4), channel_id=1, source_target_pairs={{1,2},{2,1},{0,4},{3,7},{5,6},{6,5},{4,0},{7,3},{9,10},{10,9},{8,1... | collective-permute-start | bytes 1179656 | tf_op jit(solution)/shard_map/ppermute | solution.py:449
  66.1 11.2 %collective-permute-start.17 = (bf16[64,3072]{1,0:T(8,128)(2,1)S(1)}, bf16[64,3072]{1,0:T(8,128)(2,1)S(1)}, u32[]{:S(2)}, u32[]{:S(2)}) collective-permute-start(bf16[64,3072]{1,0:T(8,128)(2,1)S(1)} %add_convert_fusion.3), channel_id=1, source_target_pairs={{0,1},{1,0},{2,3},{3,2},{4,5},{5,4},{6,7},{7,6},{8,9},{9,8},{10,11... | collective-permute-start | bytes 1179656 | tf_op jit(solution)/shard_map/ppermute | solution.py:448
  67.9 9.4 %collective-permute-start.18 = (bf16[64,3072]{1,0:T(8,128)(2,1)S(1)}, bf16[64,3072]{1,0:T(8,128)(2,1)S(1)}, u32[]{:S(2)}, u32[]{:S(2)}) collective-permute-start(bf16[64,3072]{1,0:T(8,128)(2,1)S(1)} %add_convert_fusion.2), channel_id=1, source_target_pairs={{1,2},{2,1},{0,4},{3,7},{5,6},{6,5},{4,0},{7,3},{9,10},{10,9},{8,1... | collective-permute-start | bytes 1179656 | tf_op jit(solution)/shard_map/ppermute | solution.py:449
  68.0 9.7 %collective-permute-start.19 = (bf16[1024,128]{1,0:T(8,128)(2,1)S(1)}, bf16[1024,128]{1,0:T(8,128)(2,1)S(1)}, u32[]{:S(2)}, u32[]{:S(2)}) collective-permute-start(bf16[1024,128]{1,0:T(8,128)(2,1)S(1)} %add_convert_fusion.5.a_ref), channel_id=1, source_target_pairs={{0,8},{8,0},{4,12},{12,4},{1,9},{9,1},{5,13},{13,5},{2,10},{10,2},... | collective-permute-start | bytes 786440 | tf_op jit(solution)/shard_map/ppermute | solution.py:451
  77.7 11.8 %collective-permute-start.20 = (bf16[64,3072]{1,0:T(8,128)(2,1)S(1)}, bf16[64,3072]{1,0:T(8,128)(2,1)S(1)}, u32[]{:S(2)}, u32[]{:S(2)}) collective-permute-start(bf16[64,3072]{1,0:T(8,128)(2,1)S(1)} %add_convert_fusion.1), channel_id=1, source_target_pairs={{0,1},{1,0},{2,3},{3,2},{4,5},{5,4},{6,7},{7,6},{8,9},{9,8},{10,11... | collective-permute-start | bytes 1179656 | tf_op jit(solution)/shard_map/ppermute | solution.py:448
  79.5 10.0 %collective-permute-start.21 = (bf16[64,3072]{1,0:T(8,128)(2,1)S(1)}, bf16[64,3072]{1,0:T(8,128)(2,1)S(1)}, u32[]{:S(2)}, u32[]{:S(2)}) collective-permute-start(bf16[64,3072]{1,0:T(8,128)(2,1)S(1)} %add_convert_fusion), channel_id=1, source_target_pairs={{1,2},{2,1},{0,4},{3,7},{5,6},{6,5},{4,0},{7,3},{9,10},{10,9},{8,1... | collective-permute-start | bytes 1179656 | tf_op jit(solution)/shard_map/ppermute | solution.py:449
  80.8 11.4 %collective-permute-start.22 = (bf16[256,128]{1,0:T(8,128)(2,1)S(1)}, bf16[256,128]{1,0:T(8,128)(2,1)S(1)}, u32[]{:S(2)}, u32[]{:S(2)}) collective-permute-start(bf16[256,128]{1,0:T(8,128)(2,1)S(1)} %get-tuple-element.135), channel_id=1, source_target_pairs={{0,1},{1,0},{2,3},{3,2},{4,5},{5,4},{6,7},{7,6},{8,9},{9,8},{10,11... | collective-permute-start | bytes 196616 | tf_op jit(solution)/shard_map/ppermute | solution.py:450
  82.3 11.9 %collective-permute-start.23 = (bf16[256,128]{1,0:T(8,128)(2,1)S(1)}, bf16[256,128]{1,0:T(8,128)(2,1)S(1)}, u32[]{:S(2)}, u32[]{:S(2)}) collective-permute-start(bf16[256,128]{1,0:T(8,128)(2,1)S(1)} %get-tuple-element.136), channel_id=1, source_target_pairs={{0,2},{1,3},{2,0},{3,1},{4,6},{5,7},{6,4},{7,5},{8,10},{9,11},{10,... | collective-permute-start | bytes 196616 | tf_op jit(solution)/shard_map/ppermute | solution.py:450
  83.5 10.7 %collective-permute-start.24 = (bf16[256,128]{1,0:T(8,128)(2,1)S(1)}, bf16[256,128]{1,0:T(8,128)(2,1)S(1)}, u32[]{:S(2)}, u32[]{:S(2)}) collective-permute-start(bf16[256,128]{1,0:T(8,128)(2,1)S(1)} %get-tuple-element.137), channel_id=1, source_target_pairs={{0,3},{1,2},{2,1},{3,0},{4,7},{5,6},{6,5},{7,4},{8,11},{9,10},{10,... | collective-permute-start | bytes 196616 | tf_op jit(solution)/shard_map/ppermute | solution.py:450
  (13 other events, 133.0 us)

commit v4 on v3

--- a/solution.py
+++ b/solution.py
@@ -181,7 +181,7 @@
         compiler_params=params(),
         cost_estimate=cost(2 * used * rows * width, 2 * (rows * width + used * width + 2 * rows * values)),
         name="pull_and_part_down",
-    )(*tables, place, *map(far, grads), *ups, far(features))
+    )(*tables, place, far(grads[0]), *grads[1:], *ups, far(features))
 
 
 def arrivals(z, excess):
@@ -211,40 +211,37 @@
 
 def project_kernel(ids, owners, place, *refs):
     chunks = refs[:9]
-    x_ref, out_ref, table_ref, sems = refs[9:]
+    x_ref, out_ref, table_ref, turned, sems = refs[9:]
     half, width = chunks[0].shape
     rank = 2 * half
     rows = x_ref.shape[0]
-    block = rank
+    used = CHUNKS * half
 
     @pl.when(pl.program_id(0) == 0)
     def _():
         where_to = arrivals(place[1], place[2])
-        for k, chunk in enumerate(chunks):
-            spot = where_to[k]
-
-            @pl.when(spot < CHUNKS)
-            def _():
-                start = pl.multiple_of(spot * half, half)
-                pltpu.make_async_copy(chunk, table_ref.at[pl.ds(start, half), :], sems.at[k]).start()
-
-        table_ref[CHUNKS * half :, :] = jnp.zeros((half, width), BF16)
-        for k, chunk in enumerate(chunks):
-            spot = where_to[k]
-
-            @pl.when(spot < CHUNKS)
-            def _():
-                start = pl.multiple_of(spot * half, half)
-                pltpu.make_async_copy(chunk, table_ref.at[pl.ds(start, half), :], sems.at[k]).wait()
-
-    full = lax.dot_general(
-        x_ref[...], table_ref[...], (((1,), (1,)), ((), ())), preferred_element_type=F32
-    )
-    first = pl.program_id(0) * (rows // block)
-    for j in range(rows // block):
+
+        def chunk_copy(k):
+            start = pl.multiple_of(where_to[k] * half, half)
+            return pltpu.make_async_copy(chunks[k], table_ref.at[pl.ds(start, half), :], sems.at[k])
+
+        for k in range(9):
+            pl.when(where_to[k] < CHUNKS)(chunk_copy(k).start)
+        table_ref[used:, :] = jnp.zeros((half, width), BF16)
+        for k in range(9):
+            pl.when(where_to[k] < CHUNKS)(chunk_copy(k).wait)
+
+    turned[...] = lax.dot_general(
+        table_ref[:used, :], x_ref[...], (((1,), (1,)), ((), ())), preferred_element_type=F32
+    )
+    first = pl.program_id(0) * (rows // rank)
+    for j in range(rows // rank):
         slot = owners[ids[0, first + j]]
-        piece = gathered(full[j * block : (j + 1) * block], slot, rank)
-        out_ref[j * block : (j + 1) * block, :] = piece.astype(BF16)
+        columns = slice(j * rank, (j + 1) * rank)
+        piece = jnp.concatenate(
+            [turned[pl.ds(pl.multiple_of(slot * half, half), half), columns], turned[used - half :, columns]], axis=0
+        )
+        out_ref[columns, :] = piece.T.astype(BF16)
 
 
 def project(ids, owners, place, chunks, features, tile):
@@ -264,7 +261,7 @@
             jax.ShapeDtypeStruct((rows, 2 * half), BF16),
             jax.ShapeDtypeStruct((6 * half, width), BF16),
         ],
-        scratch_shapes=[pltpu.SemaphoreType.DMA((9,))],
+        scratch_shapes=[pltpu.VMEM((CHUNKS * half, tile), F32), pltpu.SemaphoreType.DMA((9,))],
         compiler_params=params(),
         cost_estimate=cost(2 * 6 * half * rows * width, 2 * (rows * width + 12 * half * width)),
         name="project",
@@ -308,39 +305,29 @@
     )(lengths, place, *map(far, grads), far(weight))
 
 
-def rows_kernel(wide_ref, table_ref, first_ref, second_ref, out_ref):
-    term = jnp.dot(wide_ref[...], table_ref[...], preferred_element_type=F32)
-    late = pl.program_id(0) >= pl.num_programs(0) // 2
-
-    @pl.when(jnp.logical_not(late))
-    def _():
-        out_ref[...] = (first_ref[...].astype(F32) + term).astype(BF16)
-
-    @pl.when(late)
-    def _():
-        out_ref[...] = (second_ref[...].astype(F32) + term).astype(BF16)
-
-
-def add_rows(wide, table, halves, tile):
+def rows_kernel(wide_ref, table_ref, base_ref, out_ref):
+    out_ref[...] = (
+        base_ref[...].astype(F32) + jnp.dot(wide_ref[...], table_ref[...], preferred_element_type=F32)
+    ).astype(BF16)
+
+
+def add_rows(wide, table, base_half, tile):
     rows, deep = wide.shape
     width = table.shape[1]
-    steps = width // tile
-    half = steps // 2
     return pl.pallas_call(
         rows_kernel,
-        grid=(steps,),
+        grid=(width // tile // 2,),
         in_specs=[
             whole((rows, deep)),
             pl.BlockSpec((deep, tile), lambda i: (0, i)),
-            pl.BlockSpec((rows, tile), lambda i: (0, jnp.minimum(i, half - 1))),
-            pl.BlockSpec((rows, tile), lambda i: (0, jnp.maximum(i - half, 0))),
+            pl.BlockSpec((rows, tile), lambda i: (0, i)),
         ],
         out_specs=pl.BlockSpec((rows, tile), lambda i: (0, i)),
         out_shape=jax.ShapeDtypeStruct((rows, width), BF16),
         compiler_params=params(),
-        cost_estimate=cost(2 * rows * width * deep, 2 * (2 * rows * width + deep * (rows + width))),
+        cost_estimate=cost(rows * width * deep, 2 * (rows * width + deep * (rows + width // 2))),
         name="grad_rows",
-    )(wide, table, *halves)
+    )(wide, table, base_half)
 
 
 def part_up_kernel(norm, ids, lengths, owners, ranks, place, g0, g1, g2, g3, a_ref, b_ref, *rest):
@@ -388,7 +375,8 @@
     )(*tables, place, *grads, *sums)
 
 
-def last_kernel(place, own0, own1, t1, n1, t2, n2, out_ref):
+def last_kernel(place, wide_ref, table_ref, base_ref, own0, own1, t1, n1, t2, n2, filled_ref, rows_ref, down_ref):
+    del filled_ref
     half = own0.shape[0]
     rank = 2 * half
     total = (
@@ -399,25 +387,40 @@
     total += jnp.where(inner, jnp.concatenate([n1[...], n2[...]], axis=0).astype(F32), 0.0)
     keep = jnp.where(place[1] == place[2], rank, half)
     rows = lax.broadcasted_iota(jnp.int32, total.shape, 0)
-    out_ref[...] = jnp.where(rows < keep, total, 0.0).T
-
-
-def last(place, own0, own1, t1, n1, t2, n2, tile):
-    half, width = t1.shape
-    piece = pl.BlockSpec((half, tile), lambda i, place: (0, i))
+    down_ref[...] = jnp.where(rows < keep, total, 0.0).T
+    rows_ref[...] = (
+        base_ref[...].astype(F32) + jnp.dot(wide_ref[...], table_ref[...], preferred_element_type=F32)
+    ).astype(BF16)
+
+
+def last(place, wide, table, base_half, filled, sums, steps):
+    rows, deep = wide.shape
+    half, width = sums[0].shape
+    tile, piece = width // 2 // steps, width // steps
     return pl.pallas_call(
         last_kernel,
-        grid_spec=pltpu.PrefetchScalarGridSpec(
-            num_scalar_prefetch=1,
-            grid=(width // tile,),
-            in_specs=[piece] * 6,
-            out_specs=pl.BlockSpec((tile, 2 * half), lambda i, place: (i, 0)),
-        ),
-        out_shape=jax.ShapeDtypeStruct((width, 2 * half), F32),
+        grid=(steps,),
+        in_specs=[
+            smem(),
+            whole((rows, deep)),
+            pl.BlockSpec((deep, tile), lambda i: (0, steps + i)),
+            pl.BlockSpec((rows, tile), lambda i: (0, i)),
+        ]
+        + [pl.BlockSpec((half, piece), lambda i: (0, i))] * 6
+        + [pl.BlockSpec(memory_space=pl.ANY)],
+        out_specs=[
+            pl.BlockSpec((rows, tile), lambda i: (0, steps + i)),
+            pl.BlockSpec((piece, 2 * half), lambda i: (i, 0)),
+        ],
+        out_shape=[
+            jax.ShapeDtypeStruct((rows, width), BF16),
+            jax.ShapeDtypeStruct((width, 2 * half), F32),
+        ],
+        input_output_aliases={10: 0},
         compiler_params=params(),
-        cost_estimate=cost(0, 2 * 6 * half * width + 8 * half * width),
-        name="grad_down",
-    )(place, own0, own1, t1, n1, t2, n2)
+        cost_estimate=cost(rows * width * deep, 2 * (rows * width + deep * (rows + width // 2) + 10 * half * width)),
+        name="grad_rows_and_down",
+    )(place, wide, table, base_half, *sums, filled)
 
 
 def on_device(
@@ -464,12 +467,17 @@
     s1 = pair(low)
     m1 = middle(low)
 
-    s1, m1, up_x, g2, g1, up_z = tie((s1, m1, up_x, g2, g1, up_z))
+    up_x, g2, g1, up_z = tie((up_x, g2, g1, up_z))
+    to_c = jnp.stack([up_z, up_x])
     g3 = beside(g2)
-    up_c = beside(jnp.stack([up_z, up_x]))
-    s2 = pair(jnp.where(inner & ~top_in, m1, high))
-    m2 = middle(jnp.where(top_in, high, s1))
-
+    up_c = beside(to_c)
+    s1, m1, to_c = tie((s1, m1, to_c))
+    to_s2 = jnp.where(inner & ~top_in, m1, high)
+    to_m2 = jnp.where(top_in, high, s1)
+    s2 = pair(to_s2)
+    m2 = middle(to_m2)
+
+    to_s2, to_m2, up_c, g3 = tie((to_s2, to_m2, up_c, g3))
     grads = (g0, g1, g2, g3)
     ups = (up_z, up_c[0], up_x, up_c[1])
     *parts, wide = pull(tables, place, grads, ups, features, norm, 1024)
@@ -494,32 +502,31 @@
     base_b = base(block_length, place, grads, value_weight, 1, 768)
     s4, n3, base_b = tie((s4, n3, base_b))
 
-    partial, table = project(
-        block_adapter, owner_slot, place, (low, high, s1, s2, s3, s4, m1, m2, m3), features, 512
-    )
-    partial, s4, n3 = tie((partial, s4, n3))
-    beyond = beside(partial)
     to_s5 = added(parts[2], n3, inner & ~top_in)
     to_n2 = added(parts[1], jnp.where(top_in, s3, s4))
-    to_s5, to_n2, beyond = tie((to_s5, to_n2, beyond))
+    to_s5, to_n2, to_project = tie((to_s5, to_n2, s4))
     s5 = pair(to_s5)
     n2 = middle(to_n2)
-    both = (partial.astype(F32) + beyond.astype(F32)).astype(BF16)
-    both, wide, table, base_a, base_b = tie((both, wide, table, base_a, base_b))
-    other = across(both)
-    grad_rows = add_rows(wide, table, (base_a, base_b), 512)
-    grad_rows, s5, n2 = tie((grad_rows, s5, n2))
-
+    partial, table = project(
+        block_adapter, owner_slot, place, (low, high, s1, s2, s3, to_project, m1, m2, m3), features, 512
+    )
+    partial, s5, n2 = tie((partial, s5, n2))
+    beyond = across(partial)
     to_s6 = added(parts[3], jnp.where(top_in, n3, n2), inner)
     to_n1 = added(parts[4], jnp.where(top_in, s4, s5))
-    to_s6, to_n1, other = tie((to_s6, to_n1, other))
+    to_s6, to_n1, wide, table, base_a, base_b = tie((to_s6, to_n1, wide, table, base_a, base_b))
     s6 = pair(to_s6)
     n1 = middle(to_n1)
+    grad_rows = add_rows(wide, table, base_a, 768)
+    grad_rows, beyond = tie((grad_rows, beyond))
+    both = (partial.astype(F32) + beyond.astype(F32)).astype(BF16)
+    other = beside(both)
 
     ours = part_up(tables, place, grads, (both, other), norm)
     theirs = [swap(ours[d], d) for d in (1, 2, 3)]
-    grad_down = last(place, parts[5], parts[6], s6, n1, s5, n2, 1024)
-    grad_down, *theirs = tie((grad_down, *theirs))
+    wide, table, base_b, _ = tie((wide, table, base_b, ours[1]))
+    grad_rows, grad_down = last(place, wide, table, base_b, grad_rows, (parts[5], parts[6], s6, n1, s5, n2), 4)
+    grad_rows, grad_down, *theirs = tie((grad_rows, grad_down, *theirs))
     grad_up = ours[0].astype(F32)
     for value in theirs:
         grad_up = grad_up + value.astype(F32)

time: 95.2 us -> 87.9 us (0.923)
  waiting for transfers between devices: 27.9 us -> 19 us
  Pallas kernels: 37.2 us -> 34.2 us
  starting transfers between devices: 21.6 us -> 24.2 us
  local copies, waits for them, and re-layouts: 2.03 us -> 3.86 us
    ppermute x6, waiting for transfers between devices: 15.4 us -> 8.64 us  [on_device(): pair = lambda value: lax.ppermute(value, 'job', PAIR)]
    unnamed x24 -> x26, local copies, waits for them, and re-layouts: 1.99 us -> 3.83 us
    ppermute x6, starting transfers between devices: 7.53 us -> 9.01 us  [on_device(): pair = lambda value: lax.ppermute(value, 'job', PAIR)]
    ppermute x6, waiting for transfers between devices: 6.33 us -> 4.89 us  [on_device(): lax.ppermute(value, 'job', [(i, i ^ d) for i in range(JOBS)])]
    pallas_call x2, Pallas kernels: 9.72 us -> 8.39 us  [the longest x1 4.96 us: last(): pl.pallas_call(last_kernel, grid=(steps,), in_specs=[smem(), whole((rows,...]
    pallas_call x1, Pallas kernels: 6.91 us -> 5.84 us  [project(): pl.pallas_call(project_kernel, grid=(rows // tile,), in_specs=[smem()] *...]
  transfers between devices with their start and end apart: 25 -> 25, of which waited for: 12 -> 10; matrix products, arithmetic and copies ran while one was open for 4% -> 4% of each run, Pallas kernels for 32% -> 39%
where the time goes in v4:
time: 87.9 us; the launch traced here: 87.6 us
  Pallas kernels  34.2 us (39%)
  starting transfers between devices  24.2 us (28%)
  waiting for transfers between devices  19 us (22%)
  other arithmetic  4.67 us (5%)
  local copies, waits for them, and re-layouts  3.86 us (4%)
  between operations  1.54 us (2%)
    pallas_call x2, Pallas kernels, base(): pl.pallas_call(base_kernel, grid=(width // tile,), in_specs=[smem()] * 2...  11.9 us
    ppermute x6, starting transfers between devices, on_device(): pair = lambda value: lax.ppermute(value, 'job', PAIR)  9.01 us
    ppermute x6, starting transfers between devices, on_device(): lax.ppermute(value, 'job', [(i, i ^ d) for i in range(JOBS)])  8.86 us
    ppermute x6, waiting for transfers between devices, on_device(): pair = lambda value: lax.ppermute(value, 'job', PAIR)  8.64 us
    pallas_call x1, Pallas kernels, pull(): pl.pallas_call(functools.partial(pull_kernel, norm), grid=(width // tile,...  6.51 us
    pallas_call x1, Pallas kernels, project(): pl.pallas_call(project_kernel, grid=(rows // tile,), in_specs=[smem()] *...  5.84 us
    pallas_call x1, Pallas kernels, last(): pl.pallas_call(last_kernel, grid=(steps,), in_specs=[smem(), whole((rows,...  4.96 us
    ppermute x6, waiting for transfers between devices, on_device(): lax.ppermute(value, 'job', [(i, i ^ d) for i in range(JOBS)])  4.89 us
  transfers between devices with their start and end apart: 25, of which 10 were waited for; matrix products, arithmetic and copies ran while one was open for 4% of the time, Pallas kernels for 39%

profile of v4, /device:TPU:0, one launch (start us, length us, event | category | flops | bytes accessed | tf_op | source)
XLA Modules:
  0.0 87.6 jit_solution(9017007208538240104)
XLA Ops:
  1.1 2.6 %collective-permute-start.4 = (bf16[256,1024]{1,0:T(8,128)(2,1)}, bf16[256,1024]{1,0:T(8,128)(2,1)S(1)}, u32[]{:S(2)}, u32[]{:S(2)}) collective-permute-start(bf16[256,1024]{1,0:T(8,128)(2,1)} %bitcast.22), channel_id=1, source_target_pairs={{0,8},{8,0},{4,12},{12,4},{1,9},{9,1},{5,13},{13,5},{2,10},{10,2},... | collective-permute-start | bytes 1572872 | tf_op jit(solution)/shard_map/ppermute | solution.py:454
  3.7 3.6 %collective-permute-start.2 = (bf16[256,128]{1,0:T(8,128)(2,1)}, bf16[256,128]{1,0:T(8,128)(2,1)S(1)}, u32[]{:S(2)}, u32[]{:S(2)}) collective-permute-start(bf16[256,128]{1,0:T(8,128)(2,1)} %bitcast.32), channel_id=1, source_target_pairs={{0,3},{1,2},{2,1},{3,0},{4,7},{5,6},{6,5},{7,4},{8,11},{9,10},{10,... | collective-permute-start | bytes 196616 | tf_op jit(solution)/shard_map/ppermute | solution.py:453
  10.2 3.6 %collective-permute-done.1 = bf16[256,128]{1,0:T(8,128)(2,1)S(1)} collective-permute-done((bf16[256,128]{1,0:T(8,128)(2,1)}, bf16[256,128]{1,0:T(8,128)(2,1)S(1)}, u32[]{:S(2)}, u32[]{:S(2)}) %collective-permute-start.1) | collective-permute-done | bytes 65568 | tf_op jit(solution)/shard_map/ppermute | solution.py:453
  15.3 1.3 %fusion = s32[]{:T(128)} fusion(s32[4]{0:T(128)} %owners.5, s32[4]{0:T(128)} %ranks.3), kind=kLoop, calls=%fused_computation.17 | loop fusion | flops 11 | bytes 36 | tf_op jit(solution)/shard_map/reduce_sum | solution.py:443
  18.0 4.3 %collective-permute-done.3.u2 = bf16[4,256,128]{2,1,0:T(8,128)(2,1)S(1)} collective-permute-done((bf16[4,256,128]{2,1,0:T(8,128)(2,1)S(1)}, bf16[4,256,128]{2,1,0:T(8,128)(2,1)S(1)}, u32[]{:S(2)}, u32[]{:S(2)}) %collective-permute-start.3) | collective-permute-done | bytes 262176 | tf_op jit(solution)/shard_map/ppermute | solution.py:454
  22.9 1.2 %collective-permute-done.6.refs_2_ = bf16[64,3072]{1,0:T(8,128)(2,1)S(1)} collective-permute-done((bf16[64,3072]{1,0:T(8,128)(2,1)S(1)}, bf16[64,3072]{1,0:T(8,128)(2,1)S(1)}, u32[]{:S(2)}, u32[]{:S(2)}) %collective-permute-start.6) | collective-permute-done | bytes 393248 | tf_op jit(solution)/shard_map/ppermute | solution.py:451
  24.3 2.0 %collective-permute-start.10 = (bf16[64,3072]{1,0:T(8,128)(2,1)S(1)}, bf16[64,3072]{1,0:T(8,128)(2,1)S(1)}, u32[]{:S(2)}, u32[]{:S(2)}) collective-permute-start(bf16[64,3072]{1,0:T(8,128)(2,1)S(1)} %get-tuple-element.156), channel_id=1, source_target_pairs={{0,1},{1,0},{2,3},{3,2},{4,5},{5,4},{6,7},{7,6},{8,9},{9,8},{10,11... | collective-permute-start | bytes 1179656 | tf_op jit(solution)/shard_map/ppermute | solution.py:451
  29.0 6.5 %pull_and_part_down.1 = (bf16[64,3072]{1,0:T(8,128)(2,1)S(1)}, bf16[64,3072]{1,0:T(8,128)(2,1)S(1)}, bf16[64,3072]{1,0:T(8,128)(2,1)S(1)}, bf16[64,3072]{1,0:T(8...) custom-call(s32[1,8]{1,0:T(1,128)S(1)} %copy-done.9, ...), custom_call_target="tpu_custom_call" | custom-call | flops 2013265920 | bytes 12451840 | tf_op jit(solution)/shard_map/pull_and_part_down/pallas_call | solution.py:166
  36.0 1.3 %collective-permute-start.12 = (bf16[64,3072]{1,0:T(8,128)(2,1)S(1)}, bf16[64,3072]{1,0:T(8,128)(2,1)S(1)}, u32[]{:S(2)}, u32[]{:S(2)}) collective-permute-start(bf16[64,3072]{1,0:T(8,128)(2,1)S(1)} %get-tuple-element.99), channel_id=1, source_target_pairs={{0,1},{1,0},{2,3},{3,2},{4,5},{5,4},{6,7},{7,6},{8,9},{9,8},{10,11... | collective-permute-start | bytes 1179656 | tf_op jit(solution)/shard_map/ppermute | solution.py:451
  37.3 5.9 %base_term.2.base_ref = bf16[1024,1536]{1,0:T(8,128)(2,1)S(1)} custom-call(s32[1,8]{1,0:T(1,128)S(1)} %copy-done.12, s32[3]{0:T(128)S(1)} %pad_add_fusion.place, bf16[256,1024]{1,0:T(8,128)(2,1)} %bitcast.24, bf16[256,1024]{1,0:T(8,128)(2,1)} %copy-done.1, bf16[256,1024]{1,0:T(8,128)(2,1)} %copy-done.3, bf16[256,1024]{1,0:T(8,128)(2,1)} %copy-done.5, ...), custom_call_target="tpu_custom_call" | custom-call | flops 3221225472 | bytes 8388608 | tf_op jit(solution)/shard_map/base_term/pallas_call | solution.py:294
  43.2 3.5 %collective-permute-done.12.refs_4_ = bf16[64,3072]{1,0:T(8,128)(2,1)S(1)} collective-permute-done((bf16[64,3072]{1,0:T(8,128)(2,1)S(1)}, bf16[64,3072]{1,0:T(8,128)(2,1)S(1)}, u32[]{:S(2)}, u32[]{:S(2)}) %collective-permute-start.12) | collective-permute-done | bytes 393248 | tf_op jit(solution)/shard_map/ppermute | solution.py:451
  46.9 1.8 %collective-permute-start.14 = (bf16[64,3072]{1,0:T(8,128)(2,1)S(1)}, bf16[64,3072]{1,0:T(8,128)(2,1)S(1)}, u32[]{:S(2)}, u32[]{:S(2)}) collective-permute-start(bf16[64,3072]{1,0:T(8,128)(2,1)S(1)} %select_select_fusion), channel_id=1, source_target_pairs={{0,1},{1,0},{2,3},{3,2},{4,5},{5,4},{6,7},{7,6},{8,9},{9,8},{10,11... | collective-permute-start | bytes 1179656 | tf_op jit(solution)/shard_map/ppermute | solution.py:451
  48.7 6.0 %base_term.3.base_ref = bf16[1024,1536]{1,0:T(8,128)(2,1)S(1)} custom-call(s32[1,8]{1,0:T(1,128)S(1)} %copy-done.12, s32[3]{0:T(128)S(1)} %pad_add_fusion.place, bf16[256,1024]{1,0:T(8,128)(2,1)} %bitcast.25, bf16[256,1024]{1,0:T(8,128)(2,1)} %copy-done.1, bf16[256,1024]{1,0:T(8,128)(2,1)} %copy-done.3, bf16[256,1024]{1,0:T(8,128)(2,1)} %copy-done.5, ...), custom_call_target="tpu_custom_call" | custom-call | flops 3221225472 | bytes 8388608 | tf_op jit(solution)/shard_map/base_term/pallas_call | solution.py:294
  54.7 2.1 %collective-permute-done.14.refs_5_ = bf16[64,3072]{1,0:T(8,128)(2,1)S(1)} collective-permute-done((bf16[64,3072]{1,0:T(8,128)(2,1)S(1)}, bf16[64,3072]{1,0:T(8,128)(2,1)S(1)}, u32[]{:S(2)}, u32[]{:S(2)}) %collective-permute-start.14) | collective-permute-done | bytes 393248 | tf_op jit(solution)/shard_map/ppermute | solution.py:451
  57.0 2.0 %collective-permute-start.16 = (bf16[64,3072]{1,0:T(8,128)(2,1)S(1)}, bf16[64,3072]{1,0:T(8,128)(2,1)S(1)}, u32[]{:S(2)}, u32[]{:S(2)}) collective-permute-start(bf16[64,3072]{1,0:T(8,128)(2,1)S(1)} %add_convert_fusion.3), channel_id=1, source_target_pairs={{0,1},{1,0},{2,3},{3,2},{4,5},{5,4},{6,7},{7,6},{8,9},{9,8},{10,11... | collective-permute-start | bytes 1179656 | tf_op jit(solution)/shard_map/ppermute | solution.py:451
  59.1 5.8 %project.1 = (bf16[1024,128]{1,0:T(8,128)(2,1)S(1)}, bf16[384,3072]{1,0:T(8,128)(2,1)S(1)}) custom-call(s32[1,8]{1,0:T(1,128)S(1)} %copy-done.10, s32[4]{0:T(128)S(1)} %copy-done.8, s32[3]{0:T(128)S(1)} %pad_add_fusion.place, bf16[64,3072]{1,0:T(8,128)(2,1)S(1)} %get-tuple-element.80.refs_0_, bf16[64,3072]{1,0:T(8,128)(2,1)S(1)} %get-tuple-element.84.refs_1_, ...), custom_call_target="tpu_custom_call" | custom-call | flops 2415919104 | bytes 11010048 | tf_op jit(solution)/shard_map/project/pallas_call | solution.py:250
  65.0 1.6 %collective-permute-done.16.t2 = bf16[64,3072]{1,0:T(8,128)(2,1)S(1)} collective-permute-done((bf16[64,3072]{1,0:T(8,128)(2,1)S(1)}, bf16[64,3072]{1,0:T(8,128)(2,1)S(1)}, u32[]{:S(2)}, u32[]{:S(2)}) %collective-permute-start.16) | collective-permute-done | bytes 393248 | tf_op jit(solution)/shard_map/ppermute | solution.py:451
  66.6 1.5 %collective-permute-start.18 = (bf16[1024,128]{1,0:T(8,128)(2,1)S(1)}, bf16[1024,128]{1,0:T(8,128)(2,1)S(1)}, u32[]{:S(2)}, u32[]{:S(2)}) collective-permute-start(bf16[1024,128]{1,0:T(8,128)(2,1)S(1)} %get-tuple-element.131), channel_id=1, source_target_pairs={{0,8},{8,0},{4,12},{12,4},{1,9},{9,1},{5,13},{13,5},{2,10},{10,2},... | collective-permute-start | bytes 786440 | tf_op jit(solution)/shard_map/ppermute | solution.py:454
  68.5 1.8 %collective-permute-start.20 = (bf16[64,3072]{1,0:T(8,128)(2,1)S(1)}, bf16[64,3072]{1,0:T(8,128)(2,1)S(1)}, u32[]{:S(2)}, u32[]{:S(2)}) collective-permute-start(bf16[64,3072]{1,0:T(8,128)(2,1)S(1)} %add_convert_fusion.1), channel_id=1, source_target_pairs={{0,1},{1,0},{2,3},{3,2},{4,5},{5,4},{6,7},{7,6},{8,9},{9,8},{10,11... | collective-permute-start | bytes 1179656 | tf_op jit(solution)/shard_map/ppermute | solution.py:451
  70.3 3.4 %grad_rows.1.filled_ref = bf16[1024,3072]{1,0:T(8,128)(2,1)} custom-call(bf16[1024,384]{1,0:T(8,128)(2,1)S(1)} %get-tuple-element.135.wide_ref, bf16[384,3072]{1,0:T(8,128)(2,1)S(1)} %get-tuple-element.136.table_ref, bf16[1024,1536]{1,0:T(8,128)(2,1)S(1)} %base_term.2.base_ref), custom_call_target="tpu_custom_call" | custom-call | flops 1207959552 | bytes 8257536 | tf_op jit(solution)/shard_map/grad_rows/pallas_call | solution.py:317
  75.5 1.3 %part_up.1 = (bf16[256,128]{1,0:T(8,128)(2,1)S(1)}, bf16[256,128]{1,0:T(8,128)(2,1)S(1)}, bf16[256,128]{1,0:T(8,128)(2,1)S(1)}, bf16[256,128]{1,0:T(8,128)(2,1)S(1)}) custom-call(s32[1,8]{1,0:T(1,128)S(1)} %copy-done.10, s32[1,8]{1,0:T(1,128)S(1)} %copy-done.12, s32[4]{0:T(128)S(1)} %copy-done.8, s32[4]{0:T(128)S(1)} %copy-done.11, s32[3]{0:T(128)S(1)} %pad_add_fusion.place, ...), custom_call_target="tpu_custom_call" | custom-call | flops 201326592 | bytes 2621440 | tf_op jit(solution)/shard_map/part_up/pallas_call | solution.py:363
  76.9 2.0 %collective-permute-start.22 = (bf16[256,128]{1,0:T(8,128)(2,1)S(1)}, bf16[256,128]{1,0:T(8,128)(2,1)S(1)}, u32[]{:S(2)}, u32[]{:S(2)}) collective-permute-start(bf16[256,128]{1,0:T(8,128)(2,1)S(1)} %get-tuple-element.134), channel_id=1, source_target_pairs={{0,1},{1,0},{2,3},{3,2},{4,5},{5,4},{6,7},{7,6},{8,9},{9,8},{10,11... | collective-permute-start | bytes 196616 | tf_op jit(solution)/shard_map/ppermute | solution.py:453
  78.8 1.3 %collective-permute-start.23 = (bf16[256,128]{1,0:T(8,128)(2,1)S(1)}, bf16[256,128]{1,0:T(8,128)(2,1)S(1)}, u32[]{:S(2)}, u32[]{:S(2)}) collective-permute-start(bf16[256,128]{1,0:T(8,128)(2,1)S(1)} %get-tuple-element.145), channel_id=1, source_target_pairs={{0,2},{1,3},{2,0},{3,1},{4,6},{5,7},{6,4},{7,5},{8,10},{9,11},{10,... | collective-permute-start | bytes 196616 | tf_op jit(solution)/shard_map/ppermute | solution.py:453
  81.4 5.0 %grad_rows_and_down.1 = (bf16[1024,3072]{1,0:T(8,128)(2,1)}, f32[3072,128]{1,0:T(8,128)}) custom-call(s32[3]{0:T(128)S(1)} %pad_add_fusion.place, bf16[1024,384]{1,0:T(8,128)(2,1)S(1)} %get-tuple-element.135.wide_ref, bf16[384,3072]{1,0:T(8,128)(2,1)S(1)} %get-tuple-element.136.table_ref, ...), custom_call_target="tpu_custom_call", output_to_operand_aliasing={{0}: (10, {})} | custom-call | flops 1207959552 | bytes 12189696 | tf_op jit(solution)/shard_map/grad_rows_and_down/pallas_call | solution.py:400
  (75 shorter events, 14.5 us)
Async XLA Ops:
  0.6 21.7 %collective-permute-start.5 = (bf16[256,1024]{1,0:T(8,128)(2,1)}, bf16[256,1024]{1,0:T(8,128)(2,1)S(1)}, u32[]{:S(2)}, u32[]{:S(2)}) collective-permute-start(bf16[256,1024]{1,0:T(8,128)(2,1)} %bitcast.21), channel_id=1, source_target_pairs={{0,4},{4,0},{8,12},{12,8},{1,5},{5,1},{9,13},{13,9},{2,6},{6,2},{1... | collective-permute-start | bytes 1572872 | tf_op jit(solution)/shard_map/ppermute | solution.py:455
  1.1 21.1 %collective-permute-start.4 = (bf16[256,1024]{1,0:T(8,128)(2,1)}, bf16[256,1024]{1,0:T(8,128)(2,1)S(1)}, u32[]{:S(2)}, u32[]{:S(2)}) collective-permute-start(bf16[256,1024]{1,0:T(8,128)(2,1)} %bitcast.22), channel_id=1, source_target_pairs={{0,8},{8,0},{4,12},{12,4},{1,9},{9,1},{5,13},{13,5},{2,10},{10,2},... | collective-permute-start | bytes 1572872 | tf_op jit(solution)/shard_map/ppermute | solution.py:454
  3.7 6.5 %collective-permute-start.2 = (bf16[256,128]{1,0:T(8,128)(2,1)}, bf16[256,128]{1,0:T(8,128)(2,1)S(1)}, u32[]{:S(2)}, u32[]{:S(2)}) collective-permute-start(bf16[256,128]{1,0:T(8,128)(2,1)} %bitcast.32), channel_id=1, source_target_pairs={{0,3},{1,2},{2,1},{3,0},{4,7},{5,6},{6,5},{7,4},{8,11},{9,10},{10,... | collective-permute-start | bytes 196616 | tf_op jit(solution)/shard_map/ppermute | solution.py:453
  7.3 6.5 %collective-permute-start.1 = (bf16[256,128]{1,0:T(8,128)(2,1)}, bf16[256,128]{1,0:T(8,128)(2,1)S(1)}, u32[]{:S(2)}, u32[]{:S(2)}) collective-permute-start(bf16[256,128]{1,0:T(8,128)(2,1)} %bitcast.33), channel_id=1, source_target_pairs={{0,2},{1,3},{2,0},{3,1},{4,6},{5,7},{6,4},{7,5},{8,10},{9,11},{10,... | collective-permute-start | bytes 196616 | tf_op jit(solution)/shard_map/ppermute | solution.py:453
  7.3 6.5 %collective-permute-start = (bf16[256,128]{1,0:T(8,128)(2,1)}, bf16[256,128]{1,0:T(8,128)(2,1)S(1)}, u32[]{:S(2)}, u32[]{:S(2)}) collective-permute-start(bf16[256,128]{1,0:T(8,128)(2,1)} %bitcast.34), channel_id=1, source_target_pairs={{0,1},{1,0},{2,3},{3,2},{4,5},{5,4},{6,7},{7,6},{8,9},{9,8},{10,11... | collective-permute-start | bytes 196616 | tf_op jit(solution)/shard_map/ppermute | solution.py:453
  10.2 12.7 %collective-permute-start.7 = (bf16[64,3072]{1,0:T(8,128)(2,1)S(1)}, bf16[64,3072]{1,0:T(8,128)(2,1)S(1)}, u32[]{:S(2)}, u32[]{:S(2)}) collective-permute-start(bf16[64,3072]{1,0:T(8,128)(2,1)S(1)} %get-tuple-element.80.refs_0_), channel_id=1, source_target_pairs={{1,2},{2,1},{0,4},{3,7},{5,6},{6,5},{4,0},{7,3},{9,10},{10,9},{8,1... | collective-permute-start | bytes 1179656 | tf_op jit(solution)/shard_map/ppermute | solution.py:452
  13.8 10.3 %collective-permute-start.6 = (bf16[64,3072]{1,0:T(8,128)(2,1)S(1)}, bf16[64,3072]{1,0:T(8,128)(2,1)S(1)}, u32[]{:S(2)}, u32[]{:S(2)}) collective-permute-start(bf16[64,3072]{1,0:T(8,128)(2,1)S(1)} %get-tuple-element.80.refs_0_), channel_id=1, source_target_pairs={{0,1},{1,0},{2,3},{3,2},{4,5},{5,4},{6,7},{7,6},{8,9},{9,8},{10,11... | collective-permute-start | bytes 1179656 | tf_op jit(solution)/shard_map/ppermute | solution.py:451
  14.7 7.6 %collective-permute-start.3 = (bf16[4,256,128]{2,1,0:T(8,128)(2,1)S(1)}, bf16[4,256,128]{2,1,0:T(8,128)(2,1)S(1)}, u32[]{:S(2)}, u32[]{:S(2)}) collective-permute-start(bf16[4,256,128]{2,1,0:T(8,128)(2,1)S(1)} %pad_maximum_fusion.1.u0), channel_id=1, source_target_pairs={{0,8},{8,0},{4,12},{12,4},{1,9},{9,1},{5,13},{13,5},{2,10},{10,2},... | collective-permute-start | bytes 786440 | tf_op jit(solution)/shard_map/ppermute | solution.py:454
  22.4 3.9 %collective-permute-start.8 = (bf16[2,4,256,128]{3,2,1,0:T(8,128)(2,1)S(1)}, bf16[2,4,256,128]{3,2,1,0:T(8,128)(2,1)S(1)}, u32[]{:S(2)}, u32[]{:S(2)}) collective-permute-start(bf16[2,4,256,128]{3,2,1,0:T(8,128)(2,1)S(1)} %pad_maximum_fusion), channel_id=1, source_target_pairs={{0,4},{4,0},{8,12},{12,8},{1,5},{5,1},{9,13},{13,9},{2,6},{6,2},{1... | collective-permute-start | bytes 1572872 | tf_op jit(solution)/shard_map/ppermute | solution.py:455
  22.4 3.8 %collective-permute-start.9 = (bf16[256,1024]{1,0:T(8,128)(2,1)S(1)}, bf16[256,1024]{1,0:T(8,128)(2,1)S(1)}, u32[]{:S(2)}, u32[]{:S(2)}) collective-permute-start(bf16[256,1024]{1,0:T(8,128)(2,1)S(1)} %collective-permute-done.4.g2), channel_id=1, source_target_pairs={{0,4},{4,0},{8,12},{12,8},{1,5},{5,1},{9,13},{13,9},{2,6},{6,2},{1... | collective-permute-start | bytes 1572872 | tf_op jit(solution)/shard_map/ppermute | solution.py:455
  24.2 11.3 %collective-permute-start.11 = (bf16[64,3072]{1,0:T(8,128)(2,1)S(1)}, bf16[64,3072]{1,0:T(8,128)(2,1)S(1)}, u32[]{:S(2)}, u32[]{:S(2)}) collective-permute-start(bf16[64,3072]{1,0:T(8,128)(2,1)S(1)} %get-tuple-element.155), channel_id=1, source_target_pairs={{1,2},{2,1},{0,4},{3,7},{5,6},{6,5},{4,0},{7,3},{9,10},{10,9},{8,1... | collective-permute-start | bytes 1179656 | tf_op jit(solution)/shard_map/ppermute | solution.py:452
  24.3 11.5 %collective-permute-start.10 = (bf16[64,3072]{1,0:T(8,128)(2,1)S(1)}, bf16[64,3072]{1,0:T(8,128)(2,1)S(1)}, u32[]{:S(2)}, u32[]{:S(2)}) collective-permute-start(bf16[64,3072]{1,0:T(8,128)(2,1)S(1)} %get-tuple-element.156), channel_id=1, source_target_pairs={{0,1},{1,0},{2,3},{3,2},{4,5},{5,4},{6,7},{7,6},{8,9},{9,8},{10,11... | collective-permute-start | bytes 1179656 | tf_op jit(solution)/shard_map/ppermute | solution.py:451
  36.0 10.7 %collective-permute-start.12 = (bf16[64,3072]{1,0:T(8,128)(2,1)S(1)}, bf16[64,3072]{1,0:T(8,128)(2,1)S(1)}, u32[]{:S(2)}, u32[]{:S(2)}) collective-permute-start(bf16[64,3072]{1,0:T(8,128)(2,1)S(1)} %get-tuple-element.99), channel_id=1, source_target_pairs={{0,1},{1,0},{2,3},{3,2},{4,5},{5,4},{6,7},{7,6},{8,9},{9,8},{10,11... | collective-permute-start | bytes 1179656 | tf_op jit(solution)/shard_map/ppermute | solution.py:451
  37.3 9.4 %collective-permute-start.13 = (bf16[64,3072]{1,0:T(8,128)(2,1)S(1)}, bf16[64,3072]{1,0:T(8,128)(2,1)S(1)}, u32[]{:S(2)}, u32[]{:S(2)}) collective-permute-start(bf16[64,3072]{1,0:T(8,128)(2,1)S(1)} %get-tuple-element.100), channel_id=1, source_target_pairs={{1,2},{2,1},{0,4},{3,7},{5,6},{6,5},{4,0},{7,3},{9,10},{10,9},{8,1... | collective-permute-start | bytes 1179656 | tf_op jit(solution)/shard_map/ppermute | solution.py:452
  46.9 9.9 %collective-permute-start.14 = (bf16[64,3072]{1,0:T(8,128)(2,1)S(1)}, bf16[64,3072]{1,0:T(8,128)(2,1)S(1)}, u32[]{:S(2)}, u32[]{:S(2)}) collective-permute-start(bf16[64,3072]{1,0:T(8,128)(2,1)S(1)} %select_select_fusion), channel_id=1, source_target_pairs={{0,1},{1,0},{2,3},{3,2},{4,5},{5,4},{6,7},{7,6},{8,9},{9,8},{10,11... | collective-permute-start | bytes 1179656 | tf_op jit(solution)/shard_map/ppermute | solution.py:451
  48.7 8.0 %collective-permute-start.15 = (bf16[64,3072]{1,0:T(8,128)(2,1)S(1)}, bf16[64,3072]{1,0:T(8,128)(2,1)S(1)}, u32[]{:S(2)}, u32[]{:S(2)}) collective-permute-start(bf16[64,3072]{1,0:T(8,128)(2,1)S(1)} %add_convert_fusion.4), channel_id=1, source_target_pairs={{1,2},{2,1},{0,4},{3,7},{5,6},{6,5},{4,0},{7,3},{9,10},{10,9},{8,1... | collective-permute-start | bytes 1179656 | tf_op jit(solution)/shard_map/ppermute | solution.py:452
  57.0 9.5 %collective-permute-start.16 = (bf16[64,3072]{1,0:T(8,128)(2,1)S(1)}, bf16[64,3072]{1,0:T(8,128)(2,1)S(1)}, u32[]{:S(2)}, u32[]{:S(2)}) collective-permute-start(bf16[64,3072]{1,0:T(8,128)(2,1)S(1)} %add_convert_fusion.3), channel_id=1, source_target_pairs={{0,1},{1,0},{2,3},{3,2},{4,5},{5,4},{6,7},{7,6},{8,9},{9,8},{10,11... | collective-permute-start | bytes 1179656 | tf_op jit(solution)/shard_map/ppermute | solution.py:451
  59.1 7.5 %collective-permute-start.17 = (bf16[64,3072]{1,0:T(8,128)(2,1)S(1)}, bf16[64,3072]{1,0:T(8,128)(2,1)S(1)}, u32[]{:S(2)}, u32[]{:S(2)}) collective-permute-start(bf16[64,3072]{1,0:T(8,128)(2,1)S(1)} %add_convert_fusion.2), channel_id=1, source_target_pairs={{1,2},{2,1},{0,4},{3,7},{5,6},{6,5},{4,0},{7,3},{9,10},{10,9},{8,1... | collective-permute-start | bytes 1179656 | tf_op jit(solution)/shard_map/ppermute | solution.py:452
  66.6 7.2 %collective-permute-start.18 = (bf16[1024,128]{1,0:T(8,128)(2,1)S(1)}, bf16[1024,128]{1,0:T(8,128)(2,1)S(1)}, u32[]{:S(2)}, u32[]{:S(2)}) collective-permute-start(bf16[1024,128]{1,0:T(8,128)(2,1)S(1)} %get-tuple-element.131), channel_id=1, source_target_pairs={{0,8},{8,0},{4,12},{12,4},{1,9},{9,1},{5,13},{13,5},{2,10},{10,2},... | collective-permute-start | bytes 786440 | tf_op jit(solution)/shard_map/ppermute | solution.py:454
  68.5 12.9 %collective-permute-start.20 = (bf16[64,3072]{1,0:T(8,128)(2,1)S(1)}, bf16[64,3072]{1,0:T(8,128)(2,1)S(1)}, u32[]{:S(2)}, u32[]{:S(2)}) collective-permute-start(bf16[64,3072]{1,0:T(8,128)(2,1)S(1)} %add_convert_fusion.1), channel_id=1, source_target_pairs={{0,1},{1,0},{2,3},{3,2},{4,5},{5,4},{6,7},{7,6},{8,9},{9,8},{10,11... | collective-permute-start | bytes 1179656 | tf_op jit(solution)/shard_map/ppermute | solution.py:451
  70.3 11.1 %collective-permute-start.21 = (bf16[64,3072]{1,0:T(8,128)(2,1)S(1)}, bf16[64,3072]{1,0:T(8,128)(2,1)S(1)}, u32[]{:S(2)}, u32[]{:S(2)}) collective-permute-start(bf16[64,3072]{1,0:T(8,128)(2,1)S(1)} %add_convert_fusion), channel_id=1, source_target_pairs={{1,2},{2,1},{0,4},{3,7},{5,6},{6,5},{4,0},{7,3},{9,10},{10,9},{8,1... | collective-permute-start | bytes 1179656 | tf_op jit(solution)/shard_map/ppermute | solution.py:452
  76.9 10.0 %collective-permute-start.22 = (bf16[256,128]{1,0:T(8,128)(2,1)S(1)}, bf16[256,128]{1,0:T(8,128)(2,1)S(1)}, u32[]{:S(2)}, u32[]{:S(2)}) collective-permute-start(bf16[256,128]{1,0:T(8,128)(2,1)S(1)} %get-tuple-element.134), channel_id=1, source_target_pairs={{0,1},{1,0},{2,3},{3,2},{4,5},{5,4},{6,7},{7,6},{8,9},{9,8},{10,11... | collective-permute-start | bytes 196616 | tf_op jit(solution)/shard_map/ppermute | solution.py:453
  78.8 8.0 %collective-permute-start.23 = (bf16[256,128]{1,0:T(8,128)(2,1)S(1)}, bf16[256,128]{1,0:T(8,128)(2,1)S(1)}, u32[]{:S(2)}, u32[]{:S(2)}) collective-permute-start(bf16[256,128]{1,0:T(8,128)(2,1)S(1)} %get-tuple-element.145), channel_id=1, source_target_pairs={{0,2},{1,3},{2,0},{3,1},{4,6},{5,7},{6,4},{7,5},{8,10},{9,11},{10,... | collective-permute-start | bytes 196616 | tf_op jit(solution)/shard_map/ppermute | solution.py:453
  80.2 6.7 %collective-permute-start.24 = (bf16[256,128]{1,0:T(8,128)(2,1)S(1)}, bf16[256,128]{1,0:T(8,128)(2,1)S(1)}, u32[]{:S(2)}, u32[]{:S(2)}) collective-permute-start(bf16[256,128]{1,0:T(8,128)(2,1)S(1)} %get-tuple-element.146), channel_id=1, source_target_pairs={{0,3},{1,2},{2,1},{3,0},{4,7},{5,6},{6,5},{7,4},{8,11},{9,10},{10,... | collective-permute-start | bytes 196616 | tf_op jit(solution)/shard_map/ppermute | solution.py:453
  (14 other events, 82.2 us)

commit v5 on v4

--- a/solution.py
+++ b/solution.py
@@ -66,13 +66,39 @@
     )(down)
 
 
-def block_factor(ids, lengths, owners, ranks, b, rows, width):
-    adapter = ids[0, b]
-    rank = ranks[adapter]
-    live = lax.broadcasted_iota(jnp.int32, (rows, width), 0) < lengths[0, b]
+class Info:
+    def __init__(self, ref):
+        self.ref = ref
+        self.blocks = (ref.shape[0] - 3 - 2 * JOBS) // 2
+
+    @staticmethod
+    def pack(ids, lengths, owners, ranks, place):
+        return jnp.concatenate([ids[0], lengths[0], owners, ranks, place])
+
+    def adapter(self, b):
+        return self.ref[b]
+
+    def length(self, b):
+        return self.ref[self.blocks + b]
+
+    def owner(self, adapter):
+        return self.ref[2 * self.blocks + adapter]
+
+    def rank(self, adapter):
+        return self.ref[2 * self.blocks + JOBS + adapter]
+
+    def place(self):
+        first = 2 * self.blocks + 2 * JOBS
+        return self.ref[first], self.ref[first + 1], self.ref[first + 2]
+
+
+def block_factor(info, b, rows, width):
+    adapter = info.adapter(b)
+    rank = info.rank(adapter)
+    live = lax.broadcasted_iota(jnp.int32, (rows, width), 0) < info.length(b)
     keep = lax.broadcasted_iota(jnp.int32, (rows, width), 1) < rank
     scale = jnp.float32(width) / (2.0 * rank.astype(F32))
-    return owners[adapter], jnp.where(live & keep, scale, 0.0)
+    return info.owner(adapter), jnp.where(live & keep, scale, 0.0)
 
 
 def spread(low, slot):
@@ -126,13 +152,15 @@
     ]
 
 
-def pull_kernel(norm, ids, lengths, owners, ranks, place, g0, g1, g2, g3, u0, u1, u2, u3, x_ref, *rest):
+def pull_kernel(norm, info, g0, g1, g2, g3, z_ref, x_up_ref, core_ref, x_ref, *rest):
+    u0, u2, (u1, u3) = z_ref, x_up_ref, (core_ref.at[0], core_ref.at[1])
     parts, (wide_ref, up, turned, sums) = rest[:7], rest[7:]
-    t, z = place[0], place[1]
+    info = Info(info)
+    t, z, excess = info.place()
     quarter, values = g0.shape
-    rank = u0.shape[2]
+    rank = up.shape[2]
     half = rank // 2
-    block = x_ref.shape[0] // ids.shape[1]
+    block = x_ref.shape[0] // info.blocks
 
     @pl.when(pl.program_id(0) == 0)
     def _():
@@ -144,7 +172,7 @@
         for q, g in enumerate((g0, g1, g2, g3)):
             for j in range(quarter // block):
                 b = jnp.bitwise_xor(t, q) * (quarter // block) + j
-                slot, factor = block_factor(ids, lengths, owners, ranks, b, block, rank)
+                slot, factor = block_factor(info, b, block, rank)
                 pulled = jnp.dot(g[j * block : (j + 1) * block, :], up[slot], preferred_element_type=F32)
                 low = spread((pulled * factor).astype(BF16).astype(F32), slot)
                 rows = pl.ds(pl.multiple_of(b * block, block), block)
@@ -154,11 +182,11 @@
     sums[...] = (
         jnp.dot(turned[: CHUNKS * half, :], x_ref[...], preferred_element_type=F32) * norm
     ).astype(BF16)
-    for part, chunk in zip(parts, roles(z, place[2])):
+    for part, chunk in zip(parts, roles(z, excess)):
         part[...] = sums[pl.ds(pl.multiple_of(chunk * half, half), half), :]
 
 
-def pull(tables, place, grads, ups, features, norm, tile):
+def pull(info, grads, ups, features, norm, tile):
     rows, width = features.shape
     quarter, values = grads[0].shape
     rank = ups[0].shape[2]
@@ -166,9 +194,10 @@
     return pl.pallas_call(
         functools.partial(pull_kernel, norm),
         grid=(width // tile,),
-        in_specs=[smem()] * 5
+        in_specs=[smem()]
         + [whole((quarter, values))] * 4
-        + [whole((JOBS, quarter, rank))] * 4
+        + [whole((JOBS, quarter, rank))] * 2
+        + [whole((2, JOBS, quarter, rank))]
         + [pl.BlockSpec((rows, tile), lambda i: (0, i))],
         out_specs=[pl.BlockSpec((rank // 2, tile), lambda i: (0, i))] * 7 + [whole((rows, 3 * rank))],
         out_shape=[jax.ShapeDtypeStruct((rank // 2, width), BF16)] * 7
@@ -181,7 +210,7 @@
         compiler_params=params(),
         cost_estimate=cost(2 * used * rows * width, 2 * (rows * width + used * width + 2 * rows * values)),
         name="pull_and_part_down",
-    )(*tables, place, far(grads[0]), *grads[1:], *ups, far(features))
+    )(info, far(grads[0]), *grads[1:], *ups, far(features))
 
 
 def arrivals(z, excess):
@@ -209,9 +238,10 @@
     ]
 
 
-def project_kernel(ids, owners, place, *refs):
+def project_kernel(info, *refs):
     chunks = refs[:9]
     x_ref, out_ref, table_ref, turned, sems = refs[9:]
+    info = Info(info)
     half, width = chunks[0].shape
     rank = 2 * half
     rows = x_ref.shape[0]
@@ -219,24 +249,25 @@
 
     @pl.when(pl.program_id(0) == 0)
     def _():
-        where_to = arrivals(place[1], place[2])
+        _, z, excess = info.place()
+        where_to = arrivals(z, excess)
 
         def chunk_copy(k):
             start = pl.multiple_of(where_to[k] * half, half)
             return pltpu.make_async_copy(chunks[k], table_ref.at[pl.ds(start, half), :], sems.at[k])
 
         for k in range(9):
-            pl.when(where_to[k] < CHUNKS)(chunk_copy(k).start)
+            pl.when(where_to[k] < CHUNKS)(lambda k=k: chunk_copy(k).start())
         table_ref[used:, :] = jnp.zeros((half, width), BF16)
         for k in range(9):
-            pl.when(where_to[k] < CHUNKS)(chunk_copy(k).wait)
+            pl.when(where_to[k] < CHUNKS)(lambda k=k: chunk_copy(k).wait())
 
     turned[...] = lax.dot_general(
         table_ref[:used, :], x_ref[...], (((1,), (1,)), ((), ())), preferred_element_type=F32
     )
     first = pl.program_id(0) * (rows // rank)
     for j in range(rows // rank):
-        slot = owners[ids[0, first + j]]
+        slot = info.owner(info.adapter(first + j))
         columns = slice(j * rank, (j + 1) * rank)
         piece = jnp.concatenate(
             [turned[pl.ds(pl.multiple_of(slot * half, half), half), columns], turned[used - half :, columns]], axis=0
@@ -244,13 +275,13 @@
         out_ref[columns, :] = piece.T.astype(BF16)
 
 
-def project(ids, owners, place, chunks, features, tile):
+def project(info, chunks, features, tile):
     rows, width = features.shape
     half = chunks[0].shape[0]
     return pl.pallas_call(
         project_kernel,
         grid=(rows // tile,),
-        in_specs=[smem()] * 3
+        in_specs=[smem()]
         + [pl.BlockSpec(memory_space=pl.ANY)] * 9
         + [pl.BlockSpec((tile, width), lambda i: (i, 0))],
         out_specs=[
@@ -265,13 +296,14 @@
         compiler_params=params(),
         cost_estimate=cost(2 * 6 * half * rows * width, 2 * (rows * width + 12 * half * width)),
         name="project",
-    )(ids, owners, place, *chunks, far(features))
-
-
-def base_kernel(lengths, place, g0, g1, g2, g3, weight_ref, out_ref):
-    t = place[0]
+    )(info, *chunks, far(features))
+
+
+def base_kernel(info, g0, g1, g2, g3, weight_ref, out_ref):
+    info = Info(info)
+    t, _, _ = info.place()
     quarter, values = g0.shape
-    block = out_ref.shape[0] // lengths.shape[1]
+    block = out_ref.shape[0] // info.blocks
     tile = out_ref.shape[1]
     for q, g in enumerate((g0, g1, g2, g3)):
         start = pl.multiple_of(jnp.bitwise_xor(t, q) * quarter, quarter)
@@ -280,13 +312,13 @@
         )
         for j in range(quarter // block):
             b = jnp.bitwise_xor(t, q) * (quarter // block) + j
-            live = lax.broadcasted_iota(jnp.int32, (block, tile), 0) < lengths[0, b]
+            live = lax.broadcasted_iota(jnp.int32, (block, tile), 0) < info.length(b)
             out_ref[pl.ds(pl.multiple_of(start + j * block, block), block), :] = jnp.where(
                 live, term[j * block : (j + 1) * block], 0.0
             ).astype(BF16)
 
 
-def base(lengths, place, grads, weight, half_index, tile):
+def base(info, grads, weight, half_index, tile):
     width, values = weight.shape[0] // 2, weight.shape[1]
     quarter = grads[0].shape[0]
     rows = 4 * quarter
@@ -294,7 +326,7 @@
     return pl.pallas_call(
         base_kernel,
         grid=(width // tile,),
-        in_specs=[smem()] * 2
+        in_specs=[smem()]
         + [whole((quarter, values))] * 4
         + [pl.BlockSpec((tile, values), lambda i: (first + i, 0))],
         out_specs=pl.BlockSpec((rows, tile), lambda i: (0, i)),
@@ -302,7 +334,7 @@
         compiler_params=params(),
         cost_estimate=cost(2 * rows * width * values, 2 * (rows * values + width * values + rows * width)),
         name="base_term",
-    )(lengths, place, *map(far, grads), far(weight))
+    )(info, *map(far, grads), far(weight))
 
 
 def rows_kernel(wide_ref, table_ref, base_ref, out_ref):
@@ -330,19 +362,20 @@
     )(wide, table, base_half)
 
 
-def part_up_kernel(norm, ids, lengths, owners, ranks, place, g0, g1, g2, g3, a_ref, b_ref, *rest):
+def part_up_kernel(norm, info, g0, g1, g2, g3, a_ref, b_ref, *rest):
     outs, (slice_ref, wide) = rest[:JOBS], rest[JOBS:]
-    t, z, excess = place[0], place[1], place[2]
+    info = Info(info)
+    t, z, excess = info.place()
     quarter, values = g0.shape
     rank = a_ref.shape[1]
     half = rank // 2
-    block = a_ref.shape[0] // ids.shape[1]
+    block = a_ref.shape[0] // info.blocks
     columns = pl.ds(pl.multiple_of(t * quarter, quarter), quarter)
     for q, g in enumerate((g0, g1, g2, g3)):
         start = pl.multiple_of(jnp.bitwise_xor(t, q) * quarter, quarter)
         slice_ref[pl.ds(start, quarter), :] = g[:, columns]
-    for b in range(ids.shape[1]):
-        slot, factor = block_factor(ids, lengths, owners, ranks, b, block, rank)
+    for b in range(info.blocks):
+        slot, factor = block_factor(info, b, block, rank)
         rows = slice(b * block, (b + 1) * block)
         low = (a_ref[rows, :].astype(F32) + b_ref[rows, :].astype(F32)) * factor
         wide[rows, :] = spread(low.astype(BF16).astype(F32), slot).astype(BF16)
@@ -356,13 +389,13 @@
         out[...] = jnp.where(lanes < keep, gathered(full, slot, rank), 0.0).astype(BF16)
 
 
-def part_up(tables, place, grads, sums, norm):
+def part_up(info, grads, sums, norm):
     quarter, values = grads[0].shape
     rows, rank = sums[0].shape
     vmem = pl.BlockSpec(memory_space=pltpu.VMEM)
     return pl.pallas_call(
         functools.partial(part_up_kernel, norm),
-        in_specs=[smem()] * 5 + [vmem] * 6,
+        in_specs=[smem()] + [vmem] * 6,
         out_specs=[vmem] * JOBS,
         out_shape=[jax.ShapeDtypeStruct((quarter, rank), BF16)] * JOBS,
         scratch_shapes=[
@@ -372,20 +405,21 @@
         compiler_params=params(),
         cost_estimate=cost(2 * rows * quarter * 3 * rank, 2 * (rows * values + 2 * rows * rank)),
         name="part_up",
-    )(*tables, place, *grads, *sums)
-
-
-def last_kernel(place, wide_ref, table_ref, base_ref, own0, own1, t1, n1, t2, n2, filled_ref, rows_ref, down_ref):
+    )(info, *grads, *sums)
+
+
+def last_kernel(info, wide_ref, table_ref, base_ref, own0, own1, t1, n1, t2, n2, filled_ref, rows_ref, down_ref):
     del filled_ref
+    _, z, excess = Info(info).place()
     half = own0.shape[0]
     rank = 2 * half
     total = (
         jnp.concatenate([own0[...], own1[...]], axis=0).astype(F32)
         + jnp.concatenate([t1[...], t2[...]], axis=0).astype(F32)
     )
-    inner = (place[1] == 1) | (place[1] == 2)
+    inner = (z == 1) | (z == 2)
     total += jnp.where(inner, jnp.concatenate([n1[...], n2[...]], axis=0).astype(F32), 0.0)
-    keep = jnp.where(place[1] == place[2], rank, half)
+    keep = jnp.where(z == excess, rank, half)
     rows = lax.broadcasted_iota(jnp.int32, total.shape, 0)
     down_ref[...] = jnp.where(rows < keep, total, 0.0).T
     rows_ref[...] = (
@@ -393,7 +427,7 @@
     ).astype(BF16)
 
 
-def last(place, wide, table, base_half, filled, sums, steps):
+def last(info, wide, table, base_half, filled, sums, steps):
     rows, deep = wide.shape
     half, width = sums[0].shape
     tile, piece = width // 2 // steps, width // steps
@@ -420,7 +454,7 @@
         compiler_params=params(),
         cost_estimate=cost(rows * width * deep, 2 * (rows * width + deep * (rows + width // 2) + 10 * half * width)),
         name="grad_rows_and_down",
-    )(place, wide, table, base_half, *sums, filled)
+    )(info, wide, table, base_half, *sums, filled)
 
 
 def on_device(
@@ -442,7 +476,7 @@
     t, z = lax.axis_index("tensor"), lax.axis_index("job")
     excess = jnp.sum(jnp.where(adapter_rank > half, owner_slot, 0)).astype(jnp.int32)
     place = jnp.stack([t, z, excess]).astype(jnp.int32)
-    tables = (block_adapter, block_length, owner_slot, adapter_rank)
+    info = Info.pack(block_adapter, block_length, owner_slot, adapter_rank, place)
 
     inner = (z == 1) | (z == 2)
     mine = jnp.where(z < 2, 1, 2)
@@ -469,18 +503,19 @@
 
     up_x, g2, g1, up_z = tie((up_x, g2, g1, up_z))
     to_c = jnp.stack([up_z, up_x])
+    s1, m1, to_c, info = tie((s1, m1, to_c, info))
+    to_s2 = jnp.where(inner & ~top_in, m1, high)
+    to_m2 = jnp.where(top_in, high, s1)
+    to_s2, to_m2, to_c, g2 = tie((to_s2, to_m2, to_c, g2))
+    s2 = pair(to_s2)
+    m2 = middle(to_m2)
     g3 = beside(g2)
     up_c = beside(to_c)
-    s1, m1, to_c = tie((s1, m1, to_c))
-    to_s2 = jnp.where(inner & ~top_in, m1, high)
-    to_m2 = jnp.where(top_in, high, s1)
-    s2 = pair(to_s2)
-    m2 = middle(to_m2)
 
     to_s2, to_m2, up_c, g3 = tie((to_s2, to_m2, up_c, g3))
     grads = (g0, g1, g2, g3)
-    ups = (up_z, up_c[0], up_x, up_c[1])
-    *parts, wide = pull(tables, place, grads, ups, features, norm, 1024)
+    ups = (up_z, up_x, up_c)
+    *parts, wide = pull(info, grads, ups, features, norm, 1024)
 
     def added(part, value, use=None):
         value = value.astype(F32)
@@ -492,14 +527,14 @@
     to_s3, to_m3, *grads = tie((to_s3, to_m3, *grads))
     s3 = pair(to_s3)
     m3 = middle(to_m3)
-    base_a = base(block_length, place, grads, value_weight, 0, 768)
+    base_a = base(info, grads, value_weight, 0, 768)
     s3, m3, base_a = tie((s3, m3, base_a))
     to_s4 = jnp.where(inner, jnp.where(top_in, m2, m3), parts[1])
     to_n3 = added(parts[0], s3, ~top_in)
     to_s4, to_n3, *grads = tie((to_s4, to_n3, *grads))
     s4 = pair(to_s4)
     n3 = middle(to_n3)
-    base_b = base(block_length, place, grads, value_weight, 1, 768)
+    base_b = base(info, grads, value_weight, 1, 768)
     s4, n3, base_b = tie((s4, n3, base_b))
 
     to_s5 = added(parts[2], n3, inner & ~top_in)
@@ -508,7 +543,7 @@
     s5 = pair(to_s5)
     n2 = middle(to_n2)
     partial, table = project(
-        block_adapter, owner_slot, place, (low, high, s1, s2, s3, to_project, m1, m2, m3), features, 512
+        info, (low, high, s1, s2, s3, to_project, m1, m2, m3), features, 512
     )
     partial, s5, n2 = tie((partial, s5, n2))
     beyond = across(partial)
@@ -522,10 +557,10 @@
     both = (partial.astype(F32) + beyond.astype(F32)).astype(BF16)
     other = beside(both)
 
-    ours = part_up(tables, place, grads, (both, other), norm)
+    ours = part_up(info, grads, (both, other), norm)
     theirs = [swap(ours[d], d) for d in (1, 2, 3)]
     wide, table, base_b, _ = tie((wide, table, base_b, ours[1]))
-    grad_rows, grad_down = last(place, wide, table, base_b, grad_rows, (parts[5], parts[6], s6, n1, s5, n2), 4)
+    grad_rows, grad_down = last(info, wide, table, base_b, grad_rows, (parts[5], parts[6], s6, n1, s5, n2), 4)
     grad_rows, grad_down, *theirs = tie((grad_rows, grad_down, *theirs))
     grad_up = ours[0].astype(F32)
     for value in theirs:

time: 87.9 us -> 86.7 us (0.986)
  waiting for transfers between devices: 19 us -> 22.2 us
  starting transfers between devices: 24.2 us -> 21.9 us
  local copies, waits for them, and re-layouts: 3.86 us -> 2.59 us
    unnamed x26 -> x16, local copies, waits for them, and re-layouts: 3.83 us -> 1.17 us
    ppermute x6, waiting for transfers between devices: 8.64 us -> 10.6 us  [on_device(): pair = lambda value: lax.ppermute(value, 'job', PAIR)]
    ppermute x4, waiting for transfers between devices: 1.17 us -> 3.03 us  [on_device(): beside = lambda value: lax.ppermute(value, 'tensor', TENSOR_CORE)]
    ppermute x6, starting transfers between devices: 9.01 us -> 7.52 us  [on_device(): pair = lambda value: lax.ppermute(value, 'job', PAIR)]
    concatenate x0 -> x1, local copies, waits for them, and re-layouts: none -> 1.43 us  [pack(): return jnp.concatenate([ids[0], lengths[0], owners, ranks, place])]
  transfers between devices with their start and end apart: 25 -> 25, of which waited for: 10 -> 13; matrix products, arithmetic and copies ran while one was open for 4% -> 5% of each run, Pallas kernels for 39% -> 40%
where the time goes in v5:
time: 86.7 us; the launch traced here: 86.4 us
  Pallas kernels  34.3 us (40%)
  waiting for transfers between devices  22.2 us (26%)
  starting transfers between devices  21.9 us (25%)
  other arithmetic  3.95 us (5%)
  local copies, waits for them, and re-layouts  2.59 us (3%)
  between operations  1.5 us (2%)
    pallas_call x2, Pallas kernels, base(): pl.pallas_call(base_kernel, grid=(width // tile,), in_specs=[smem()] + [w...  11.9 us
    ppermute x6, waiting for transfers between devices, on_device(): pair = lambda value: lax.ppermute(value, 'job', PAIR)  10.6 us
    ppermute x6, starting transfers between devices, on_device(): lax.ppermute(value, 'job', [(i, i ^ d) for i in range(JOBS)])  8.86 us
    ppermute x6, starting transfers between devices, on_device(): pair = lambda value: lax.ppermute(value, 'job', PAIR)  7.52 us
    pallas_call x1, Pallas kernels, pull(): pl.pallas_call(functools.partial(pull_kernel, norm), grid=(width // tile,...  6.67 us
    pallas_call x1, Pallas kernels, project(): pl.pallas_call(project_kernel, grid=(rows // tile,), in_specs=[smem()] +...  5.79 us
    pallas_call x1, Pallas kernels, last(): pl.pallas_call(last_kernel, grid=(steps,), in_specs=[smem(), whole((rows,...  4.96 us
    ppermute x6, waiting for transfers between devices, on_device(): lax.ppermute(value, 'job', [(i, i ^ d) for i in range(JOBS)])  4.85 us
  transfers between devices with their start and end apart: 25, of which 13 were waited for; matrix products, arithmetic and copies ran while one was open for 5% of the time, Pallas kernels for 40%

profile of v5, /device:TPU:0, one launch (start us, length us, event | category | flops | bytes accessed | tf_op | source)
XLA Modules:
  0.0 86.4 jit_solution(3889728030328863662)
XLA Ops:
  1.1 2.6 %collective-permute-start.6 = (bf16[256,1024]{1,0:T(8,128)(2,1)}, bf16[256,1024]{1,0:T(8,128)(2,1)S(1)}, u32[]{:S(2)}, u32[]{:S(2)}) collective-permute-start(bf16[256,1024]{1,0:T(8,128)(2,1)} %bitcast.20), channel_id=1, source_target_pairs={{0,8},{8,0},{4,12},{12,4},{1,9},{9,1},{5,13},{13,5},{2,10},{10,2},... | collective-permute-start | bytes 1572872 | tf_op jit(solution)/shard_map/ppermute | solution.py:488
  3.7 3.6 %collective-permute-start.4 = (bf16[256,128]{1,0:T(8,128)(2,1)}, bf16[256,128]{1,0:T(8,128)(2,1)S(1)}, u32[]{:S(2)}, u32[]{:S(2)}) collective-permute-start(bf16[256,128]{1,0:T(8,128)(2,1)} %bitcast.30), channel_id=1, source_target_pairs={{0,3},{1,2},{2,1},{3,0},{4,7},{5,6},{6,5},{7,4},{8,11},{9,10},{10,... | collective-permute-start | bytes 196616 | tf_op jit(solution)/shard_map/ppermute | solution.py:487
  10.2 3.6 %collective-permute-done.3 = bf16[256,128]{1,0:T(8,128)(2,1)S(1)} collective-permute-done((bf16[256,128]{1,0:T(8,128)(2,1)}, bf16[256,128]{1,0:T(8,128)(2,1)S(1)}, u32[]{:S(2)}, u32[]{:S(2)}) %collective-permute-start.3) | collective-permute-done | bytes 65568 | tf_op jit(solution)/shard_map/ppermute | solution.py:487
  15.3 1.3 %fusion = s32[]{:T(128)} fusion(s32[4]{0:T(128)} %param.16, s32[4]{0:T(128)} %param.17), kind=kLoop, calls=%fused_computation.15 | loop fusion | flops 11 | bytes 36 | tf_op jit(solution)/shard_map/reduce_sum | solution.py:477
  17.3 1.4 %concatenate.3.info = s32[27]{0:T(128)S(1)} concatenate(s32[8]{0:T(128)} %bitcast.36, s32[8]{0:T(128)} %bitcast.37, s32[4]{0:T(128)} %param.16, s32[4]{0:T(128)} %param.17, s32[1]{0:T(128)} %bitcast.10, s32[1]{0:T(128)} %bitcast.11, s32[1]{0:T(128)} %bitcast.12), dimensions={0} | concatenate | bytes 216 | tf_op jit(solution)/shard_map/concatenate | solution.py:76
  18.7 3.6 %collective-permute-done.5.x_up_ref = bf16[4,256,128]{2,1,0:T(8,128)(2,1)S(1)} collective-permute-done((bf16[4,256,128]{2,1,0:T(8,128)(2,1)S(1)}, bf16[4,256,128]{2,1,0:T(8,128)(2,1)S(1)}, u32[]{:S(2)}, u32[]{:S(2)}) %collective-permute-start.5) | collective-permute-done | bytes 262176 | tf_op jit(solution)/shard_map/ppermute | solution.py:488
  22.4 1.8 %collective-permute-done.refs_2_ = bf16[64,3072]{1,0:T(8,128)(2,1)S(1)} collective-permute-done((bf16[64,3072]{1,0:T(8,128)(2,1)S(1)}, bf16[64,3072]{1,0:T(8,128)(2,1)S(1)}, u32[]{:S(2)}, u32[]{:S(2)}) %collective-permute-start) | collective-permute-done | bytes 393248 | tf_op jit(solution)/shard_map/ppermute | solution.py:485
  26.9 6.7 %pull_and_part_down.1 = (bf16[64,3072]{1,0:T(8,128)(2,1)S(1)}, bf16[64,3072]{1,0:T(8,128)(2,1)S(1)}, bf16[64,3072]{1,0:T(8,128)(2,1)S(1)}, bf16[64,3072]{1,0:T(8...) custom-call(s32[27]{0:T(128)S(1)} %concatenate.3.info, ...), custom_call_target="tpu_custom_call" | custom-call | flops 2013265920 | bytes 12451840 | tf_op jit(solution)/shard_map/pull_and_part_down/pallas_call | solution.py:194
  33.6 2.3 %collective-permute-done.10.refs_3_ = bf16[64,3072]{1,0:T(8,128)(2,1)S(1)} collective-permute-done((bf16[64,3072]{1,0:T(8,128)(2,1)S(1)}, bf16[64,3072]{1,0:T(8,128)(2,1)S(1)}, u32[]{:S(2)}, u32[]{:S(2)}) %collective-permute-start.10) | collective-permute-done | bytes 393248 | tf_op jit(solution)/shard_map/ppermute | solution.py:485
  36.0 1.8 %collective-permute-start.12 = (bf16[64,3072]{1,0:T(8,128)(2,1)S(1)}, bf16[64,3072]{1,0:T(8,128)(2,1)S(1)}, u32[]{:S(2)}, u32[]{:S(2)}) collective-permute-start(bf16[64,3072]{1,0:T(8,128)(2,1)S(1)} %get-tuple-element.111), channel_id=1, source_target_pairs={{0,1},{1,0},{2,3},{3,2},{4,5},{5,4},{6,7},{7,6},{8,9},{9,8},{10,11... | collective-permute-start | bytes 1179656 | tf_op jit(solution)/shard_map/ppermute | solution.py:485
  37.9 5.9 %base_term.2.base_ref = bf16[1024,1536]{1,0:T(8,128)(2,1)S(1)} custom-call(s32[27]{0:T(128)S(1)} %concatenate.3.info, bf16[256,1024]{1,0:T(8,128)(2,1)} %bitcast.22, bf16[256,1024]{1,0:T(8,128)(2,1)} %copy-done.1, bf16[256,1024]{1,0:T(8,128)(2,1)} %copy-done.3, bf16[256,1024]{1,0:T(8,128)(2,1)} %copy-done.5, bf16[3072,1024]{1,0:T(8,128)(2,1)} %weight_ref.3), custom_call_target="tpu_custom_call" | custom-call | flops 3221225472 | bytes 8388608 | tf_op jit(solution)/shard_map/base_term/pallas_call | solution.py:326
  43.8 2.6 %collective-permute-done.12.refs_4_ = bf16[64,3072]{1,0:T(8,128)(2,1)S(1)} collective-permute-done((bf16[64,3072]{1,0:T(8,128)(2,1)S(1)}, bf16[64,3072]{1,0:T(8,128)(2,1)S(1)}, u32[]{:S(2)}, u32[]{:S(2)}) %collective-permute-start.12) | collective-permute-done | bytes 393248 | tf_op jit(solution)/shard_map/ppermute | solution.py:485
  46.6 1.8 %collective-permute-start.14 = (bf16[64,3072]{1,0:T(8,128)(2,1)S(1)}, bf16[64,3072]{1,0:T(8,128)(2,1)S(1)}, u32[]{:S(2)}, u32[]{:S(2)}) collective-permute-start(bf16[64,3072]{1,0:T(8,128)(2,1)S(1)} %select_select_fusion), channel_id=1, source_target_pairs={{0,1},{1,0},{2,3},{3,2},{4,5},{5,4},{6,7},{7,6},{8,9},{9,8},{10,11... | collective-permute-start | bytes 1179656 | tf_op jit(solution)/shard_map/ppermute | solution.py:485
  48.4 5.9 %base_term.3.base_ref = bf16[1024,1536]{1,0:T(8,128)(2,1)S(1)} custom-call(s32[27]{0:T(128)S(1)} %concatenate.3.info, bf16[256,1024]{1,0:T(8,128)(2,1)} %bitcast.23, bf16[256,1024]{1,0:T(8,128)(2,1)} %copy-done.1, bf16[256,1024]{1,0:T(8,128)(2,1)} %copy-done.3, bf16[256,1024]{1,0:T(8,128)(2,1)} %copy-done.5, bf16[3072,1024]{1,0:T(8,128)(2,1)} %weight_ref.3), custom_call_target="tpu_custom_call" | custom-call | flops 3221225472 | bytes 8388608 | tf_op jit(solution)/shard_map/base_term/pallas_call | solution.py:326
  54.3 1.6 %collective-permute-done.14.refs_5_ = bf16[64,3072]{1,0:T(8,128)(2,1)S(1)} collective-permute-done((bf16[64,3072]{1,0:T(8,128)(2,1)S(1)}, bf16[64,3072]{1,0:T(8,128)(2,1)S(1)}, u32[]{:S(2)}, u32[]{:S(2)}) %collective-permute-start.14) | collective-permute-done | bytes 393248 | tf_op jit(solution)/shard_map/ppermute | solution.py:485
  56.2 1.8 %collective-permute-start.16 = (bf16[64,3072]{1,0:T(8,128)(2,1)S(1)}, bf16[64,3072]{1,0:T(8,128)(2,1)S(1)}, u32[]{:S(2)}, u32[]{:S(2)}) collective-permute-start(bf16[64,3072]{1,0:T(8,128)(2,1)S(1)} %add_convert_fusion.3), channel_id=1, source_target_pairs={{0,1},{1,0},{2,3},{3,2},{4,5},{5,4},{6,7},{7,6},{8,9},{9,8},{10,11... | collective-permute-start | bytes 1179656 | tf_op jit(solution)/shard_map/ppermute | solution.py:485
  58.1 5.8 %project.1 = (bf16[1024,128]{1,0:T(8,128)(2,1)S(1)}, bf16[384,3072]{1,0:T(8,128)(2,1)S(1)}) custom-call(s32[27]{0:T(128)S(1)} %concatenate.3.info, bf16[64,3072]{1,0:T(8,128)(2,1)S(1)} %get-tuple-element.84.refs_0_, bf16[64,3072]{1,0:T(8,128)(2,1)S(1)} %get-tuple-element.90.refs_1_, bf16[64,3072]{1,0:T(8,128)(2,1)S(1)} %collective-permute-done.refs_2_, ...), custom_call_target="tpu_custom_call" | custom-call | flops 2415919104 | bytes 11010048 | tf_op jit(solution)/shard_map/project/pallas_call | solution.py:281
  63.9 2.4 %collective-permute-done.16.t2 = bf16[64,3072]{1,0:T(8,128)(2,1)S(1)} collective-permute-done((bf16[64,3072]{1,0:T(8,128)(2,1)S(1)}, bf16[64,3072]{1,0:T(8,128)(2,1)S(1)}, u32[]{:S(2)}, u32[]{:S(2)}) %collective-permute-start.16) | collective-permute-done | bytes 393248 | tf_op jit(solution)/shard_map/ppermute | solution.py:485
  67.3 1.8 %collective-permute-start.20 = (bf16[64,3072]{1,0:T(8,128)(2,1)S(1)}, bf16[64,3072]{1,0:T(8,128)(2,1)S(1)}, u32[]{:S(2)}, u32[]{:S(2)}) collective-permute-start(bf16[64,3072]{1,0:T(8,128)(2,1)S(1)} %add_convert_fusion.1), channel_id=1, source_target_pairs={{0,1},{1,0},{2,3},{3,2},{4,5},{5,4},{6,7},{7,6},{8,9},{9,8},{10,11... | collective-permute-start | bytes 1179656 | tf_op jit(solution)/shard_map/ppermute | solution.py:485
  69.2 3.4 %grad_rows.1.filled_ref = bf16[1024,3072]{1,0:T(8,128)(2,1)} custom-call(bf16[1024,384]{1,0:T(8,128)(2,1)S(1)} %get-tuple-element.147.wide_ref, bf16[384,3072]{1,0:T(8,128)(2,1)S(1)} %get-tuple-element.148.table_ref, bf16[1024,1536]{1,0:T(8,128)(2,1)S(1)} %base_term.2.base_ref), custom_call_target="tpu_custom_call" | custom-call | flops 1207959552 | bytes 8257536 | tf_op jit(solution)/shard_map/grad_rows/pallas_call | solution.py:349
  74.4 1.3 %part_up.1 = (bf16[256,128]{1,0:T(8,128)(2,1)S(1)}, bf16[256,128]{1,0:T(8,128)(2,1)S(1)}, bf16[256,128]{1,0:T(8,128)(2,1)S(1)}, bf16[256,128]{1,0:T(8,128)(2,1)S(1)}) custom-call(s32[27]{0:T(128)S(1)} %concatenate.3.info, bf16[256,1024]{1,0:T(8,128)(2,1)S(1)} %bitcast.24, bf16[256,1024]{1,0:T(8,128)(2,1)S(1)} %copy-done.2, bf16[256,1024]{1,0:T(8,128)(2,1)S(1)} %copy-done.4, ...), custom_call_target="tpu_custom_call" | custom-call | flops 201326592 | bytes 2621440 | tf_op jit(solution)/shard_map/part_up/pallas_call | solution.py:396
  75.7 2.0 %collective-permute-start.22 = (bf16[256,128]{1,0:T(8,128)(2,1)S(1)}, bf16[256,128]{1,0:T(8,128)(2,1)S(1)}, u32[]{:S(2)}, u32[]{:S(2)}) collective-permute-start(bf16[256,128]{1,0:T(8,128)(2,1)S(1)} %get-tuple-element.146), channel_id=1, source_target_pairs={{0,1},{1,0},{2,3},{3,2},{4,5},{5,4},{6,7},{7,6},{8,9},{9,8},{10,11... | collective-permute-start | bytes 196616 | tf_op jit(solution)/shard_map/ppermute | solution.py:487
  77.7 1.3 %collective-permute-start.23 = (bf16[256,128]{1,0:T(8,128)(2,1)S(1)}, bf16[256,128]{1,0:T(8,128)(2,1)S(1)}, u32[]{:S(2)}, u32[]{:S(2)}) collective-permute-start(bf16[256,128]{1,0:T(8,128)(2,1)S(1)} %get-tuple-element.157), channel_id=1, source_target_pairs={{0,2},{1,3},{2,0},{3,1},{4,6},{5,7},{6,4},{7,5},{8,10},{9,11},{10,... | collective-permute-start | bytes 196616 | tf_op jit(solution)/shard_map/ppermute | solution.py:487
  80.2 5.0 %grad_rows_and_down.1 = (bf16[1024,3072]{1,0:T(8,128)(2,1)}, f32[3072,128]{1,0:T(8,128)}) custom-call(s32[27]{0:T(128)S(1)} %concatenate.3.info, bf16[1024,384]{1,0:T(8,128)(2,1)S(1)} %get-tuple-element.147.wide_ref, bf16[384,3072]{1,0:T(8,128)(2,1)S(1)} %get-tuple-element.148.table_ref, ...), custom_call_target="tpu_custom_call", output_to_operand_aliasing={{0}: (10, {})} | custom-call | flops 1207959552 | bytes 12189696 | tf_op jit(solution)/shard_map/grad_rows_and_down/pallas_call | solution.py:434
  (64 shorter events, 13.6 us)
Async XLA Ops:
  0.6 21.7 %collective-permute-start.7 = (bf16[256,1024]{1,0:T(8,128)(2,1)}, bf16[256,1024]{1,0:T(8,128)(2,1)S(1)}, u32[]{:S(2)}, u32[]{:S(2)}) collective-permute-start(bf16[256,1024]{1,0:T(8,128)(2,1)} %bitcast.19), channel_id=1, source_target_pairs={{0,4},{4,0},{8,12},{12,8},{1,5},{5,1},{9,13},{13,9},{2,6},{6,2},{1... | collective-permute-start | bytes 1572872 | tf_op jit(solution)/shard_map/ppermute | solution.py:489
  1.1 21.1 %collective-permute-start.6 = (bf16[256,1024]{1,0:T(8,128)(2,1)}, bf16[256,1024]{1,0:T(8,128)(2,1)S(1)}, u32[]{:S(2)}, u32[]{:S(2)}) collective-permute-start(bf16[256,1024]{1,0:T(8,128)(2,1)} %bitcast.20), channel_id=1, source_target_pairs={{0,8},{8,0},{4,12},{12,4},{1,9},{9,1},{5,13},{13,5},{2,10},{10,2},... | collective-permute-start | bytes 1572872 | tf_op jit(solution)/shard_map/ppermute | solution.py:488
  3.7 6.5 %collective-permute-start.4 = (bf16[256,128]{1,0:T(8,128)(2,1)}, bf16[256,128]{1,0:T(8,128)(2,1)S(1)}, u32[]{:S(2)}, u32[]{:S(2)}) collective-permute-start(bf16[256,128]{1,0:T(8,128)(2,1)} %bitcast.30), channel_id=1, source_target_pairs={{0,3},{1,2},{2,1},{3,0},{4,7},{5,6},{6,5},{7,4},{8,11},{9,10},{10,... | collective-permute-start | bytes 196616 | tf_op jit(solution)/shard_map/ppermute | solution.py:487
  7.3 6.5 %collective-permute-start.3 = (bf16[256,128]{1,0:T(8,128)(2,1)}, bf16[256,128]{1,0:T(8,128)(2,1)S(1)}, u32[]{:S(2)}, u32[]{:S(2)}) collective-permute-start(bf16[256,128]{1,0:T(8,128)(2,1)} %bitcast.31), channel_id=1, source_target_pairs={{0,2},{1,3},{2,0},{3,1},{4,6},{5,7},{6,4},{7,5},{8,10},{9,11},{10,... | collective-permute-start | bytes 196616 | tf_op jit(solution)/shard_map/ppermute | solution.py:487
  7.3 6.5 %collective-permute-start.2 = (bf16[256,128]{1,0:T(8,128)(2,1)}, bf16[256,128]{1,0:T(8,128)(2,1)S(1)}, u32[]{:S(2)}, u32[]{:S(2)}) collective-permute-start(bf16[256,128]{1,0:T(8,128)(2,1)} %bitcast.32), channel_id=1, source_target_pairs={{0,1},{1,0},{2,3},{3,2},{4,5},{5,4},{6,7},{7,6},{8,9},{9,8},{10,11... | collective-permute-start | bytes 196616 | tf_op jit(solution)/shard_map/ppermute | solution.py:487
  10.2 12.2 %collective-permute-start.1 = (bf16[64,3072]{1,0:T(8,128)(2,1)S(1)}, bf16[64,3072]{1,0:T(8,128)(2,1)S(1)}, u32[]{:S(2)}, u32[]{:S(2)}) collective-permute-start(bf16[64,3072]{1,0:T(8,128)(2,1)S(1)} %get-tuple-element.84.refs_0_), channel_id=1, source_target_pairs={{1,2},{2,1},{0,4},{3,7},{5,6},{6,5},{4,0},{7,3},{9,10},{10,9},{8,1... | collective-permute-start | bytes 1179656 | tf_op jit(solution)/shard_map/ppermute | solution.py:486
  13.8 10.3 %collective-permute-start = (bf16[64,3072]{1,0:T(8,128)(2,1)S(1)}, bf16[64,3072]{1,0:T(8,128)(2,1)S(1)}, u32[]{:S(2)}, u32[]{:S(2)}) collective-permute-start(bf16[64,3072]{1,0:T(8,128)(2,1)S(1)} %get-tuple-element.84.refs_0_), channel_id=1, source_target_pairs={{0,1},{1,0},{2,3},{3,2},{4,5},{5,4},{6,7},{7,6},{8,9},{9,8},{10,11... | collective-permute-start | bytes 1179656 | tf_op jit(solution)/shard_map/ppermute | solution.py:485
  14.7 7.6 %collective-permute-start.5 = (bf16[4,256,128]{2,1,0:T(8,128)(2,1)S(1)}, bf16[4,256,128]{2,1,0:T(8,128)(2,1)S(1)}, u32[]{:S(2)}, u32[]{:S(2)}) collective-permute-start(bf16[4,256,128]{2,1,0:T(8,128)(2,1)S(1)} %pad_maximum_fusion.1.z_ref), channel_id=1, source_target_pairs={{0,8},{8,0},{4,12},{12,4},{1,9},{9,1},{5,13},{13,5},{2,10},{10,2},... | collective-permute-start | bytes 786440 | tf_op jit(solution)/shard_map/ppermute | solution.py:488
  24.2 2.0 %collective-permute-start.8 = (bf16[2,4,256,128]{3,2,1,0:T(8,128)(2,1)S(1)}, bf16[2,4,256,128]{3,2,1,0:T(8,128)(2,1)S(1)}, u32[]{:S(2)}, u32[]{:S(2)}) collective-permute-start(bf16[2,4,256,128]{3,2,1,0:T(8,128)(2,1)S(1)} %pad_maximum_fusion), channel_id=1, source_target_pairs={{0,4},{4,0},{8,12},{12,8},{1,5},{5,1},{9,13},{13,9},{2,6},{6,2},{1... | collective-permute-start | bytes 1572872 | tf_op jit(solution)/shard_map/ppermute | solution.py:489
  24.3 2.6 %collective-permute-start.9 = (bf16[256,1024]{1,0:T(8,128)(2,1)S(1)}, bf16[256,1024]{1,0:T(8,128)(2,1)S(1)}, u32[]{:S(2)}, u32[]{:S(2)}) collective-permute-start(bf16[256,1024]{1,0:T(8,128)(2,1)S(1)} %collective-permute-done.6.g2), channel_id=1, source_target_pairs={{0,4},{4,0},{8,12},{12,8},{1,5},{5,1},{9,13},{13,9},{2,6},{6,2},{1... | collective-permute-start | bytes 1572872 | tf_op jit(solution)/shard_map/ppermute | solution.py:489
  24.8 11.1 %collective-permute-start.10 = (bf16[64,3072]{1,0:T(8,128)(2,1)S(1)}, bf16[64,3072]{1,0:T(8,128)(2,1)S(1)}, u32[]{:S(2)}, u32[]{:S(2)}) collective-permute-start(bf16[64,3072]{1,0:T(8,128)(2,1)S(1)} %get-tuple-element.95), channel_id=1, source_target_pairs={{0,1},{1,0},{2,3},{3,2},{4,5},{5,4},{6,7},{7,6},{8,9},{9,8},{10,11... | collective-permute-start | bytes 1179656 | tf_op jit(solution)/shard_map/ppermute | solution.py:485
  25.1 10.8 %collective-permute-start.11 = (bf16[64,3072]{1,0:T(8,128)(2,1)S(1)}, bf16[64,3072]{1,0:T(8,128)(2,1)S(1)}, u32[]{:S(2)}, u32[]{:S(2)}) collective-permute-start(bf16[64,3072]{1,0:T(8,128)(2,1)S(1)} %get-tuple-element.96), channel_id=1, source_target_pairs={{1,2},{2,1},{0,4},{3,7},{5,6},{6,5},{4,0},{7,3},{9,10},{10,9},{8,1... | collective-permute-start | bytes 1179656 | tf_op jit(solution)/shard_map/ppermute | solution.py:486
  36.0 10.3 %collective-permute-start.12 = (bf16[64,3072]{1,0:T(8,128)(2,1)S(1)}, bf16[64,3072]{1,0:T(8,128)(2,1)S(1)}, u32[]{:S(2)}, u32[]{:S(2)}) collective-permute-start(bf16[64,3072]{1,0:T(8,128)(2,1)S(1)} %get-tuple-element.111), channel_id=1, source_target_pairs={{0,1},{1,0},{2,3},{3,2},{4,5},{5,4},{6,7},{7,6},{8,9},{9,8},{10,11... | collective-permute-start | bytes 1179656 | tf_op jit(solution)/shard_map/ppermute | solution.py:485
  37.8 8.5 %collective-permute-start.13 = (bf16[64,3072]{1,0:T(8,128)(2,1)S(1)}, bf16[64,3072]{1,0:T(8,128)(2,1)S(1)}, u32[]{:S(2)}, u32[]{:S(2)}) collective-permute-start(bf16[64,3072]{1,0:T(8,128)(2,1)S(1)} %get-tuple-element.112), channel_id=1, source_target_pairs={{1,2},{2,1},{0,4},{3,7},{5,6},{6,5},{4,0},{7,3},{9,10},{10,9},{8,1... | collective-permute-start | bytes 1179656 | tf_op jit(solution)/shard_map/ppermute | solution.py:486
  46.6 9.4 %collective-permute-start.14 = (bf16[64,3072]{1,0:T(8,128)(2,1)S(1)}, bf16[64,3072]{1,0:T(8,128)(2,1)S(1)}, u32[]{:S(2)}, u32[]{:S(2)}) collective-permute-start(bf16[64,3072]{1,0:T(8,128)(2,1)S(1)} %select_select_fusion), channel_id=1, source_target_pairs={{0,1},{1,0},{2,3},{3,2},{4,5},{5,4},{6,7},{7,6},{8,9},{9,8},{10,11... | collective-permute-start | bytes 1179656 | tf_op jit(solution)/shard_map/ppermute | solution.py:485
  48.4 7.6 %collective-permute-start.15 = (bf16[64,3072]{1,0:T(8,128)(2,1)S(1)}, bf16[64,3072]{1,0:T(8,128)(2,1)S(1)}, u32[]{:S(2)}, u32[]{:S(2)}) collective-permute-start(bf16[64,3072]{1,0:T(8,128)(2,1)S(1)} %add_convert_fusion.4), channel_id=1, source_target_pairs={{1,2},{2,1},{0,4},{3,7},{5,6},{6,5},{4,0},{7,3},{9,10},{10,9},{8,1... | collective-permute-start | bytes 1179656 | tf_op jit(solution)/shard_map/ppermute | solution.py:486
  56.2 10.0 %collective-permute-start.16 = (bf16[64,3072]{1,0:T(8,128)(2,1)S(1)}, bf16[64,3072]{1,0:T(8,128)(2,1)S(1)}, u32[]{:S(2)}, u32[]{:S(2)}) collective-permute-start(bf16[64,3072]{1,0:T(8,128)(2,1)S(1)} %add_convert_fusion.3), channel_id=1, source_target_pairs={{0,1},{1,0},{2,3},{3,2},{4,5},{5,4},{6,7},{7,6},{8,9},{9,8},{10,11... | collective-permute-start | bytes 1179656 | tf_op jit(solution)/shard_map/ppermute | solution.py:485
  58.0 8.2 %collective-permute-start.17 = (bf16[64,3072]{1,0:T(8,128)(2,1)S(1)}, bf16[64,3072]{1,0:T(8,128)(2,1)S(1)}, u32[]{:S(2)}, u32[]{:S(2)}) collective-permute-start(bf16[64,3072]{1,0:T(8,128)(2,1)S(1)} %add_convert_fusion.2), channel_id=1, source_target_pairs={{1,2},{2,1},{0,4},{3,7},{5,6},{6,5},{4,0},{7,3},{9,10},{10,9},{8,1... | collective-permute-start | bytes 1179656 | tf_op jit(solution)/shard_map/ppermute | solution.py:486
  66.2 6.4 %collective-permute-start.18 = (bf16[1024,128]{1,0:T(8,128)(2,1)S(1)}, bf16[1024,128]{1,0:T(8,128)(2,1)S(1)}, u32[]{:S(2)}, u32[]{:S(2)}) collective-permute-start(bf16[1024,128]{1,0:T(8,128)(2,1)S(1)} %get-tuple-element.143), channel_id=1, source_target_pairs={{0,8},{8,0},{4,12},{12,4},{1,9},{9,1},{5,13},{13,5},{2,10},{10,2},... | collective-permute-start | bytes 786440 | tf_op jit(solution)/shard_map/ppermute | solution.py:488
  67.3 12.9 %collective-permute-start.20 = (bf16[64,3072]{1,0:T(8,128)(2,1)S(1)}, bf16[64,3072]{1,0:T(8,128)(2,1)S(1)}, u32[]{:S(2)}, u32[]{:S(2)}) collective-permute-start(bf16[64,3072]{1,0:T(8,128)(2,1)S(1)} %add_convert_fusion.1), channel_id=1, source_target_pairs={{0,1},{1,0},{2,3},{3,2},{4,5},{5,4},{6,7},{7,6},{8,9},{9,8},{10,11... | collective-permute-start | bytes 1179656 | tf_op jit(solution)/shard_map/ppermute | solution.py:485
  69.1 11.1 %collective-permute-start.21 = (bf16[64,3072]{1,0:T(8,128)(2,1)S(1)}, bf16[64,3072]{1,0:T(8,128)(2,1)S(1)}, u32[]{:S(2)}, u32[]{:S(2)}) collective-permute-start(bf16[64,3072]{1,0:T(8,128)(2,1)S(1)} %add_convert_fusion), channel_id=1, source_target_pairs={{1,2},{2,1},{0,4},{3,7},{5,6},{6,5},{4,0},{7,3},{9,10},{10,9},{8,1... | collective-permute-start | bytes 1179656 | tf_op jit(solution)/shard_map/ppermute | solution.py:486
  75.7 10.0 %collective-permute-start.22 = (bf16[256,128]{1,0:T(8,128)(2,1)S(1)}, bf16[256,128]{1,0:T(8,128)(2,1)S(1)}, u32[]{:S(2)}, u32[]{:S(2)}) collective-permute-start(bf16[256,128]{1,0:T(8,128)(2,1)S(1)} %get-tuple-element.146), channel_id=1, source_target_pairs={{0,1},{1,0},{2,3},{3,2},{4,5},{5,4},{6,7},{7,6},{8,9},{9,8},{10,11... | collective-permute-start | bytes 196616 | tf_op jit(solution)/shard_map/ppermute | solution.py:487
  77.7 8.0 %collective-permute-start.23 = (bf16[256,128]{1,0:T(8,128)(2,1)S(1)}, bf16[256,128]{1,0:T(8,128)(2,1)S(1)}, u32[]{:S(2)}, u32[]{:S(2)}) collective-permute-start(bf16[256,128]{1,0:T(8,128)(2,1)S(1)} %get-tuple-element.157), channel_id=1, source_target_pairs={{0,2},{1,3},{2,0},{3,1},{4,6},{5,7},{6,4},{7,5},{8,10},{9,11},{10,... | collective-permute-start | bytes 196616 | tf_op jit(solution)/shard_map/ppermute | solution.py:487
  79.0 6.7 %collective-permute-start.24 = (bf16[256,128]{1,0:T(8,128)(2,1)S(1)}, bf16[256,128]{1,0:T(8,128)(2,1)S(1)}, u32[]{:S(2)}, u32[]{:S(2)}) collective-permute-start(bf16[256,128]{1,0:T(8,128)(2,1)S(1)} %get-tuple-element.158), channel_id=1, source_target_pairs={{0,3},{1,2},{2,1},{3,0},{4,7},{5,6},{6,5},{7,4},{8,11},{9,10},{10,... | collective-permute-start | bytes 196616 | tf_op jit(solution)/shard_map/ppermute | solution.py:487
  (9 other events, 69.5 us)

commit v6 on v5

--- a/solution.py
+++ b/solution.py
@@ -545,7 +545,7 @@
     partial, table = project(
         info, (low, high, s1, s2, s3, to_project, m1, m2, m3), features, 512
     )
-    partial, s5, n2 = tie((partial, s5, n2))
+    partial, s5 = tie((partial, s5))
     beyond = across(partial)
     to_s6 = added(parts[3], jnp.where(top_in, n3, n2), inner)
     to_n1 = added(parts[4], jnp.where(top_in, s4, s5))

time: 86.7 us -> 86.4 us (level)
  starting transfers between devices: 21.9 us -> 20.6 us
  waiting for transfers between devices: 22.2 us -> 23.2 us
    ppermute x6, starting transfers between devices: 7.52 us -> 6.61 us  [on_device(): pair = lambda value: lax.ppermute(value, 'job', PAIR)]
where the time goes in v6:
time: 86.4 us; the launch traced here: 86.1 us
  Pallas kernels  34.3 us (40%)
  waiting for transfers between devices  23.2 us (27%)
  starting transfers between devices  20.6 us (24%)
  other arithmetic  3.95 us (5%)
  local copies, waits for them, and re-layouts  2.59 us (3%)
  between operations  1.52 us (2%)
    pallas_call x2, Pallas kernels, base(): pl.pallas_call(base_kernel, grid=(width // tile,), in_specs=[smem()] + [w...  11.9 us
    ppermute x6, waiting for transfers between devices, on_device(): pair = lambda value: lax.ppermute(value, 'job', PAIR)  10.6 us
    ppermute x6, starting transfers between devices, on_device(): lax.ppermute(value, 'job', [(i, i ^ d) for i in range(JOBS)])  8.89 us
    pallas_call x1, Pallas kernels, pull(): pl.pallas_call(functools.partial(pull_kernel, norm), grid=(width // tile,...  6.67 us
    ppermute x6, starting transfers between devices, on_device(): pair = lambda value: lax.ppermute(value, 'job', PAIR)  6.61 us
    pallas_call x1, Pallas kernels, project(): pl.pallas_call(project_kernel, grid=(rows // tile,), in_specs=[smem()] +...  5.76 us
    pallas_call x1, Pallas kernels, last(): pl.pallas_call(last_kernel, grid=(steps,), in_specs=[smem(), whole((rows,...  4.96 us
    ppermute x6, waiting for transfers between devices, on_device(): lax.ppermute(value, 'job', [(i, i ^ d) for i in range(JOBS)])  4.65 us
  transfers between devices with their start and end apart: 25, of which 13 were waited for; matrix products, arithmetic and copies ran while one was open for 5% of the time, Pallas kernels for 40%

profile of v6, /device:TPU:0, one launch (start us, length us, event | category | flops | bytes accessed | tf_op | source)
XLA Modules:
  0.0 86.1 jit_solution(8405890171286341074)
XLA Ops:
  1.1 2.6 %collective-permute-start.6 = (bf16[256,1024]{1,0:T(8,128)(2,1)}, bf16[256,1024]{1,0:T(8,128)(2,1)S(1)}, u32[]{:S(2)}, u32[]{:S(2)}) collective-permute-start(bf16[256,1024]{1,0:T(8,128)(2,1)} %bitcast.20), channel_id=1, source_target_pairs={{0,8},{8,0},{4,12},{12,4},{1,9},{9,1},{5,13},{13,5},{2,10},{10,2},... | collective-permute-start | bytes 1572872 | tf_op jit(solution)/shard_map/ppermute | solution.py:488
  3.7 3.6 %collective-permute-start.4 = (bf16[256,128]{1,0:T(8,128)(2,1)}, bf16[256,128]{1,0:T(8,128)(2,1)S(1)}, u32[]{:S(2)}, u32[]{:S(2)}) collective-permute-start(bf16[256,128]{1,0:T(8,128)(2,1)} %bitcast.30), channel_id=1, source_target_pairs={{0,3},{1,2},{2,1},{3,0},{4,7},{5,6},{6,5},{7,4},{8,11},{9,10},{10,... | collective-permute-start | bytes 196616 | tf_op jit(solution)/shard_map/ppermute | solution.py:487
  10.2 3.6 %collective-permute-done.3 = bf16[256,128]{1,0:T(8,128)(2,1)S(1)} collective-permute-done((bf16[256,128]{1,0:T(8,128)(2,1)}, bf16[256,128]{1,0:T(8,128)(2,1)S(1)}, u32[]{:S(2)}, u32[]{:S(2)}) %collective-permute-start.3) | collective-permute-done | bytes 65568 | tf_op jit(solution)/shard_map/ppermute | solution.py:487
  15.3 1.3 %fusion = s32[]{:T(128)} fusion(s32[4]{0:T(128)} %param.16, s32[4]{0:T(128)} %param.17), kind=kLoop, calls=%fused_computation.15 | loop fusion | flops 11 | bytes 36 | tf_op jit(solution)/shard_map/reduce_sum | solution.py:477
  17.3 1.4 %concatenate.3.info = s32[27]{0:T(128)S(1)} concatenate(s32[8]{0:T(128)} %bitcast.36, s32[8]{0:T(128)} %bitcast.37, s32[4]{0:T(128)} %param.16, s32[4]{0:T(128)} %param.17, s32[1]{0:T(128)} %bitcast.10, s32[1]{0:T(128)} %bitcast.11, s32[1]{0:T(128)} %bitcast.12), dimensions={0} | concatenate | bytes 216 | tf_op jit(solution)/shard_map/concatenate | solution.py:76
  18.7 3.6 %collective-permute-done.5.x_up_ref = bf16[4,256,128]{2,1,0:T(8,128)(2,1)S(1)} collective-permute-done((bf16[4,256,128]{2,1,0:T(8,128)(2,1)S(1)}, bf16[4,256,128]{2,1,0:T(8,128)(2,1)S(1)}, u32[]{:S(2)}, u32[]{:S(2)}) %collective-permute-start.5) | collective-permute-done | bytes 262176 | tf_op jit(solution)/shard_map/ppermute | solution.py:488
  22.4 1.8 %collective-permute-done.refs_2_ = bf16[64,3072]{1,0:T(8,128)(2,1)S(1)} collective-permute-done((bf16[64,3072]{1,0:T(8,128)(2,1)S(1)}, bf16[64,3072]{1,0:T(8,128)(2,1)S(1)}, u32[]{:S(2)}, u32[]{:S(2)}) %collective-permute-start) | collective-permute-done | bytes 393248 | tf_op jit(solution)/shard_map/ppermute | solution.py:485
  26.9 6.7 %pull_and_part_down.1 = (bf16[64,3072]{1,0:T(8,128)(2,1)S(1)}, bf16[64,3072]{1,0:T(8,128)(2,1)S(1)}, bf16[64,3072]{1,0:T(8,128)(2,1)S(1)}, bf16[64,3072]{1,0:T(8...) custom-call(s32[27]{0:T(128)S(1)} %concatenate.3.info, ...), custom_call_target="tpu_custom_call" | custom-call | flops 2013265920 | bytes 12451840 | tf_op jit(solution)/shard_map/pull_and_part_down/pallas_call | solution.py:194
  33.6 2.3 %collective-permute-done.10.refs_3_ = bf16[64,3072]{1,0:T(8,128)(2,1)S(1)} collective-permute-done((bf16[64,3072]{1,0:T(8,128)(2,1)S(1)}, bf16[64,3072]{1,0:T(8,128)(2,1)S(1)}, u32[]{:S(2)}, u32[]{:S(2)}) %collective-permute-start.10) | collective-permute-done | bytes 393248 | tf_op jit(solution)/shard_map/ppermute | solution.py:485
  36.0 1.8 %collective-permute-start.12 = (bf16[64,3072]{1,0:T(8,128)(2,1)S(1)}, bf16[64,3072]{1,0:T(8,128)(2,1)S(1)}, u32[]{:S(2)}, u32[]{:S(2)}) collective-permute-start(bf16[64,3072]{1,0:T(8,128)(2,1)S(1)} %get-tuple-element.110), channel_id=1, source_target_pairs={{0,1},{1,0},{2,3},{3,2},{4,5},{5,4},{6,7},{7,6},{8,9},{9,8},{10,11... | collective-permute-start | bytes 1179656 | tf_op jit(solution)/shard_map/ppermute | solution.py:485
  37.9 5.9 %base_term.2.base_ref = bf16[1024,1536]{1,0:T(8,128)(2,1)S(1)} custom-call(s32[27]{0:T(128)S(1)} %concatenate.3.info, bf16[256,1024]{1,0:T(8,128)(2,1)} %bitcast.22, bf16[256,1024]{1,0:T(8,128)(2,1)} %copy-done.1, bf16[256,1024]{1,0:T(8,128)(2,1)} %copy-done.3, bf16[256,1024]{1,0:T(8,128)(2,1)} %copy-done.5, bf16[3072,1024]{1,0:T(8,128)(2,1)} %weight_ref.3), custom_call_target="tpu_custom_call" | custom-call | flops 3221225472 | bytes 8388608 | tf_op jit(solution)/shard_map/base_term/pallas_call | solution.py:326
  43.8 2.6 %collective-permute-done.12.refs_4_ = bf16[64,3072]{1,0:T(8,128)(2,1)S(1)} collective-permute-done((bf16[64,3072]{1,0:T(8,128)(2,1)S(1)}, bf16[64,3072]{1,0:T(8,128)(2,1)S(1)}, u32[]{:S(2)}, u32[]{:S(2)}) %collective-permute-start.12) | collective-permute-done | bytes 393248 | tf_op jit(solution)/shard_map/ppermute | solution.py:485
  46.6 1.8 %collective-permute-start.14 = (bf16[64,3072]{1,0:T(8,128)(2,1)S(1)}, bf16[64,3072]{1,0:T(8,128)(2,1)S(1)}, u32[]{:S(2)}, u32[]{:S(2)}) collective-permute-start(bf16[64,3072]{1,0:T(8,128)(2,1)S(1)} %select_select_fusion), channel_id=1, source_target_pairs={{0,1},{1,0},{2,3},{3,2},{4,5},{5,4},{6,7},{7,6},{8,9},{9,8},{10,11... | collective-permute-start | bytes 1179656 | tf_op jit(solution)/shard_map/ppermute | solution.py:485
  48.4 5.9 %base_term.3.base_ref = bf16[1024,1536]{1,0:T(8,128)(2,1)S(1)} custom-call(s32[27]{0:T(128)S(1)} %concatenate.3.info, bf16[256,1024]{1,0:T(8,128)(2,1)} %bitcast.23, bf16[256,1024]{1,0:T(8,128)(2,1)} %copy-done.1, bf16[256,1024]{1,0:T(8,128)(2,1)} %copy-done.3, bf16[256,1024]{1,0:T(8,128)(2,1)} %copy-done.5, bf16[3072,1024]{1,0:T(8,128)(2,1)} %weight_ref.3), custom_call_target="tpu_custom_call" | custom-call | flops 3221225472 | bytes 8388608 | tf_op jit(solution)/shard_map/base_term/pallas_call | solution.py:326
  54.3 1.6 %collective-permute-done.14.refs_5_ = bf16[64,3072]{1,0:T(8,128)(2,1)S(1)} collective-permute-done((bf16[64,3072]{1,0:T(8,128)(2,1)S(1)}, bf16[64,3072]{1,0:T(8,128)(2,1)S(1)}, u32[]{:S(2)}, u32[]{:S(2)}) %collective-permute-start.14) | collective-permute-done | bytes 393248 | tf_op jit(solution)/shard_map/ppermute | solution.py:485
  56.2 1.8 %collective-permute-start.17 = (bf16[64,3072]{1,0:T(8,128)(2,1)S(1)}, bf16[64,3072]{1,0:T(8,128)(2,1)S(1)}, u32[]{:S(2)}, u32[]{:S(2)}) collective-permute-start(bf16[64,3072]{1,0:T(8,128)(2,1)S(1)} %add_convert_fusion.3), channel_id=1, source_target_pairs={{0,1},{1,0},{2,3},{3,2},{4,5},{5,4},{6,7},{7,6},{8,9},{9,8},{10,11... | collective-permute-start | bytes 1179656 | tf_op jit(solution)/shard_map/ppermute | solution.py:485
  58.1 5.8 %project.1 = (bf16[1024,128]{1,0:T(8,128)(2,1)S(1)}, bf16[384,3072]{1,0:T(8,128)(2,1)S(1)}) custom-call(s32[27]{0:T(128)S(1)} %concatenate.3.info, bf16[64,3072]{1,0:T(8,128)(2,1)S(1)} %get-tuple-element.83.refs_0_, bf16[64,3072]{1,0:T(8,128)(2,1)S(1)} %get-tuple-element.89.refs_1_, bf16[64,3072]{1,0:T(8,128)(2,1)S(1)} %collective-permute-done.refs_2_, ...), custom_call_target="tpu_custom_call" | custom-call | flops 2415919104 | bytes 11010048 | tf_op jit(solution)/shard_map/project/pallas_call | solution.py:281
  63.8 2.4 %collective-permute-done.17.t2 = bf16[64,3072]{1,0:T(8,128)(2,1)S(1)} collective-permute-done((bf16[64,3072]{1,0:T(8,128)(2,1)S(1)}, bf16[64,3072]{1,0:T(8,128)(2,1)S(1)}, u32[]{:S(2)}, u32[]{:S(2)}) %collective-permute-start.17) | collective-permute-done | bytes 393248 | tf_op jit(solution)/shard_map/ppermute | solution.py:485
  68.3 3.4 %grad_rows.1.filled_ref = bf16[1024,3072]{1,0:T(8,128)(2,1)} custom-call(bf16[1024,384]{1,0:T(8,128)(2,1)S(1)} %get-tuple-element.145.wide_ref, bf16[384,3072]{1,0:T(8,128)(2,1)S(1)} %get-tuple-element.146.table_ref, bf16[1024,1536]{1,0:T(8,128)(2,1)S(1)} %base_term.2.base_ref), custom_call_target="tpu_custom_call" | custom-call | flops 1207959552 | bytes 8257536 | tf_op jit(solution)/shard_map/grad_rows/pallas_call | solution.py:349
  72.8 1.5 %collective-permute-done.19.b_ref = bf16[1024,128]{1,0:T(8,128)(2,1)S(1)} collective-permute-done((bf16[1024,128]{1,0:T(8,128)(2,1)S(1)}, bf16[1024,128]{1,0:T(8,128)(2,1)S(1)}, u32[]{:S(2)}, u32[]{:S(2)}) %collective-permute-start.19) | collective-permute-done | bytes 262176 | tf_op jit(solution)/shard_map/ppermute | solution.py:489
  74.3 1.3 %part_up.1 = (bf16[256,128]{1,0:T(8,128)(2,1)S(1)}, bf16[256,128]{1,0:T(8,128)(2,1)S(1)}, bf16[256,128]{1,0:T(8,128)(2,1)S(1)}, bf16[256,128]{1,0:T(8,128)(2,1)S(1)}) custom-call(s32[27]{0:T(128)S(1)} %concatenate.3.info, bf16[256,1024]{1,0:T(8,128)(2,1)S(1)} %bitcast.24, bf16[256,1024]{1,0:T(8,128)(2,1)S(1)} %copy-done.2, bf16[256,1024]{1,0:T(8,128)(2,1)S(1)} %copy-done.4, ...), custom_call_target="tpu_custom_call" | custom-call | flops 201326592 | bytes 2621440 | tf_op jit(solution)/shard_map/part_up/pallas_call | solution.py:396
  75.6 2.1 %collective-permute-start.22 = (bf16[256,128]{1,0:T(8,128)(2,1)S(1)}, bf16[256,128]{1,0:T(8,128)(2,1)S(1)}, u32[]{:S(2)}, u32[]{:S(2)}) collective-permute-start(bf16[256,128]{1,0:T(8,128)(2,1)S(1)} %get-tuple-element.144), channel_id=1, source_target_pairs={{0,1},{1,0},{2,3},{3,2},{4,5},{5,4},{6,7},{7,6},{8,9},{9,8},{10,11... | collective-permute-start | bytes 196616 | tf_op jit(solution)/shard_map/ppermute | solution.py:487
  78.4 1.8 %collective-permute-start.24 = (bf16[256,128]{1,0:T(8,128)(2,1)S(1)}, bf16[256,128]{1,0:T(8,128)(2,1)S(1)}, u32[]{:S(2)}, u32[]{:S(2)}) collective-permute-start(bf16[256,128]{1,0:T(8,128)(2,1)S(1)} %get-tuple-element.156), channel_id=1, source_target_pairs={{0,3},{1,2},{2,1},{3,0},{4,7},{5,6},{6,5},{7,4},{8,11},{9,10},{10,... | collective-permute-start | bytes 196616 | tf_op jit(solution)/shard_map/ppermute | solution.py:487
  80.1 5.0 %grad_rows_and_down.1 = (bf16[1024,3072]{1,0:T(8,128)(2,1)}, f32[3072,128]{1,0:T(8,128)}) custom-call(s32[27]{0:T(128)S(1)} %concatenate.3.info, bf16[1024,384]{1,0:T(8,128)(2,1)S(1)} %get-tuple-element.145.wide_ref, bf16[384,3072]{1,0:T(8,128)(2,1)S(1)} %get-tuple-element.146.table_ref, ...), custom_call_target="tpu_custom_call", output_to_operand_aliasing={{0}: (10, {})} | custom-call | flops 1207959552 | bytes 12189696 | tf_op jit(solution)/shard_map/grad_rows_and_down/pallas_call | solution.py:434
  (64 shorter events, 13.1 us)
Async XLA Ops:
  0.6 21.7 %collective-permute-start.7 = (bf16[256,1024]{1,0:T(8,128)(2,1)}, bf16[256,1024]{1,0:T(8,128)(2,1)S(1)}, u32[]{:S(2)}, u32[]{:S(2)}) collective-permute-start(bf16[256,1024]{1,0:T(8,128)(2,1)} %bitcast.19), channel_id=1, source_target_pairs={{0,4},{4,0},{8,12},{12,8},{1,5},{5,1},{9,13},{13,9},{2,6},{6,2},{1... | collective-permute-start | bytes 1572872 | tf_op jit(solution)/shard_map/ppermute | solution.py:489
  1.1 21.1 %collective-permute-start.6 = (bf16[256,1024]{1,0:T(8,128)(2,1)}, bf16[256,1024]{1,0:T(8,128)(2,1)S(1)}, u32[]{:S(2)}, u32[]{:S(2)}) collective-permute-start(bf16[256,1024]{1,0:T(8,128)(2,1)} %bitcast.20), channel_id=1, source_target_pairs={{0,8},{8,0},{4,12},{12,4},{1,9},{9,1},{5,13},{13,5},{2,10},{10,2},... | collective-permute-start | bytes 1572872 | tf_op jit(solution)/shard_map/ppermute | solution.py:488
  3.7 6.5 %collective-permute-start.4 = (bf16[256,128]{1,0:T(8,128)(2,1)}, bf16[256,128]{1,0:T(8,128)(2,1)S(1)}, u32[]{:S(2)}, u32[]{:S(2)}) collective-permute-start(bf16[256,128]{1,0:T(8,128)(2,1)} %bitcast.30), channel_id=1, source_target_pairs={{0,3},{1,2},{2,1},{3,0},{4,7},{5,6},{6,5},{7,4},{8,11},{9,10},{10,... | collective-permute-start | bytes 196616 | tf_op jit(solution)/shard_map/ppermute | solution.py:487
  7.3 6.5 %collective-permute-start.3 = (bf16[256,128]{1,0:T(8,128)(2,1)}, bf16[256,128]{1,0:T(8,128)(2,1)S(1)}, u32[]{:S(2)}, u32[]{:S(2)}) collective-permute-start(bf16[256,128]{1,0:T(8,128)(2,1)} %bitcast.31), channel_id=1, source_target_pairs={{0,2},{1,3},{2,0},{3,1},{4,6},{5,7},{6,4},{7,5},{8,10},{9,11},{10,... | collective-permute-start | bytes 196616 | tf_op jit(solution)/shard_map/ppermute | solution.py:487
  7.3 6.5 %collective-permute-start.2 = (bf16[256,128]{1,0:T(8,128)(2,1)}, bf16[256,128]{1,0:T(8,128)(2,1)S(1)}, u32[]{:S(2)}, u32[]{:S(2)}) collective-permute-start(bf16[256,128]{1,0:T(8,128)(2,1)} %bitcast.32), channel_id=1, source_target_pairs={{0,1},{1,0},{2,3},{3,2},{4,5},{5,4},{6,7},{7,6},{8,9},{9,8},{10,11... | collective-permute-start | bytes 196616 | tf_op jit(solution)/shard_map/ppermute | solution.py:487
  10.2 12.2 %collective-permute-start.1 = (bf16[64,3072]{1,0:T(8,128)(2,1)S(1)}, bf16[64,3072]{1,0:T(8,128)(2,1)S(1)}, u32[]{:S(2)}, u32[]{:S(2)}) collective-permute-start(bf16[64,3072]{1,0:T(8,128)(2,1)S(1)} %get-tuple-element.83.refs_0_), channel_id=1, source_target_pairs={{1,2},{2,1},{0,4},{3,7},{5,6},{6,5},{4,0},{7,3},{9,10},{10,9},{8,1... | collective-permute-start | bytes 1179656 | tf_op jit(solution)/shard_map/ppermute | solution.py:486
  13.8 10.3 %collective-permute-start = (bf16[64,3072]{1,0:T(8,128)(2,1)S(1)}, bf16[64,3072]{1,0:T(8,128)(2,1)S(1)}, u32[]{:S(2)}, u32[]{:S(2)}) collective-permute-start(bf16[64,3072]{1,0:T(8,128)(2,1)S(1)} %get-tuple-element.83.refs_0_), channel_id=1, source_target_pairs={{0,1},{1,0},{2,3},{3,2},{4,5},{5,4},{6,7},{7,6},{8,9},{9,8},{10,11... | collective-permute-start | bytes 1179656 | tf_op jit(solution)/shard_map/ppermute | solution.py:485
  14.7 7.6 %collective-permute-start.5 = (bf16[4,256,128]{2,1,0:T(8,128)(2,1)S(1)}, bf16[4,256,128]{2,1,0:T(8,128)(2,1)S(1)}, u32[]{:S(2)}, u32[]{:S(2)}) collective-permute-start(bf16[4,256,128]{2,1,0:T(8,128)(2,1)S(1)} %pad_maximum_fusion.1.z_ref), channel_id=1, source_target_pairs={{0,8},{8,0},{4,12},{12,4},{1,9},{9,1},{5,13},{13,5},{2,10},{10,2},... | collective-permute-start | bytes 786440 | tf_op jit(solution)/shard_map/ppermute | solution.py:488
  24.2 2.0 %collective-permute-start.8 = (bf16[2,4,256,128]{3,2,1,0:T(8,128)(2,1)S(1)}, bf16[2,4,256,128]{3,2,1,0:T(8,128)(2,1)S(1)}, u32[]{:S(2)}, u32[]{:S(2)}) collective-permute-start(bf16[2,4,256,128]{3,2,1,0:T(8,128)(2,1)S(1)} %pad_maximum_fusion), channel_id=1, source_target_pairs={{0,4},{4,0},{8,12},{12,8},{1,5},{5,1},{9,13},{13,9},{2,6},{6,2},{1... | collective-permute-start | bytes 1572872 | tf_op jit(solution)/shard_map/ppermute | solution.py:489
  24.3 2.6 %collective-permute-start.9 = (bf16[256,1024]{1,0:T(8,128)(2,1)S(1)}, bf16[256,1024]{1,0:T(8,128)(2,1)S(1)}, u32[]{:S(2)}, u32[]{:S(2)}) collective-permute-start(bf16[256,1024]{1,0:T(8,128)(2,1)S(1)} %collective-permute-done.6.g2), channel_id=1, source_target_pairs={{0,4},{4,0},{8,12},{12,8},{1,5},{5,1},{9,13},{13,9},{2,6},{6,2},{1... | collective-permute-start | bytes 1572872 | tf_op jit(solution)/shard_map/ppermute | solution.py:489
  24.8 11.1 %collective-permute-start.10 = (bf16[64,3072]{1,0:T(8,128)(2,1)S(1)}, bf16[64,3072]{1,0:T(8,128)(2,1)S(1)}, u32[]{:S(2)}, u32[]{:S(2)}) collective-permute-start(bf16[64,3072]{1,0:T(8,128)(2,1)S(1)} %get-tuple-element.94), channel_id=1, source_target_pairs={{0,1},{1,0},{2,3},{3,2},{4,5},{5,4},{6,7},{7,6},{8,9},{9,8},{10,11... | collective-permute-start | bytes 1179656 | tf_op jit(solution)/shard_map/ppermute | solution.py:485
  25.1 10.8 %collective-permute-start.11 = (bf16[64,3072]{1,0:T(8,128)(2,1)S(1)}, bf16[64,3072]{1,0:T(8,128)(2,1)S(1)}, u32[]{:S(2)}, u32[]{:S(2)}) collective-permute-start(bf16[64,3072]{1,0:T(8,128)(2,1)S(1)} %get-tuple-element.95), channel_id=1, source_target_pairs={{1,2},{2,1},{0,4},{3,7},{5,6},{6,5},{4,0},{7,3},{9,10},{10,9},{8,1... | collective-permute-start | bytes 1179656 | tf_op jit(solution)/shard_map/ppermute | solution.py:486
  36.0 10.3 %collective-permute-start.12 = (bf16[64,3072]{1,0:T(8,128)(2,1)S(1)}, bf16[64,3072]{1,0:T(8,128)(2,1)S(1)}, u32[]{:S(2)}, u32[]{:S(2)}) collective-permute-start(bf16[64,3072]{1,0:T(8,128)(2,1)S(1)} %get-tuple-element.110), channel_id=1, source_target_pairs={{0,1},{1,0},{2,3},{3,2},{4,5},{5,4},{6,7},{7,6},{8,9},{9,8},{10,11... | collective-permute-start | bytes 1179656 | tf_op jit(solution)/shard_map/ppermute | solution.py:485
  37.8 8.5 %collective-permute-start.13 = (bf16[64,3072]{1,0:T(8,128)(2,1)S(1)}, bf16[64,3072]{1,0:T(8,128)(2,1)S(1)}, u32[]{:S(2)}, u32[]{:S(2)}) collective-permute-start(bf16[64,3072]{1,0:T(8,128)(2,1)S(1)} %get-tuple-element.111), channel_id=1, source_target_pairs={{1,2},{2,1},{0,4},{3,7},{5,6},{6,5},{4,0},{7,3},{9,10},{10,9},{8,1... | collective-permute-start | bytes 1179656 | tf_op jit(solution)/shard_map/ppermute | solution.py:486
  46.6 9.4 %collective-permute-start.14 = (bf16[64,3072]{1,0:T(8,128)(2,1)S(1)}, bf16[64,3072]{1,0:T(8,128)(2,1)S(1)}, u32[]{:S(2)}, u32[]{:S(2)}) collective-permute-start(bf16[64,3072]{1,0:T(8,128)(2,1)S(1)} %select_select_fusion), channel_id=1, source_target_pairs={{0,1},{1,0},{2,3},{3,2},{4,5},{5,4},{6,7},{7,6},{8,9},{9,8},{10,11... | collective-permute-start | bytes 1179656 | tf_op jit(solution)/shard_map/ppermute | solution.py:485
  48.4 7.6 %collective-permute-start.15 = (bf16[64,3072]{1,0:T(8,128)(2,1)S(1)}, bf16[64,3072]{1,0:T(8,128)(2,1)S(1)}, u32[]{:S(2)}, u32[]{:S(2)}) collective-permute-start(bf16[64,3072]{1,0:T(8,128)(2,1)S(1)} %add_convert_fusion.4), channel_id=1, source_target_pairs={{1,2},{2,1},{0,4},{3,7},{5,6},{6,5},{4,0},{7,3},{9,10},{10,9},{8,1... | collective-permute-start | bytes 1179656 | tf_op jit(solution)/shard_map/ppermute | solution.py:486
  56.2 10.0 %collective-permute-start.17 = (bf16[64,3072]{1,0:T(8,128)(2,1)S(1)}, bf16[64,3072]{1,0:T(8,128)(2,1)S(1)}, u32[]{:S(2)}, u32[]{:S(2)}) collective-permute-start(bf16[64,3072]{1,0:T(8,128)(2,1)S(1)} %add_convert_fusion.3), channel_id=1, source_target_pairs={{0,1},{1,0},{2,3},{3,2},{4,5},{5,4},{6,7},{7,6},{8,9},{9,8},{10,11... | collective-permute-start | bytes 1179656 | tf_op jit(solution)/shard_map/ppermute | solution.py:485
  58.0 9.1 %collective-permute-start.16 = (bf16[64,3072]{1,0:T(8,128)(2,1)S(1)}, bf16[64,3072]{1,0:T(8,128)(2,1)S(1)}, u32[]{:S(2)}, u32[]{:S(2)}) collective-permute-start(bf16[64,3072]{1,0:T(8,128)(2,1)S(1)} %add_convert_fusion.2), channel_id=1, source_target_pairs={{1,2},{2,1},{0,4},{3,7},{5,6},{6,5},{4,0},{7,3},{9,10},{10,9},{8,1... | collective-permute-start | bytes 1179656 | tf_op jit(solution)/shard_map/ppermute | solution.py:486
  66.2 6.4 %collective-permute-start.18 = (bf16[1024,128]{1,0:T(8,128)(2,1)S(1)}, bf16[1024,128]{1,0:T(8,128)(2,1)S(1)}, u32[]{:S(2)}, u32[]{:S(2)}) collective-permute-start(bf16[1024,128]{1,0:T(8,128)(2,1)S(1)} %get-tuple-element.141), channel_id=1, source_target_pairs={{0,8},{8,0},{4,12},{12,4},{1,9},{9,1},{5,13},{13,5},{2,10},{10,2},... | collective-permute-start | bytes 786440 | tf_op jit(solution)/shard_map/ppermute | solution.py:488
  67.3 12.8 %collective-permute-start.20 = (bf16[64,3072]{1,0:T(8,128)(2,1)S(1)}, bf16[64,3072]{1,0:T(8,128)(2,1)S(1)}, u32[]{:S(2)}, u32[]{:S(2)}) collective-permute-start(bf16[64,3072]{1,0:T(8,128)(2,1)S(1)} %add_convert_fusion.1), channel_id=1, source_target_pairs={{0,1},{1,0},{2,3},{3,2},{4,5},{5,4},{6,7},{7,6},{8,9},{9,8},{10,11... | collective-permute-start | bytes 1179656 | tf_op jit(solution)/shard_map/ppermute | solution.py:485
  68.2 11.9 %collective-permute-start.21 = (bf16[64,3072]{1,0:T(8,128)(2,1)S(1)}, bf16[64,3072]{1,0:T(8,128)(2,1)S(1)}, u32[]{:S(2)}, u32[]{:S(2)}) collective-permute-start(bf16[64,3072]{1,0:T(8,128)(2,1)S(1)} %add_convert_fusion), channel_id=1, source_target_pairs={{1,2},{2,1},{0,4},{3,7},{5,6},{6,5},{4,0},{7,3},{9,10},{10,9},{8,1... | collective-permute-start | bytes 1179656 | tf_op jit(solution)/shard_map/ppermute | solution.py:486
  75.6 9.8 %collective-permute-start.22 = (bf16[256,128]{1,0:T(8,128)(2,1)S(1)}, bf16[256,128]{1,0:T(8,128)(2,1)S(1)}, u32[]{:S(2)}, u32[]{:S(2)}) collective-permute-start(bf16[256,128]{1,0:T(8,128)(2,1)S(1)} %get-tuple-element.144), channel_id=1, source_target_pairs={{0,1},{1,0},{2,3},{3,2},{4,5},{5,4},{6,7},{7,6},{8,9},{9,8},{10,11... | collective-permute-start | bytes 196616 | tf_op jit(solution)/shard_map/ppermute | solution.py:487
  77.7 7.7 %collective-permute-start.23 = (bf16[256,128]{1,0:T(8,128)(2,1)S(1)}, bf16[256,128]{1,0:T(8,128)(2,1)S(1)}, u32[]{:S(2)}, u32[]{:S(2)}) collective-permute-start(bf16[256,128]{1,0:T(8,128)(2,1)S(1)} %get-tuple-element.155), channel_id=1, source_target_pairs={{0,2},{1,3},{2,0},{3,1},{4,6},{5,7},{6,4},{7,5},{8,10},{9,11},{10,... | collective-permute-start | bytes 196616 | tf_op jit(solution)/shard_map/ppermute | solution.py:487
  78.4 7.1 %collective-permute-start.24 = (bf16[256,128]{1,0:T(8,128)(2,1)S(1)}, bf16[256,128]{1,0:T(8,128)(2,1)S(1)}, u32[]{:S(2)}, u32[]{:S(2)}) collective-permute-start(bf16[256,128]{1,0:T(8,128)(2,1)S(1)} %get-tuple-element.156), channel_id=1, source_target_pairs={{0,3},{1,2},{2,1},{3,0},{4,7},{5,6},{6,5},{7,4},{8,11},{9,10},{10,... | collective-permute-start | bytes 196616 | tf_op jit(solution)/shard_map/ppermute | solution.py:487
  (9 other events, 69.1 us)
